TPU v7x, 32 devices: a whole 2x2x4 slice. The times are simulated.
32 devices in a mesh: groups: 2 (over x), expert: 16 (over z, y, core).
Axes of the slice: x: 2, y: 2, z: 4, core: 2. Of those that a mesh axis runs over, the one named last changes fastest.
Arguments:
- tokens: bfloat16 [4096, 2048], P(('groups', 'expert')), parts along dimension 0, may hold values from -6 to 6
- grad_out: bfloat16 [4096, 2048], P(('groups', 'expert')), parts along dimension 0, may hold values from -6 to 6
- expert_ids: int32 [4096, 4], P(('groups', 'expert')), parts along dimension 0, may hold values from 0 to 15, all different within a row; in each aligned block of 128 rows (0 to 127, 128 to 255, ...) at most 36 rows name the same one
- combine: float32 [4096, 4], P(('groups', 'expert')), parts along dimension 0, may hold values from 0.05 to 0.6
- frozen_gate: bfloat16 [16, 2048, 768], P('expert'), may hold values from -0.125 to 0.125
- frozen_up: bfloat16 [16, 2048, 768], P('expert'), may hold values from -0.125 to 0.125
- frozen_down: bfloat16 [16, 768, 2048], P('expert'), may hold values from -0.21875 to 0.21875
- adapter_gate_in: bfloat16 [16, 32, 2048], P('expert'), may hold values from -0.125 to 0.125
- adapter_gate_out: bfloat16 [16, 32, 768], P('expert'), may hold values from -1 to 1
- adapter_up_in: bfloat16 [16, 32, 2048], P('expert'), may hold values from -0.125 to 0.125
- adapter_up_out: bfloat16 [16, 32, 768], P('expert'), may hold values from -1 to 1
- adapter_down_in: bfloat16 [16, 32, 768], P('expert'), may hold values from -0.21875 to 0.21875
- adapter_down_out: bfloat16 [16, 32, 2048], P('expert'), may hold values from -1 to 1
Outputs:
- grad_tokens: bfloat16 [4096, 2048], P(('groups', 'expert')), parts along dimension 0
- grad_combine: float32 [4096, 4], P(('groups', 'expert')), parts along dimension 0
- grad_gate_in: float32 [32, 32, 2048], P(('groups', 'expert')), parts along dimension 0
- grad_gate_out: float32 [32, 32, 768], P(('groups', 'expert')), parts along dimension 0
- grad_up_in: float32 [32, 32, 2048], P(('groups', 'expert')), parts along dimension 0
- grad_up_out: float32 [32, 32, 768], P(('groups', 'expert')), parts along dimension 0
- grad_down_in: float32 [32, 32, 768], P(('groups', 'expert')), parts along dimension 0
- grad_down_out: float32 [32, 32, 2048], P(('groups', 'expert')), parts along dimension 0
There are 2 independent parts, one for each index of `groups`. A program takes and returns all parts, laid end to end along the dimension named above; an argument that names none is the same for every part. Nothing has to cross between parts.
Inputs may be any that keep to these rules, and one draw needn't show every extreme that they name: `expert_ids`: in each token's row the 4 experts differ. Among the rows of one device no expert is named more than 36 times, a bound that some block reaches; every expert is named somewhere.
All inputs are finite; a program needn't handle non-finite values.
Results may differ from a plain program's by a relative error of at most 0.017.
Values may be sent and summed in bfloat16 or wider, within the bound.
No kernel may reach another device: no remote copies, remote signals or barrier semaphores. Data moves between devices by JAX's collectives and lax.ppermute only.
A program may use at most 128 MiB of HBM per device.

v0:
```python
import jax
import jax.numpy as jnp
from jax import lax
from jax.sharding import PartitionSpec as P

adapter_scale_factor = 2.0


def expert_forward(
    input_token_rows,
    gate_weight_matrix,
    up_weight_matrix,
    down_weight_matrix,
    gate_adapter_input,
    gate_adapter_output,
    up_adapter_input,
    up_adapter_output,
    down_adapter_input,
    down_adapter_output,
):
    lowrank_gate_product = jnp.dot(
        input_token_rows, gate_adapter_input.T, preferred_element_type=jnp.float32
    ).astype(jnp.bfloat16)
    lowrank_up_product = jnp.dot(
        input_token_rows, up_adapter_input.T, preferred_element_type=jnp.float32
    ).astype(jnp.bfloat16)
    gate_preactivation = jnp.dot(
        input_token_rows, gate_weight_matrix, preferred_element_type=jnp.float32
    ) + adapter_scale_factor * jnp.dot(
        lowrank_gate_product, gate_adapter_output, preferred_element_type=jnp.float32
    )
    up_preactivation = jnp.dot(
        input_token_rows, up_weight_matrix, preferred_element_type=jnp.float32
    ) + adapter_scale_factor * jnp.dot(
        lowrank_up_product, up_adapter_output, preferred_element_type=jnp.float32
    )
    hidden_activation = (jax.nn.silu(gate_preactivation) * up_preactivation).astype(jnp.bfloat16)
    lowrank_down_product = jnp.dot(
        hidden_activation, down_adapter_input.T, preferred_element_type=jnp.float32
    ).astype(jnp.bfloat16)
    layer_output = (
        jnp.dot(hidden_activation, down_weight_matrix, preferred_element_type=jnp.float32)
        + adapter_scale_factor
        * jnp.dot(lowrank_down_product, down_adapter_output, preferred_element_type=jnp.float32)
    ).astype(jnp.bfloat16)
    return (
        lowrank_gate_product,
        lowrank_up_product,
        gate_preactivation,
        up_preactivation,
        hidden_activation,
        lowrank_down_product,
        layer_output,
    )


def expert_backward(
    input_token_rows,
    gradient_token_rows,
    weight_rows,
    saved,
    gate_weight_matrix,
    up_weight_matrix,
    down_weight_matrix,
    gate_adapter_input,
    gate_adapter_output,
    up_adapter_input,
    up_adapter_output,
    down_adapter_input,
    down_adapter_output,
):
    (
        lowrank_gate_product,
        lowrank_up_product,
        gate_preactivation,
        up_preactivation,
        hidden_activation,
        lowrank_down_product,
        layer_output,
    ) = saved
    routing_weight_column = weight_rows[:, None]
    down_projection_backward = (
        routing_weight_column
        * jnp.dot(gradient_token_rows, down_adapter_output.T, preferred_element_type=jnp.float32)
    ).astype(jnp.bfloat16)
    weighted_lowrank_product = (
        routing_weight_column * lowrank_down_product.astype(jnp.float32)
    ).astype(jnp.bfloat16)
    hidden_gradient = routing_weight_column * jnp.dot(
        gradient_token_rows, down_weight_matrix.T, preferred_element_type=jnp.float32
    ) + adapter_scale_factor * jnp.dot(
        down_projection_backward, down_adapter_input, preferred_element_type=jnp.float32
    )
    sigmoid_gate = jax.nn.sigmoid(gate_preactivation)
    gate_activation_gradient = (
        hidden_gradient
        * up_preactivation
        * sigmoid_gate
        * (1.0 + gate_preactivation * (1.0 - sigmoid_gate))
    ).astype(jnp.bfloat16)
    up_activation_gradient = (hidden_gradient * gate_preactivation * sigmoid_gate).astype(
        jnp.bfloat16
    )
    gate_projection_backward = jnp.dot(
        gate_activation_gradient, gate_adapter_output.T, preferred_element_type=jnp.float32
    ).astype(jnp.bfloat16)
    up_projection_backward = jnp.dot(
        up_activation_gradient, up_adapter_output.T, preferred_element_type=jnp.float32
    ).astype(jnp.bfloat16)
    input_gradient = jnp.dot(
        gate_activation_gradient, gate_weight_matrix.T, preferred_element_type=jnp.float32
    ) + jnp.dot(up_activation_gradient, up_weight_matrix.T, preferred_element_type=jnp.float32)
    input_gradient = input_gradient + adapter_scale_factor * (
        jnp.dot(gate_projection_backward, gate_adapter_input, preferred_element_type=jnp.float32)
        + jnp.dot(up_projection_backward, up_adapter_input, preferred_element_type=jnp.float32)
    )
    input_gradient = input_gradient.astype(jnp.bfloat16)
    grads = (
        adapter_scale_factor
        * jnp.dot(gate_projection_backward.T, input_token_rows, preferred_element_type=jnp.float32),
        adapter_scale_factor
        * jnp.dot(
            lowrank_gate_product.T, gate_activation_gradient, preferred_element_type=jnp.float32
        ),
        adapter_scale_factor
        * jnp.dot(up_projection_backward.T, input_token_rows, preferred_element_type=jnp.float32),
        adapter_scale_factor
        * jnp.dot(lowrank_up_product.T, up_activation_gradient, preferred_element_type=jnp.float32),
        adapter_scale_factor
        * jnp.dot(
            down_projection_backward.T, hidden_activation, preferred_element_type=jnp.float32
        ),
        adapter_scale_factor
        * jnp.dot(
            weighted_lowrank_product.T, gradient_token_rows, preferred_element_type=jnp.float32
        ),
    )
    return (input_gradient, grads)


def on_device(
    tokens,
    grad_out,
    expert_ids,
    combine,
    frozen_gate,
    frozen_up,
    frozen_down,
    adapter_gate_in,
    adapter_gate_out,
    adapter_up_in,
    adapter_up_out,
    adapter_down_in,
    adapter_down_out,
):
    tok_rows, width = tokens.shape
    routes = expert_ids.shape[1]
    experts = lax.axis_size("expert")
    capacity = tok_rows * routes * 9 // (8 * experts)
    assigned = tok_rows * routes
    flat_experts = expert_ids.reshape(assigned)
    onehot = (flat_experts[:, None] == jnp.arange(experts, dtype=jnp.int32)[None, :]).astype(
        jnp.int32
    )
    before = jnp.cumsum(onehot, axis=0) - onehot
    slot_index = jnp.sum(before * onehot, axis=1)
    target = flat_experts * capacity + slot_index
    slot_table = (
        jnp.full((experts * capacity,), assigned, jnp.int32)
        .at[target]
        .set(jnp.arange(assigned, dtype=jnp.int32))
    )
    source_row = slot_table // routes
    zero_row = jnp.zeros((1, width), jnp.bfloat16)
    send_tokens = jnp.concatenate([tokens, zero_row], axis=0)[source_row].reshape(
        experts, capacity, width
    )
    send_grads = jnp.concatenate([grad_out, zero_row], axis=0)[source_row].reshape(
        experts, capacity, width
    )
    send_weights = jnp.concatenate(
        [combine.reshape(assigned), jnp.zeros((1,), jnp.float32)], axis=0
    )[slot_table].reshape(experts, capacity)
    matrices = (
        frozen_gate[0],
        frozen_up[0],
        frozen_down[0],
        adapter_gate_in[0],
        adapter_gate_out[0],
        adapter_up_in[0],
        adapter_up_out[0],
        adapter_down_in[0],
        adapter_down_out[0],
    )
    got_tokens, got_grads, got_weights = (
        lax.all_to_all(send_tokens, "expert", split_axis=0, concat_axis=0, tiled=True),
        lax.all_to_all(send_grads, "expert", split_axis=0, concat_axis=0, tiled=True),
        lax.all_to_all(
            send_weights.astype(jnp.bfloat16), "expert", split_axis=0, concat_axis=0, tiled=True
        ).astype(send_weights.dtype),
    )
    input_token_rows = got_tokens.reshape(experts * capacity, width)
    saved = expert_forward(input_token_rows, *matrices)
    gradient_token_rows = got_grads.reshape(experts * capacity, width)
    weight_rows = got_weights.reshape(experts * capacity)
    input_gradient, grads = expert_backward(
        input_token_rows, gradient_token_rows, weight_rows, saved, *matrices
    )
    layer_output = saved[6]
    back_grad, back_output = (
        lax.all_to_all(
            input_gradient.reshape(experts, capacity, width),
            "expert",
            split_axis=0,
            concat_axis=0,
            tiled=True,
        ),
        lax.all_to_all(
            layer_output.reshape(experts, capacity, width),
            "expert",
            split_axis=0,
            concat_axis=0,
            tiled=True,
        ),
    )
    assign_grad = back_grad.reshape(experts * capacity, width)[target].reshape(
        tok_rows, routes, width
    )
    assign_output = back_output.reshape(experts * capacity, width)[target].reshape(
        tok_rows, routes, width
    )
    grad_combine = jnp.einsum(
        "tkd,td->tk", assign_output, grad_out, preferred_element_type=jnp.float32
    )
    grad_tokens = jnp.sum(assign_grad.astype(jnp.float32), axis=1).astype(jnp.bfloat16)
    return (
        grad_tokens,
        grad_combine,
        grads[0][None],
        grads[1][None],
        grads[2][None],
        grads[3][None],
        grads[4][None],
        grads[5][None],
    )


def solution(mesh):
    placed = (
        P(("groups", "expert"), None),
        P(("groups", "expert"), None),
        P(("groups", "expert"), None),
        P(("groups", "expert"), None),
        P("expert", None, None),
        P("expert", None, None),
        P("expert", None, None),
        P("expert", None, None),
        P("expert", None, None),
        P("expert", None, None),
        P("expert", None, None),
        P("expert", None, None),
        P("expert", None, None),
    )
    return jax.shard_map(
        on_device,
        mesh=mesh,
        in_specs=placed,
        out_specs=(
            P(("groups", "expert"), None),
            P(("groups", "expert"), None),
            P(("groups", "expert"), None, None),
            P(("groups", "expert"), None, None),
            P(("groups", "expert"), None, None),
            P(("groups", "expert"), None, None),
            P(("groups", "expert"), None, None),
            P(("groups", "expert"), None, None),
        ),
        check_vma=False,
    )
```

profile of v0, /device:TPU:16, one launch (start us, length us, event | category | flops | bytes accessed | tf_op | source)
XLA Modules:
  0.0 325.2 jit_solution(15480881948893504461)
XLA Ops:
  5.3 2.4 scatter_custom_fusion
  7.8 3.9 %gather_fusion = bf16[576]{0:T(1024)(128)(2,1)S(1)} fusion(bf16[513]{0:T(1024)(128)(2,1)S(1)} %pad_maximum_fusion, s32[1024]{0:T(1024)S(1)} %get-tuple-element.14), kind=kCustom, calls=%fused_computation | custom fusion | bytes 4608 | tf_op jit(solution)/shard_map/gather | solution.py:181
  12.5 6.2 %all-to-all-start = ((bf16[16,1,36]{2,1,0:T(2,128)(2,1)}), bf16[16,1,36]{2,1,0:T(2,128)(2,1)S(1)}, u32[]{:S(2)}, u32[]{:S(2)}) async-start(bf16[16,1,36]{2,1,0:T(2,128)(2,1)} %convert_element_type.91), calls=%async_computation | async-start | bytes 16384 | tf_op jit(solution)/shard_map/all_to_all | solution.py:198
  20.6 7.9 %gather_fusion.2 = bf16[576,2048]{1,0:T(8,128)(2,1)} fusion(bf16[129,2048]{1,0:T(8,128)(2,1)} %concatenate.11, s32[1024]{0:T(1024)S(1)} %get-tuple-element.13), kind=kCustom, calls=%fused_computation.2 | custom fusion | bytes 4720896 | tf_op jit(solution)/shard_map/gather | solution.py:175
  28.5 4.1 %reshape.120 = bf16[16,36,2048]{2,1,0:T(8,128)(2,1)} reshape(bf16[576,2048]{1,0:T(8,128)(2,1)} %gather_fusion.2) | data formatting | bytes 4718592 | tf_op jit(solution)/shard_map/reshape | solution.py:175
  32.6 6.0 %all-to-all-start.2 = ((bf16[16,36,2048]{2,1,0:T(8,128)(2,1)}), bf16[16,36,2048]{2,1,0:T(8,128)(2,1)}, u32[]{:S(2)}, u32[]{:S(2)}) async-start(bf16[16,36,2048]{2,1,0:T(8,128)(2,1)} %reshape.120), calls=%async_computation.2 | async-start | bytes 5242880 | tf_op jit(solution)/shard_map/all_to_all | solution.py:196
  40.5 8.0 %gather_fusion.1 = bf16[576,2048]{1,0:T(8,128)(2,1)} fusion(bf16[129,2048]{1,0:T(8,128)(2,1)} %concatenate.10, s32[1024]{0:T(1024)S(1)} %get-tuple-element.13), kind=kCustom, calls=%fused_computation.1 | custom fusion | bytes 4720896 | tf_op jit(solution)/shard_map/gather | solution.py:178
  48.5 4.1 %reshape.118 = bf16[16,36,2048]{2,1,0:T(8,128)(2,1)} reshape(bf16[576,2048]{1,0:T(8,128)(2,1)} %gather_fusion.1) | data formatting | bytes 4718592 | tf_op jit(solution)/shard_map/reshape | solution.py:178
  52.6 45.0 %all-to-all-done.2 = bf16[16,36,2048]{2,1,0:T(8,128)(2,1)} async-done(((bf16[16,36,2048]{2,1,0:T(8,128)(2,1)}), bf16[16,36,2048]{2,1,0:T(8,128)(2,1)}, u32[]{:S(2)}, u32[]{:S(2)}) %all-to-all-start.2) | async-done | bytes 2359328 | tf_op jit(solution)/shard_map/all_to_all | solution.py:196
  97.6 4.7 %all-to-all-start.1 = ((bf16[16,36,2048]{2,1,0:T(8,128)(2,1)}), bf16[16,36,2048]{2,1,0:T(8,128)(2,1)}, u32[]{:S(2)}, u32[]{:S(2)}) async-start(bf16[16,36,2048]{2,1,0:T(8,128)(2,1)} %reshape.118), calls=%async_computation.1 | async-start | bytes 5242880 | tf_op jit(solution)/shard_map/all_to_all | solution.py:197
  102.4 4.2 %reshape.121 = bf16[576,2048]{1,0:T(8,128)(2,1)} reshape(bf16[16,36,2048]{2,1,0:T(8,128)(2,1)} %all-to-all-done.2) | data formatting | bytes 4718592 | tf_op jit(solution)/shard_map/reshape | solution.py:202
  106.6 3.2 convolution_convert_fusion.3
  111.3 5.3 %fusion.2 = f32[576,768]{1,0:T(8,128)} fusion(bf16[576,2048]{1,0:T(8,128)(2,1)S(1)} %copy-done.2, bf16[1,2048,768]{2,1,0:T(8,128)(2,1)} %param.17), kind=kOutput, calls=%fused_computation.10 | convolution fusion | flops 1811939328 | bytes 7274496 | tf_op jit(solution)/shard_map/dot_general | solution.py:27
  116.6 3.2 fusion.6
  119.8 41.5 %all-to-all-done.1 = bf16[16,36,2048]{2,1,0:T(8,128)(2,1)} async-done(((bf16[16,36,2048]{2,1,0:T(8,128)(2,1)}), bf16[16,36,2048]{2,1,0:T(8,128)(2,1)}, u32[]{:S(2)}, u32[]{:S(2)}) %all-to-all-start.1) | async-done | bytes 2359328 | tf_op jit(solution)/shard_map/all_to_all | solution.py:197
  161.3 4.1 %reshape.119 = bf16[576,2048]{1,0:T(8,128)(2,1)} reshape(bf16[16,36,2048]{2,1,0:T(8,128)(2,1)} %all-to-all-done.1) | data formatting | bytes 4718592 | tf_op jit(solution)/shard_map/reshape | solution.py:204
  165.4 2.6 fusion.20
  172.7 2.5 multiply_convert_fusion
  181.2 4.8 %all-to-all-start.4 = ((bf16[16,36,2048]{2,1,0:T(8,128)(2,1)}), bf16[16,36,2048]{2,1,0:T(8,128)(2,1)S(1)}, u32[]{:S(2)}, u32[]{:S(2)}) async-start(bf16[16,36,2048]{2,1,0:T(8,128)(2,1)} %reshape.125), calls=%async_computation.4 | async-start | bytes 5242880 | tf_op jit(solution)/shard_map/all_to_all | solution.py:218
  195.5 2.5 add_convert_fusion.1
  198.0 4.1 %reshape.122 = bf16[16,36,2048]{2,1,0:T(8,128)(2,1)} reshape(bf16[576,2048]{1,0:T(8,128)(2,1)} %add_convert_fusion.1) | data formatting | bytes 4718592 | tf_op jit(solution)/shard_map/reshape | solution.py:212
  202.1 42.8 %all-to-all-done.4 = bf16[16,36,2048]{2,1,0:T(8,128)(2,1)S(1)} async-done(((bf16[16,36,2048]{2,1,0:T(8,128)(2,1)}), bf16[16,36,2048]{2,1,0:T(8,128)(2,1)S(1)}, u32[]{:S(2)}, u32[]{:S(2)}) %all-to-all-start.4) | async-done | bytes 2359328 | tf_op jit(solution)/shard_map/all_to_all | solution.py:218
  246.4 4.7 %all-to-all-start.3 = ((bf16[16,36,2048]{2,1,0:T(8,128)(2,1)}), bf16[16,36,2048]{2,1,0:T(8,128)(2,1)}, u32[]{:S(2)}, u32[]{:S(2)}) async-start(bf16[16,36,2048]{2,1,0:T(8,128)(2,1)} %reshape.122), calls=%async_computation.3 | async-start | bytes 5242880 | tf_op jit(solution)/shard_map/all_to_all | solution.py:211
  261.1 2.7 reshape.126
  263.8 3.3 %gather_fusion.4 = bf16[512,2048]{1,0:T(8,128)(2,1)} fusion(bf16[576,2048]{1,0:T(8,128)(2,1)S(1)} %reshape.126, s32[1024]{0:T(1024)S(1)} %pad_clamp_fusion), kind=kCustom, calls=%fused_computation.4 | custom fusion | bytes 4196352 | tf_op jit(solution)/shard_map/gather | solution.py:229
  267.1 2.8 reshape.127
  269.9 2.8 fusion.21
  273.4 36.7 %all-to-all-done.3 = bf16[16,36,2048]{2,1,0:T(8,128)(2,1)} async-done(((bf16[16,36,2048]{2,1,0:T(8,128)(2,1)}), bf16[16,36,2048]{2,1,0:T(8,128)(2,1)}, u32[]{:S(2)}, u32[]{:S(2)}) %all-to-all-start.3) | async-done | bytes 2359328 | tf_op jit(solution)/shard_map/all_to_all | solution.py:211
  310.0 2.7 reshape.123
  312.7 3.3 %gather_fusion.3 = bf16[512,2048]{1,0:T(8,128)(2,1)} fusion(bf16[576,2048]{1,0:T(8,128)(2,1)S(1)} %reshape.123, s32[1024]{0:T(1024)S(1)} %pad_clamp_fusion), kind=kCustom, calls=%fused_computation.3 | custom fusion | bytes 4196352 | tf_op jit(solution)/shard_map/gather | solution.py:226
  316.0 4.2 %reshape.124 = bf16[128,4,2048]{2,1,0:T(4,128)(2,1)} reshape(bf16[512,2048]{1,0:T(8,128)(2,1)} %gather_fusion.3) | data formatting | bytes 4194304 | tf_op jit(solution)/shard_map/reshape | solution.py:226
  320.2 5.0 %reduce_sum.25 = bf16[128,2048]{1,0:T(8,128)(2,1)} reduce(bf16[128,4,2048]{2,1,0:T(4,128)(2,1)} %reshape.124, bf16[]{:T(256)} %constant.20.clone.1), dimensions={1}, to_apply=%region_4.5 | reduce | flops 786432 | bytes 2621442 | tf_op jit(solution)/shard_map/reduce_sum | solution.py:235
  (110 shorter events, 42.9 us)
Async XLA Ops:
  0.6 168.4 %copy-start = (bf16[1,768,2048]{2,1,0:T(8,128)(2,1)S(1)}, bf16[1,768,2048]{2,1,0:T(8,128)(2,1)}, u32[]{:S(2)}) copy-start(bf16[1,768,2048]{2,1,0:T(8,128)(2,1)} %param.19) | copy-start | bytes 9437188
  12.5 20.2 %all-to-all-start = ((bf16[16,1,36]{2,1,0:T(2,128)(2,1)}), bf16[16,1,36]{2,1,0:T(2,128)(2,1)S(1)}, u32[]{:S(2)}, u32[]{:S(2)}) async-start(bf16[16,1,36]{2,1,0:T(2,128)(2,1)} %convert_element_type.91), calls=%async_computation | async-start | bytes 16384 | tf_op jit(solution)/shard_map/all_to_all | solution.py:198
  32.6 65.0 %all-to-all-start.2 = ((bf16[16,36,2048]{2,1,0:T(8,128)(2,1)}), bf16[16,36,2048]{2,1,0:T(8,128)(2,1)}, u32[]{:S(2)}, u32[]{:S(2)}) async-start(bf16[16,36,2048]{2,1,0:T(8,128)(2,1)} %reshape.120), calls=%async_computation.2 | async-start | bytes 5242880 | tf_op jit(solution)/shard_map/all_to_all | solution.py:196
  97.6 63.7 %all-to-all-start.1 = ((bf16[16,36,2048]{2,1,0:T(8,128)(2,1)}), bf16[16,36,2048]{2,1,0:T(8,128)(2,1)}, u32[]{:S(2)}, u32[]{:S(2)}) async-start(bf16[16,36,2048]{2,1,0:T(8,128)(2,1)} %reshape.118), calls=%async_computation.1 | async-start | bytes 5242880 | tf_op jit(solution)/shard_map/all_to_all | solution.py:197
  102.4 4.2 %copy-start.12 = (bf16[1,32,2048]{2,1,0:T(8,128)(2,1)S(1)}, bf16[1,32,2048]{2,1,0:T(8,128)(2,1)}, u32[]{:S(2)}) copy-start(bf16[1,32,2048]{2,1,0:T(8,128)(2,1)} %param.20) | copy-start | bytes 393220
  106.6 3.2 copy-start.2
  106.6 3.2 copy-start.14
  111.3 5.3 %copy-start.28 = (bf16[1,2048,768]{2,1,0:T(8,128)(2,1)S(1)}, bf16[1,2048,768]{2,1,0:T(8,128)(2,1)}, u32[]{:S(2)}) copy-start(bf16[1,2048,768]{2,1,0:T(8,128)(2,1)} %param.18) | copy-start | bytes 9437188
  119.8 45.6 %copy-start.11 = (bf16[1,32,2048]{2,1,0:T(8,128)(2,1)S(1)}, bf16[1,32,2048]{2,1,0:T(8,128)(2,1)}, u32[]{:S(2)}) copy-start(bf16[1,32,2048]{2,1,0:T(8,128)(2,1)} %param.25) | copy-start | bytes 393220
  165.4 3.2 copy-start.23
  165.4 3.7 %copy-start.4 = (bf16[576,2048]{1,0:T(8,128)(2,1)S(1)}, bf16[576,2048]{1,0:T(8,128)(2,1)}, u32[]{:S(2)}) copy-start(bf16[576,2048]{1,0:T(8,128)(2,1)} %reshape.119) | copy-start | bytes 7077892
  169.1 2.1 copy-start.10
  169.1 2.1 copy-start.15
  169.1 2.1 copy-start.21
  171.2 1.5 copy-start.31
  176.1 2.0 copy-start.19
  181.2 4.8 %copy-start.22 = (bf16[1,32,768]{2,1,0:T(8,128)(2,1)S(1)}, bf16[1,32,768]{2,1,0:T(8,128)(2,1)}, u32[]{:S(2)}) copy-start(bf16[1,32,768]{2,1,0:T(8,128)(2,1)} %param.21) | copy-start | bytes 147460
  181.2 6.4 %copy-start.27 = (bf16[1,32,768]{2,1,0:T(8,128)(2,1)S(1)}, bf16[1,32,768]{2,1,0:T(8,128)(2,1)}, u32[]{:S(2)}) copy-start(bf16[1,32,768]{2,1,0:T(8,128)(2,1)} %param.23) | copy-start | bytes 147460
  181.2 63.7 %all-to-all-start.4 = ((bf16[16,36,2048]{2,1,0:T(8,128)(2,1)}), bf16[16,36,2048]{2,1,0:T(8,128)(2,1)S(1)}, u32[]{:S(2)}, u32[]{:S(2)}) async-start(bf16[16,36,2048]{2,1,0:T(8,128)(2,1)} %reshape.125), calls=%async_computation.4 | async-start | bytes 5242880 | tf_op jit(solution)/shard_map/all_to_all | solution.py:218
  189.1 2.2 copy-start.29
  191.3 2.0 copy-start.8
  191.3 2.2 copy-start.30
  202.1 49.0 %copy-start.18 = (bf16[576,32]{0,1:T(8,128)(2,1)S(1)}, bf16[576,32]{0,1:T(8,128)(2,1)}, u32[]{:S(2)}) copy-start(bf16[576,32]{0,1:T(8,128)(2,1)} %copy-done.17) | copy-start | bytes 110596
  202.1 51.2 %copy-start.16 = (bf16[576,32]{0,1:T(8,128)(2,1)S(1)}, bf16[576,32]{0,1:T(8,128)(2,1)}, u32[]{:S(2)}) copy-start(bf16[576,32]{0,1:T(8,128)(2,1)} %convolution_convert_fusion.3) | copy-start | bytes 110596
  202.1 53.3 %copy-start.25 = (bf16[576,32]{0,1:T(8,128)(2,1)S(1)}, bf16[576,32]{0,1:T(8,128)(2,1)}, u32[]{:S(2)}) copy-start(bf16[576,32]{0,1:T(8,128)(2,1)} %convolution_convert_fusion.4) | copy-start | bytes 110596
  244.9 1.5 copy-start.6
  246.4 63.7 %all-to-all-start.3 = ((bf16[16,36,2048]{2,1,0:T(8,128)(2,1)}), bf16[16,36,2048]{2,1,0:T(8,128)(2,1)}, u32[]{:S(2)}, u32[]{:S(2)}) async-start(bf16[16,36,2048]{2,1,0:T(8,128)(2,1)} %reshape.122), calls=%async_computation.3 | async-start | bytes 5242880 | tf_op jit(solution)/shard_map/all_to_all | solution.py:211
  251.0 6.4 %copy-start.3 = (bf16[576,2048]{1,0:T(8,128)(2,1)S(1)}, bf16[576,2048]{1,0:T(8,128)(2,1)}, u32[]{:S(2)}) copy-start(bf16[576,2048]{1,0:T(8,128)(2,1)} %reshape.121) | copy-start | bytes 7077892
  257.4 2.5 copy-start.5
  257.4 2.5 copy-start.20
  267.1 2.8 copy-start.13
  316.0 9.2 %copy-start.1 = (bf16[1,768,2048]{2,1,0:T(8,128)(2,1)S(1)}, bf16[1,768,2048]{2,1,0:T(8,128)(2,1)}, u32[]{:S(2)}) copy-start(bf16[1,768,2048]{2,1,0:T(8,128)(2,1)} %param.19) | copy-start | bytes 9437188
  (5 other events, 4.3 us)
where the time goes:
time: 327 us; the launch traced here: 325 us
  waiting for transfers between devices  166 us (51%)
  local copies, waits for them, and re-layouts  77.1 us (24%)
  matrix products  47.5 us (15%)
  starting transfers between devices  26.4 us (8%)
  other arithmetic  7.16 us (2%)
    all_to_all x1, waiting for transfers between devices, on_device(): lax.all_to_all(send_tokens, 'expert', split_axis=0, concat_axis=0, tiled=...  45 us
    all_to_all x1, waiting for transfers between devices, on_device(): lax.all_to_all(layer_output.reshape(experts, capacity, width), 'expert',...  42.8 us
    all_to_all x1, waiting for transfers between devices, on_device(): lax.all_to_all(send_grads, 'expert', split_axis=0, concat_axis=0, tiled=T...  41.5 us
    all_to_all x1, waiting for transfers between devices, on_device(): lax.all_to_all(input_gradient.reshape(experts, capacity, width), 'expert'...  36.7 us
    gather x1, local copies, waits for them, and re-layouts, on_device(): jnp.concatenate([grad_out, zero_row], axis=0)[source_row]  7.96 us
    gather x1, local copies, waits for them, and re-layouts, on_device(): jnp.concatenate([tokens, zero_row], axis=0)[source_row]  7.95 us
    unnamed x66, local copies, waits for them, and re-layouts  7.05 us
    reshape x2, local copies, waits for them, and re-layouts, on_device(): back_grad.reshape(experts * capacity, width)[target]  6.9 us
  transfers between devices with their start and end apart: 5, of which 4 were waited for; matrix products, arithmetic and copies ran while one was open for 25% of the time, Pallas kernels for 0%

commit v1 on v0

v1 whole, which is shorter than its diff:
```python
import functools

import jax
import jax.numpy as jnp
from jax import lax
from jax.experimental import pallas as pl
from jax.experimental.pallas import tpu as pltpu
from jax.sharding import PartitionSpec as P

SCALE = 2.0
PLANE = 4
LANES = 128
F32 = jnp.float32
BF16 = jnp.bfloat16
VMEM_LIMIT = 40 * 1024 * 1024


def nn(a, b):
    return lax.dot_general(a, b, (((1,), (0,)), ((), ())), preferred_element_type=F32)


def nt(a, b):
    return lax.dot_general(a, b, (((1,), (1,)), ((), ())), preferred_element_type=F32)


def two_parts(value):
    high = value.astype(BF16).astype(F32)
    return high, value - high


def vmem():
    return pl.BlockSpec(memory_space=pltpu.VMEM)


def smem():
    return pl.BlockSpec(memory_space=pltpu.SMEM)


def anywhere():
    return pl.BlockSpec(memory_space=pl.ANY)


def cost(flops, moved, exps=0):
    return pl.CostEstimate(flops=int(flops), bytes_accessed=int(moved), transcendentals=int(exps))


def params():
    return pltpu.CompilerParams(vmem_limit_bytes=VMEM_LIMIT)


def one_hots(names, slots, side, routes):
    turned = side.T
    tokens = side.shape[0]
    earlier = lax.broadcasted_iota(jnp.int32, (tokens, tokens), 0)
    later = lax.broadcasted_iota(jnp.int32, (tokens, tokens), 1)
    ahead = jnp.where(earlier < later, 1.0, 0.0).astype(BF16)
    place = lax.broadcasted_iota(jnp.int32, (slots, tokens), 0).astype(F32)
    found = []
    for name in names:
        hits = [jnp.where(turned[k : k + 1, :] == name, 1.0, 0.0) for k in range(routes)]
        member = sum(hits)
        wide = jnp.broadcast_to(member, (8, tokens)).astype(BF16)
        slot = nn(wide, ahead)[0:1, :]
        found.append((jnp.where((place == slot) & (member > 0.0), 1.0, 0.0), hits))
    return turned, found


def pack_kernel(routes, grad_ref, ids_ref, weight_ref, out_ref):
    width = grad_ref.shape[1]
    out_ref[:, :width] = grad_ref[...]
    names = ids_ref[...].astype(F32) + 1.0
    high, low = two_parts(weight_ref[...])
    lane = lax.broadcasted_iota(jnp.int32, (grad_ref.shape[0], LANES), 1)
    side = jnp.zeros((grad_ref.shape[0], LANES), F32)
    for group, values in enumerate((names, names, high, low)):
        for k in range(routes):
            side = jnp.where(lane == group * routes + k, values[:, k : k + 1], side)
    out_ref[:, width:] = side.astype(BF16)


def select_kernel(routes, slots, choices, info_ref, *refs):
    xs, gs = refs[:choices], refs[choices : 2 * choices]
    outs = refs[2 * choices : 2 * choices + PLANE]
    side_ref, x_buf, g_buf, x_sem, g_sem = refs[2 * choices + PLANE :]
    for i in range(choices):

        @pl.when(info_ref[PLANE] == i)
        def _():
            g_copy = pltpu.make_async_copy(gs[i], g_buf, g_sem)
            x_copy = pltpu.make_async_copy(xs[i], x_buf, x_sem)
            g_copy.start()
            x_copy.start()
            g_copy.wait()
            x_copy.wait()

    width = x_buf.shape[1]
    side_ref[...] = g_buf[:, width:]
    side = g_buf[:, width:].astype(F32)
    names = [info_ref[m].astype(F32) + 1.0 for m in range(PLANE)]
    turned, found = one_hots(names, slots, side, routes)
    lane = lax.broadcasted_iota(jnp.int32, (slots, LANES), 1)
    picks = jnp.concatenate([hot for hot, _ in found], axis=0).astype(BF16)
    x_rows = nn(picks, x_buf[...])
    g_rows = nn(picks, g_buf[:, :width])
    for m, (hot, hits) in enumerate(found):
        rows = slice(m * slots, (m + 1) * slots)
        outs[m][:, :width] = x_rows[rows].astype(BF16)
        outs[m][:, width : 2 * width] = g_rows[rows].astype(BF16)
        parts = []
        for group in (2, 3):
            weight = sum(hits[k] * turned[group * routes + k : group * routes + k + 1, :] for k in range(routes))
            parts.append(jnp.sum(hot * weight, axis=1, keepdims=True))
        outs[m][:, 2 * width :] = jnp.where(lane == 0, parts[0], jnp.where(lane == 1, parts[1], 0.0)).astype(BF16)


def stacked(refs, low, high):
    return jnp.concatenate([r[:, low:high].astype(F32) for r in refs], axis=0)


def expert_kernel(routes, slots, rank, *refs):
    rows_in = refs[:PLANE]
    gate_w, up_w, down_w, gate_a, gate_b, up_a, up_b, down_a, down_b = refs[PLANE : PLANE + 9]
    outs = refs[PLANE + 9 : 2 * PLANE + 9]
    acts_ref, lows_ref = refs[2 * PLANE + 9 :]
    width, hidden_units = gate_w.shape
    x = stacked(rows_in, 0, width).astype(BF16)
    g = stacked(rows_in, width, 2 * width).astype(BF16)
    side = stacked(rows_in, 2 * width, 2 * width + LANES)
    weight = side[:, 0:1] + side[:, 1:2]

    low_gate = nt(x, gate_a[...]).astype(BF16)
    low_up = nt(x, up_a[...]).astype(BF16)
    gate_pre = nn(x, gate_w[...]) + SCALE * nn(low_gate, gate_b[...])
    up_pre = nn(x, up_w[...]) + SCALE * nn(low_up, up_b[...])
    q = jax.nn.sigmoid(gate_pre)
    silu = gate_pre * q
    hidden = (silu * up_pre).astype(BF16)
    low_down = nt(hidden, down_a[...]).astype(BF16)
    g_hidden = nt(g, down_w[...])
    g_low = nt(g, down_b[...])
    dots = jnp.sum(hidden.astype(F32) * g_hidden, axis=1, keepdims=True) + SCALE * jnp.sum(
        low_down.astype(F32) * g_low, axis=1, keepdims=True
    )
    down_back = (weight * g_low).astype(BF16)
    weighted_low = (weight * low_down.astype(F32)).astype(BF16)
    grad_hidden = weight * g_hidden + SCALE * nn(down_back, down_a[...])
    gate_grad = (grad_hidden * up_pre * q * (1.0 + gate_pre * (1.0 - q))).astype(BF16)
    up_grad = (grad_hidden * silu).astype(BF16)
    gate_back = nt(gate_grad, gate_b[...]).astype(BF16)
    up_back = nt(up_grad, up_b[...]).astype(BF16)
    input_grad = (
        nt(gate_grad, gate_w[...])
        + nt(up_grad, up_w[...])
        + SCALE * (nn(gate_back, gate_a[...]) + nn(up_back, up_a[...]))
    )
    high, low = two_parts(dots)
    lane = lax.broadcasted_iota(jnp.int32, (PLANE * slots, LANES), 1)
    side_back = jnp.where(lane < routes, high, jnp.where(lane < 2 * routes, low, 0.0))
    for m in range(PLANE):
        rows = slice(m * slots, (m + 1) * slots)
        outs[m][:, :width] = input_grad[rows].astype(BF16)
        outs[m][:, width:] = side_back[rows].astype(BF16)
    acts_ref[:, :hidden_units] = hidden
    acts_ref[:, hidden_units : 2 * hidden_units] = gate_grad
    acts_ref[:, 2 * hidden_units :] = up_grad
    for i, value in enumerate((gate_back, low_gate, up_back, low_up, down_back, weighted_low)):
        lows_ref[:, i * rank : (i + 1) * rank] = value.astype(F32)
    lows_ref[:, 6 * rank :] = jnp.zeros((PLANE * slots, lows_ref.shape[1] - 6 * rank), F32)


def combine_kernel(routes, slots, info_ref, side_ref, *refs):
    backs, out_ref = refs[:PLANE], refs[PLANE]
    width = backs[0].shape[1] - LANES
    side = side_ref[...].astype(F32)
    names = [info_ref[m].astype(F32) + 1.0 for m in range(PLANE)]
    _, found = one_hots(names, slots, side, routes)
    turned = [hot.T.astype(BF16) for hot, _ in found]
    total = jnp.zeros((side.shape[0], LANES), F32)
    for m in range(PLANE):
        total = total + jnp.where(side == names[m], nn(turned[m], backs[m][:, width:]), 0.0)
    out_ref[:, width:] = total.astype(BF16)
    rows = stacked(backs, 0, width).astype(BF16)
    picks = jnp.concatenate([hot for hot, _ in found], axis=0)
    out_ref[:, :width] = lax.dot_general(
        picks.astype(BF16), rows, (((0,), (0,)), ((), ())), preferred_element_type=F32
    ).astype(BF16)


def finish_kernel(routes, *refs):
    parts, (tokens_ref, combine_ref) = refs[:-2], refs[-2:]
    width = tokens_ref.shape[1]
    tokens_ref[...] = sum(r[:, :width].astype(F32) for r in parts).astype(BF16)
    side = sum(r[:, width:].astype(F32) for r in parts)
    combine_ref[...] = side[:, :routes] + side[:, routes : 2 * routes]


def adapter_kernel(stages, rank, *refs):
    rows_in = refs[: stages * PLANE]
    acts = refs[stages * PLANE : stages * (PLANE + 1)]
    lows = refs[stages * (PLANE + 1) : stages * (PLANE + 2)]
    gate_in, gate_out, up_in, up_out, down_in, down_out = refs[stages * (PLANE + 2) :]
    width, hidden_units = gate_in.shape[2], gate_out.shape[2]
    turned = jnp.concatenate([r[...] for r in lows], axis=0).T.astype(BF16)
    part = [turned[i * rank : (i + 1) * rank] for i in range(6)]
    x = stacked(rows_in, 0, width).astype(BF16)
    g = stacked(rows_in, width, 2 * width).astype(BF16)
    hidden = jnp.concatenate([r[:, :hidden_units] for r in acts], axis=0)
    gate_grad = jnp.concatenate([r[:, hidden_units : 2 * hidden_units] for r in acts], axis=0)
    up_grad = jnp.concatenate([r[:, 2 * hidden_units :] for r in acts], axis=0)
    gate_in[0] = SCALE * nn(part[0], x)
    gate_out[0] = SCALE * nn(part[1], gate_grad)
    up_in[0] = SCALE * nn(part[2], x)
    up_out[0] = SCALE * nn(part[3], up_grad)
    down_in[0] = SCALE * nn(part[4], hidden)
    down_out[0] = SCALE * nn(part[5], g)


def on_device(tokens, grad_out, expert_ids, combine, *weights):
    rows, width = tokens.shape
    routes = expert_ids.shape[1]
    experts = lax.axis_size("expert")
    planes = experts // PLANE
    capacity = rows * routes * 9 // (8 * experts)
    slots = -(-capacity // 8) * 8
    matrices = [w[0] for w in weights]
    hidden_units = matrices[0].shape[1]
    rank = matrices[3].shape[0]
    low_lanes = -(-6 * rank // LANES) * LANES
    wide = width + LANES
    shape = jax.ShapeDtypeStruct

    me = lax.axis_index("expert").astype(jnp.int32)
    here, seat = me // PLANE, me % PLANE
    names = jnp.stack([here * PLANE + (seat ^ m) for m in range(PLANE)])

    def along(value, step):
        pairs = [
            (p * PLANE + s, (p + step) * PLANE + s) for p in range(planes) for s in range(PLANE) if 0 <= p + step < planes
        ]
        return lax.ppermute(value, "expert", pairs)

    def flipped(value, mask):
        return lax.ppermute(value, "expert", [(i, i ^ mask) for i in range(experts)])

    packed = pl.pallas_call(
        functools.partial(pack_kernel, routes),
        out_shape=shape((rows, wide), BF16),
        in_specs=[vmem()] * 3,
        out_specs=vmem(),
        compiler_params=params(),
        cost_estimate=cost(0, 4 * rows * width),
        name="pack",
    )(grad_out, expert_ids, combine)

    blocks = {0: (tokens, packed)}
    for step in range(1, planes):
        for sign in (1, -1):
            x, g = blocks[sign * (step - 1)]
            blocks[sign * step] = (along(x, -sign), along(g, -sign))

    def select(stage):
        offsets = sorted({(p ^ stage) - p for p in range(planes)}, key=lambda o: (abs(o), o))
        mine = (here ^ stage) - here
        choice = sum(jnp.where(mine == o, i, 0) for i, o in enumerate(offsets))
        info = jnp.concatenate([names, jnp.reshape(choice, (1,))]).astype(jnp.int32)
        choices = len(offsets)
        return pl.pallas_call(
            functools.partial(select_kernel, routes, slots, choices),
            out_shape=[shape((slots, 2 * width + LANES), BF16)] * PLANE + [shape((rows, LANES), BF16)],
            in_specs=[smem()] + [anywhere()] * (2 * choices),
            out_specs=[vmem()] * (PLANE + 1),
            scratch_shapes=[
                pltpu.VMEM((rows, width), BF16),
                pltpu.VMEM((rows, wide), BF16),
                pltpu.SemaphoreType.DMA,
                pltpu.SemaphoreType.DMA,
            ],
            compiler_params=params(),
            cost_estimate=cost(4 * PLANE * slots * rows * width, 4 * rows * width + 4 * PLANE * slots * width),
            name="select",
        )(info, *[blocks[o][0] for o in offsets], *[blocks[o][1] for o in offsets])

    def expert(got):
        return pl.pallas_call(
            functools.partial(expert_kernel, routes, slots, rank),
            out_shape=[shape((slots, wide), BF16)] * PLANE
            + [shape((PLANE * slots, 3 * hidden_units), BF16), shape((PLANE * slots, low_lanes), F32)],
            in_specs=[vmem()] * (PLANE + 9),
            out_specs=[vmem()] * (PLANE + 2),
            compiler_params=params(),
            cost_estimate=cost(
                10 * PLANE * slots * width * hidden_units, 6 * width * hidden_units, PLANE * slots * hidden_units
            ),
            name="expert",
        )(*got, *matrices)

    def gather_back(side, backs):
        return pl.pallas_call(
            functools.partial(combine_kernel, routes, slots),
            out_shape=shape((rows, wide), BF16),
            in_specs=[smem()] + [vmem()] * (PLANE + 1),
            out_specs=vmem(),
            compiler_params=params(),
            cost_estimate=cost(2 * PLANE * slots * rows * width, 2 * (rows + PLANE * slots) * width),
            name="combine",
        )(names, side, *backs)

    parts, received, acts, lows = [], [], [], []
    for stage in range(planes):
        *picked, side = select(stage)
        got = [picked[0]] + [flipped(picked[m], m) for m in range(1, PLANE)]
        *backs, act, low = expert(got)
        returned = [backs[0]] + [flipped(backs[m], m) for m in range(1, PLANE)]
        part = gather_back(side, returned)
        parts.append(part if stage == 0 else flipped(part, stage * PLANE))
        received += got
        acts.append(act)
        lows.append(low)

    grad_tokens, grad_combine = pl.pallas_call(
        functools.partial(finish_kernel, routes),
        out_shape=[shape((rows, width), BF16), shape((rows, routes), F32)],
        in_specs=[vmem()] * planes,
        out_specs=[vmem()] * 2,
        compiler_params=params(),
        cost_estimate=cost(0, 2 * (planes + 1) * rows * width),
        name="finish",
    )(*parts)
    sides = [width, hidden_units, width, hidden_units, hidden_units, width]
    total = planes * PLANE * slots
    grads = pl.pallas_call(
        functools.partial(adapter_kernel, planes, rank),
        out_shape=[shape((1, rank, s), F32) for s in sides],
        in_specs=[vmem()] * (planes * (PLANE + 2)),
        out_specs=[vmem()] * 6,
        compiler_params=params(),
        cost_estimate=cost(2 * rank * total * sum(sides), total * (4 * width + 6 * hidden_units)),
        name="adapter_grads",
    )(*received, *acts, *lows)
    return (grad_tokens, grad_combine, *grads)


def solution(mesh):
    by_token = P(("groups", "expert"), None)
    by_part = P(("groups", "expert"), None, None)
    return jax.shard_map(
        on_device,
        mesh=mesh,
        in_specs=(by_token,) * 4 + (P("expert", None, None),) * 9,
        out_specs=(by_token,) * 2 + (by_part,) * 6,
        check_vma=False,
    )
```

time: 327 us -> 210 us (0.64)
  waiting for transfers between devices: 166 us -> 61.7 us
  Pallas kernels: 0 us -> 47.9 us
  matrix products: 47.5 us -> 0 us
  local copies, waits for them, and re-layouts: 77.1 us -> 36 us
  starting transfers between devices: 26.4 us -> 61.5 us
  other arithmetic: 7.16 us -> 0.08 us
    all_to_all x5 -> x0, waiting for transfers between devices: 166 us -> none  [the longest x1 45 us: on_device(): lax.all_to_all(send_tokens, 'expert', split_axis=0, concat_axis=0, tiled=...]
    ppermute x0 -> x39, waiting for transfers between devices: none -> 61.7 us  [the longest x27 40.8 us: flipped(): lax.ppermute(value, 'expert', [(i, i ^ mask) for i in range(experts)])]
    ppermute x0 -> x39, starting transfers between devices: none -> 61.5 us  [the longest x12 38 us: along(): return lax.ppermute(value, 'expert', pairs)]
    pallas_call x0 -> x15, Pallas kernels: none -> 47.9 us  [the longest x4 27.7 us: expert(): pl.pallas_call(functools.partial(expert_kernel, routes, slots, rank), out...]
    dot_general x25 -> x0, matrix products: 47.5 us -> none  [the longest x1 5.28 us: expert_forward(): jnp.dot(input_token_rows, gate_weight_matrix, preferred_element_type=jnp....]
    reshape x11 -> x0, local copies, waits for them, and re-layouts: 35.3 us -> none  [the longest x2 6.9 us: on_device(): back_grad.reshape(experts * capacity, width)[target]]
    unnamed x66 -> x147, local copies, waits for them, and re-layouts: 7.05 us -> 35.6 us
    gather x5 -> x0, local copies, waits for them, and re-layouts: 26.4 us -> none  [the longest x1 7.96 us: on_device(): jnp.concatenate([grad_out, zero_row], axis=0)[source_row]]
  transfers between devices with their start and end apart: 5 -> 39, of which waited for: 4 -> 14; matrix products, arithmetic and copies ran while one was open for 25% -> 1% of each run, Pallas kernels for 0% -> 22%
where the time goes in v1:
time: 210 us; the launch traced here: 208 us
  waiting for transfers between devices  61.7 us (29%)
  starting transfers between devices  61.5 us (29%)
  Pallas kernels  47.9 us (23%)
  local copies, waits for them, and re-layouts  36 us (17%)
    ppermute x27, waiting for transfers between devices, flipped(): lax.ppermute(value, 'expert', [(i, i ^ mask) for i in range(experts)])  40.8 us
    ppermute x12, starting transfers between devices, along(): return lax.ppermute(value, 'expert', pairs)  38 us
    unnamed x147, local copies, waits for them, and re-layouts  35.6 us
    pallas_call x4, Pallas kernels, expert(): pl.pallas_call(functools.partial(expert_kernel, routes, slots, rank), out...  27.7 us
    ppermute x27, starting transfers between devices, flipped(): lax.ppermute(value, 'expert', [(i, i ^ mask) for i in range(experts)])  23.5 us
    ppermute x12, waiting for transfers between devices, along(): return lax.ppermute(value, 'expert', pairs)  20.9 us
    pallas_call x4, Pallas kernels, select(): pl.pallas_call(functools.partial(select_kernel, routes, slots, choices),...  8.69 us
    pallas_call x4, Pallas kernels, gather_back(): pl.pallas_call(functools.partial(combine_kernel, routes, slots), out_shap...  5.9 us
  transfers between devices with their start and end apart: 39, of which 14 were waited for; matrix products, arithmetic and copies ran while one was open for 1% of the time, Pallas kernels for 22%

profile of v1, /device:TPU:16, one launch (start us, length us, event | category | flops | bytes accessed | tf_op | source)
XLA Modules:
  0.0 208.4 jit_solution(17857136469110404284)
XLA Ops:
  0.6 2.4 %collective-permute-start.7 = (bf16[128,2048]{1,0:T(8,128)(2,1)}, bf16[128,2048]{1,0:T(8,128)(2,1)S(1)}, u32[]{:S(2)}, u32[]{:S(2)}) collective-permute-start(bf16[128,2048]{1,0:T(8,128)(2,1)} %refs_0_.1), channel_id=1, source_target_pairs={{4,0},{5,1},{6,2},{7,3},{8,4},{9,5},{10,6},{11,7},{12,8},{13,9},{1... | collective-permute-start | bytes 1572872 | tf_op jit(solution)/shard_map/ppermute | solution.py:240
  3.0 3.5 %collective-permute-start.6 = (bf16[128,2048]{1,0:T(8,128)(2,1)}, bf16[128,2048]{1,0:T(8,128)(2,1)S(1)}, u32[]{:S(2)}, u32[]{:S(2)}) collective-permute-start(bf16[128,2048]{1,0:T(8,128)(2,1)} %refs_0_.1), channel_id=1, source_target_pairs={{0,4},{1,5},{2,6},{3,7},{4,8},{5,9},{6,10},{7,11},{8,12},{9,13},{1... | collective-permute-start | bytes 1572872 | tf_op jit(solution)/shard_map/ppermute | solution.py:240
  9.3 2.3 %collective-permute-start.9 = (bf16[128,2176]{1,0:T(8,128)(2,1)S(1)}, bf16[128,2176]{1,0:T(8,128)(2,1)S(1)}, u32[]{:S(2)}, u32[]{:S(2)}) collective-permute-start(bf16[128,2176]{1,0:T(8,128)(2,1)S(1)} %pack.1.refs_1_), channel_id=1, source_target_pairs={{4,0},{5,1},{6,2},{7,3},{8,4},{9,5},{10,6},{11,7},{12,8},{13,9},{1... | collective-permute-start | bytes 1671176 | tf_op jit(solution)/shard_map/ppermute | solution.py:240
  11.7 3.5 %collective-permute-start.8 = (bf16[128,2176]{1,0:T(8,128)(2,1)S(1)}, bf16[128,2176]{1,0:T(8,128)(2,1)S(1)}, u32[]{:S(2)}, u32[]{:S(2)}) collective-permute-start(bf16[128,2176]{1,0:T(8,128)(2,1)S(1)} %pack.1.refs_1_), channel_id=1, source_target_pairs={{0,4},{1,5},{2,6},{3,7},{4,8},{5,9},{6,10},{7,11},{8,12},{9,13},{1... | collective-permute-start | bytes 1671176 | tf_op jit(solution)/shard_map/ppermute | solution.py:240
  17.6 2.3 %collective-permute-start.18 = (bf16[128,2048]{1,0:T(8,128)(2,1)S(1)}, bf16[128,2048]{1,0:T(8,128)(2,1)}, u32[]{:S(2)}, u32[]{:S(2)}) collective-permute-start(bf16[128,2048]{1,0:T(8,128)(2,1)S(1)} %collective-permute-done.7.refs_1_), channel_id=1, source_target_pairs={{4,0},{5,1},{6,2},{7,3},{8,4},{9,5},{10,6},{11,7},{12,8},{13,9},{1... | collective-permute-start | bytes 1572872 | tf_op jit(solution)/shard_map/ppermute | solution.py:240
  20.0 4.2 %collective-permute-start.17 = (bf16[128,2048]{1,0:T(8,128)(2,1)S(1)}, bf16[128,2048]{1,0:T(8,128)(2,1)}, u32[]{:S(2)}, u32[]{:S(2)}) collective-permute-start(bf16[128,2048]{1,0:T(8,128)(2,1)S(1)} %collective-permute-done.6.refs_0_), channel_id=1, source_target_pairs={{0,4},{1,5},{2,6},{3,7},{4,8},{5,9},{6,10},{7,11},{8,12},{9,13},{1... | collective-permute-start | bytes 1572872 | tf_op jit(solution)/shard_map/ppermute | solution.py:240
  24.2 5.3 %collective-permute-done.9.refs_3_.refs_5_ = bf16[128,2176]{1,0:T(8,128)(2,1)S(1)} collective-permute-done((bf16[128,2176]{1,0:T(8,128)(2,1)S(1)}, bf16[128,2176]{1,0:T(8,128)(2,1)S(1)}, u32[]{:S(2)}, u32[]{:S(2)}) %collective-permute-start.9) | collective-permute-done | bytes 557088 | tf_op jit(solution)/shard_map/ppermute | solution.py:240
  29.5 2.3 %collective-permute-start.20 = (bf16[128,2176]{1,0:T(8,128)(2,1)S(1)}, bf16[128,2176]{1,0:T(8,128)(2,1)}, u32[]{:S(2)}, u32[]{:S(2)}) collective-permute-start(bf16[128,2176]{1,0:T(8,128)(2,1)S(1)} %collective-permute-done.9.refs_3_.refs_5_), channel_id=1, source_target_pairs={{4,0},{5,1},{6,2},{7,3},{8,4},{9,5},{10,6},{11,7},{12,8},{13,9},{1... | collective-permute-start | bytes 1671176 | tf_op jit(solution)/shard_map/ppermute | solution.py:240
  31.9 4.2 %collective-permute-start.19 = (bf16[128,2176]{1,0:T(8,128)(2,1)S(1)}, bf16[128,2176]{1,0:T(8,128)(2,1)}, u32[]{:S(2)}, u32[]{:S(2)}) collective-permute-start(bf16[128,2176]{1,0:T(8,128)(2,1)S(1)} %collective-permute-done.8.refs_2_.refs_4_), channel_id=1, source_target_pairs={{0,4},{1,5},{2,6},{3,7},{4,8},{5,9},{6,10},{7,11},{8,12},{9,13},{1... | collective-permute-start | bytes 1671176 | tf_op jit(solution)/shard_map/ppermute | solution.py:240
  36.1 4.7 %collective-permute-done.18.refs_1_ = bf16[128,2048]{1,0:T(8,128)(2,1)} collective-permute-done((bf16[128,2048]{1,0:T(8,128)(2,1)S(1)}, bf16[128,2048]{1,0:T(8,128)(2,1)}, u32[]{:S(2)}, u32[]{:S(2)}) %collective-permute-start.18) | collective-permute-done | bytes 524320 | tf_op jit(solution)/shard_map/ppermute | solution.py:240
  40.8 2.3 %collective-permute-start.29 = (bf16[128,2048]{1,0:T(8,128)(2,1)}, bf16[128,2048]{1,0:T(8,128)(2,1)}, u32[]{:S(2)}, u32[]{:S(2)}) collective-permute-start(bf16[128,2048]{1,0:T(8,128)(2,1)} %collective-permute-done.18.refs_1_), channel_id=1, source_target_pairs={{4,0},{5,1},{6,2},{7,3},{8,4},{9,5},{10,6},{11,7},{12,8},{13,9},{1... | collective-permute-start | bytes 1572872 | tf_op jit(solution)/shard_map/ppermute | solution.py:240
  43.2 4.2 %collective-permute-start.28 = (bf16[128,2048]{1,0:T(8,128)(2,1)}, bf16[128,2048]{1,0:T(8,128)(2,1)}, u32[]{:S(2)}, u32[]{:S(2)}) collective-permute-start(bf16[128,2048]{1,0:T(8,128)(2,1)} %collective-permute-done.17.refs_0_), channel_id=1, source_target_pairs={{0,4},{1,5},{2,6},{3,7},{4,8},{5,9},{6,10},{7,11},{8,12},{9,13},{1... | collective-permute-start | bytes 1572872 | tf_op jit(solution)/shard_map/ppermute | solution.py:240
  47.6 2.1 select.11
  52.8 2.3 %collective-permute-start.31 = (bf16[128,2176]{1,0:T(8,128)(2,1)}, bf16[128,2176]{1,0:T(8,128)(2,1)}, u32[]{:S(2)}, u32[]{:S(2)}) collective-permute-start(bf16[128,2176]{1,0:T(8,128)(2,1)} %collective-permute-done.20.refs_3_), channel_id=1, source_target_pairs={{4,0},{5,1},{6,2},{7,3},{8,4},{9,5},{10,6},{11,7},{12,8},{13,9},{1... | collective-permute-start | bytes 1671176 | tf_op jit(solution)/shard_map/ppermute | solution.py:240
  55.2 4.2 %collective-permute-start.30 = (bf16[128,2176]{1,0:T(8,128)(2,1)}, bf16[128,2176]{1,0:T(8,128)(2,1)}, u32[]{:S(2)}, u32[]{:S(2)}) collective-permute-start(bf16[128,2176]{1,0:T(8,128)(2,1)} %collective-permute-done.19.refs_2_), channel_id=1, source_target_pairs={{0,4},{1,5},{2,6},{3,7},{4,8},{5,9},{6,10},{7,11},{8,12},{9,13},{1... | collective-permute-start | bytes 1671176 | tf_op jit(solution)/shard_map/ppermute | solution.py:240
  59.5 3.7 %select.12 = (bf16[40,4224]{1,0:T(8,128)(2,1)S(1)}, bf16[40,4224]{1,0:T(8,128)(2,1)}, bf16[40,4224]{1,0:T(8,128)(2,1)}, bf16[40,4224]{1,0:T(8,128)(2,1)}, bf16[128,128]{1,0:T(8,128)(2,1)S(1)}) custom-call(s32[5]{0:T(128)S(1)} %concatenate.18.info_ref, bf16[128,2048]{1,0:T(8,128)(2,1)} %collective-permute-done.17.refs_0_, ...), custom_call_target="tpu_custom_call" | custom-call | flops 167772160 | bytes 2359296 | tf_op jit(solution)/shard_map/select/pallas_call | solution.py:267
  66.7 8.0 %collective-permute-done.31.refs_7_ = bf16[128,2176]{1,0:T(8,128)(2,1)} collective-permute-done((bf16[128,2176]{1,0:T(8,128)(2,1)}, bf16[128,2176]{1,0:T(8,128)(2,1)}, u32[]{:S(2)}, u32[]{:S(2)}) %collective-permute-start.31) | collective-permute-done | bytes 557088 | tf_op jit(solution)/shard_map/ppermute | solution.py:240
  82.8 1.7 collective-permute-start.32
  86.0 1.9 copy-done.3
  88.8 7.6 %expert.5 = (bf16[40,2176]{1,0:T(8,128)(2,1)S(1)}, bf16[40,2176]{1,0:T(8,128)(2,1)S(1)}, bf16[40,2176]{1,0:T(8,128)(2,1)S(1)}, bf16[40,2176]{1,0:T(8,128)(2,1)},...) custom-call(bf16[40,4224]{1,0:T(8,128)(2,1)S(1)} %copy-done.19, ...), custom_call_target="tpu_custom_call" | custom-call | flops 2516582400 | bytes 9437184 | tf_op jit(solution)/shard_map/expert/pallas_call | solution.py:284
  99.9 7.7 %expert.6 = (bf16[40,2176]{1,0:T(8,128)(2,1)S(1)}, bf16[40,2176]{1,0:T(8,128)(2,1)}, bf16[40,2176]{1,0:T(8,128)(2,1)}, bf16[40,2176]{1,0:T(8,128)(2,1)}, bf16[16...) custom-call(bf16[40,4224]{1,0:T(8,128)(2,1)S(1)} %copy-done.22, bf16[40,4224]{1,0:T(8,128)(2,1)} %collective-permute-done.21.refs_1_.refs_9_, ...), custom_call_target="tpu_custom_call" | custom-call | flops 2516582400 | bytes 9437184 | tf_op jit(solution)/shard_map/expert/pallas_call | solution.py:284
  112.0 6.6 %expert.7 = (bf16[40,2176]{1,0:T(8,128)(2,1)S(1)}, bf16[40,2176]{1,0:T(8,128)(2,1)}, bf16[40,2176]{1,0:T(8,128)(2,1)S(1)}, bf16[40,2176]{1,0:T(8,128)(2,1)S(1)},...) custom-call(bf16[40,4224]{1,0:T(8,128)(2,1)S(1)} %get-tuple-element.88.refs_0_.refs_12_, ...), custom_call_target="tpu_custom_call" | custom-call | flops 2516582400 | bytes 9437184 | tf_op jit(solution)/shard_map/expert/pallas_call | solution.py:284
  140.9 9.7 %collective-permute-done.36.refs_2_ = bf16[40,2176]{1,0:T(8,128)(2,1)S(1)} collective-permute-done((bf16[40,2176]{1,0:T(8,128)(2,1)}, bf16[40,2176]{1,0:T(8,128)(2,1)S(1)}, u32[]{:S(2)}, u32[]{:S(2)}) %collective-permute-start.36) | collective-permute-done | bytes 174112 | tf_op jit(solution)/shard_map/ppermute | solution.py:243
  150.6 2.9 %collective-permute-start.16 = (bf16[128,2176]{1,0:T(8,128)(2,1)S(1)}, bf16[128,2176]{1,0:T(8,128)(2,1)S(1)}, u32[]{:S(2)}, u32[]{:S(2)}) collective-permute-start(bf16[128,2176]{1,0:T(8,128)(2,1)S(1)} %combine.5), channel_id=1, source_target_pairs={{0,4},{1,5},{2,6},{3,7},{4,0},{5,1},{6,2},{7,3},{8,12},{9,13},{10,... | collective-permute-start | bytes 1671176 | tf_op jit(solution)/shard_map/ppermute | solution.py:243
  157.4 3.7 %collective-permute-start.38 = (bf16[128,2176]{1,0:T(8,128)(2,1)S(1)}, bf16[128,2176]{1,0:T(8,128)(2,1)S(1)}, u32[]{:S(2)}, u32[]{:S(2)}) collective-permute-start(bf16[128,2176]{1,0:T(8,128)(2,1)S(1)} %combine.7), channel_id=1, source_target_pairs={{0,12},{1,13},{2,14},{3,15},{4,8},{5,9},{6,10},{7,11},{8,4},{9,5},... | collective-permute-start | bytes 1671176 | tf_op jit(solution)/shard_map/ppermute | solution.py:243
  161.2 1.9 copy-done.4
  163.1 5.8 %expert.4 = (bf16[40,2176]{1,0:T(8,128)(2,1)S(1)}, bf16[40,2176]{1,0:T(8,128)(2,1)S(1)}, bf16[40,2176]{1,0:T(8,128)(2,1)S(1)}, bf16[40,2176]{1,0:T(8,128)(2,1)S(...) custom-call(bf16[40,4224]{1,0:T(8,128)(2,1)S(1)} %get-tuple-element.61.refs_0_, ...), custom_call_target="tpu_custom_call" | custom-call | flops 2516582400 | bytes 9437184 | tf_op jit(solution)/shard_map/expert/pallas_call | solution.py:284
  170.9 5.4 %collective-permute-done.4.refs_2_ = bf16[40,2176]{1,0:T(8,128)(2,1)S(1)} collective-permute-done((bf16[40,2176]{1,0:T(8,128)(2,1)S(1)}, bf16[40,2176]{1,0:T(8,128)(2,1)S(1)}, u32[]{:S(2)}, u32[]{:S(2)}) %collective-permute-start.4) | collective-permute-done | bytes 174112 | tf_op jit(solution)/shard_map/ppermute | solution.py:243
  176.3 2.8 %collective-permute-done.5.refs_3_ = bf16[40,2176]{1,0:T(8,128)(2,1)S(1)} collective-permute-done((bf16[40,2176]{1,0:T(8,128)(2,1)S(1)}, bf16[40,2176]{1,0:T(8,128)(2,1)S(1)}, u32[]{:S(2)}, u32[]{:S(2)}) %collective-permute-start.5) | collective-permute-done | bytes 174112 | tf_op jit(solution)/shard_map/ppermute | solution.py:243
  180.4 4.1 %adapter_grads.1 = (f32[1,32,2048]{2,1,0:T(8,128)}, f32[1,32,768]{2,1,0:T(8,128)}, f32[1,32,2048]{2,1,0:T(8,128)}, f32[1,32,768]{2,1,0:T(8,128)}, f32[1,32,768]{2,1,0:T(8,128)}, /*index=5*/f32[1,32,2048]{2,1,0:T(8,128)}) custom-call(bf16[40,4224]{1,0:T(8,128)(2,1)S(1)} %get-tuple-element.61.refs_0_, bf16[40,4224]{1,0:T(8,128)(2,1)S(1)} %collective-permute-done.refs_1_, ...), custom_call_target="tpu_custom_call" | custom-call | flops 346030080 | bytes 8192000 | tf_op jit(solution)/shard_map/adapter_grads/pallas_call | solution.py:331
  184.5 6.6 %collective-permute-done.27.refs_2_ = bf16[128,2176]{1,0:T(8,128)(2,1)S(1)} collective-permute-done((bf16[128,2176]{1,0:T(8,128)(2,1)S(1)}, bf16[128,2176]{1,0:T(8,128)(2,1)S(1)}, u32[]{:S(2)}, u32[]{:S(2)}) %collective-permute-start.27) | collective-permute-done | bytes 557088 | tf_op jit(solution)/shard_map/ppermute | solution.py:243
  191.1 15.4 %collective-permute-done.38.refs_3_ = bf16[128,2176]{1,0:T(8,128)(2,1)S(1)} collective-permute-done((bf16[128,2176]{1,0:T(8,128)(2,1)S(1)}, bf16[128,2176]{1,0:T(8,128)(2,1)S(1)}, u32[]{:S(2)}, u32[]{:S(2)}) %collective-permute-start.38) | collective-permute-done | bytes 557088 | tf_op jit(solution)/shard_map/ppermute | solution.py:243
  (213 shorter events, 61.5 us)
Async XLA Ops:
  3.0 17.0 %collective-permute-start.6 = (bf16[128,2048]{1,0:T(8,128)(2,1)}, bf16[128,2048]{1,0:T(8,128)(2,1)S(1)}, u32[]{:S(2)}, u32[]{:S(2)}) collective-permute-start(bf16[128,2048]{1,0:T(8,128)(2,1)} %refs_0_.1), channel_id=1, source_target_pairs={{0,4},{1,5},{2,6},{3,7},{4,8},{5,9},{6,10},{7,11},{8,12},{9,13},{1... | collective-permute-start | bytes 1572872 | tf_op jit(solution)/shard_map/ppermute | solution.py:240
  9.3 20.1 %collective-permute-start.9 = (bf16[128,2176]{1,0:T(8,128)(2,1)S(1)}, bf16[128,2176]{1,0:T(8,128)(2,1)S(1)}, u32[]{:S(2)}, u32[]{:S(2)}) collective-permute-start(bf16[128,2176]{1,0:T(8,128)(2,1)S(1)} %pack.1.refs_1_), channel_id=1, source_target_pairs={{4,0},{5,1},{6,2},{7,3},{8,4},{9,5},{10,6},{11,7},{12,8},{13,9},{1... | collective-permute-start | bytes 1671176 | tf_op jit(solution)/shard_map/ppermute | solution.py:240
  11.7 20.2 %collective-permute-start.8 = (bf16[128,2176]{1,0:T(8,128)(2,1)S(1)}, bf16[128,2176]{1,0:T(8,128)(2,1)S(1)}, u32[]{:S(2)}, u32[]{:S(2)}) collective-permute-start(bf16[128,2176]{1,0:T(8,128)(2,1)S(1)} %pack.1.refs_1_), channel_id=1, source_target_pairs={{0,4},{1,5},{2,6},{3,7},{4,8},{5,9},{6,10},{7,11},{8,12},{9,13},{1... | collective-permute-start | bytes 1671176 | tf_op jit(solution)/shard_map/ppermute | solution.py:240
  17.6 23.3 %collective-permute-start.18 = (bf16[128,2048]{1,0:T(8,128)(2,1)S(1)}, bf16[128,2048]{1,0:T(8,128)(2,1)}, u32[]{:S(2)}, u32[]{:S(2)}) collective-permute-start(bf16[128,2048]{1,0:T(8,128)(2,1)S(1)} %collective-permute-done.7.refs_1_), channel_id=1, source_target_pairs={{4,0},{5,1},{6,2},{7,3},{8,4},{9,5},{10,6},{11,7},{12,8},{13,9},{1... | collective-permute-start | bytes 1572872 | tf_op jit(solution)/shard_map/ppermute | solution.py:240
  20.0 23.3 %collective-permute-start.17 = (bf16[128,2048]{1,0:T(8,128)(2,1)S(1)}, bf16[128,2048]{1,0:T(8,128)(2,1)}, u32[]{:S(2)}, u32[]{:S(2)}) collective-permute-start(bf16[128,2048]{1,0:T(8,128)(2,1)S(1)} %collective-permute-done.6.refs_0_), channel_id=1, source_target_pairs={{0,4},{1,5},{2,6},{3,7},{4,8},{5,9},{6,10},{7,11},{8,12},{9,13},{1... | collective-permute-start | bytes 1572872 | tf_op jit(solution)/shard_map/ppermute | solution.py:240
  29.5 23.3 %collective-permute-start.20 = (bf16[128,2176]{1,0:T(8,128)(2,1)S(1)}, bf16[128,2176]{1,0:T(8,128)(2,1)}, u32[]{:S(2)}, u32[]{:S(2)}) collective-permute-start(bf16[128,2176]{1,0:T(8,128)(2,1)S(1)} %collective-permute-done.9.refs_3_.refs_5_), channel_id=1, source_target_pairs={{4,0},{5,1},{6,2},{7,3},{8,4},{9,5},{10,6},{11,7},{12,8},{13,9},{1... | collective-permute-start | bytes 1671176 | tf_op jit(solution)/shard_map/ppermute | solution.py:240
  31.9 23.3 %collective-permute-start.19 = (bf16[128,2176]{1,0:T(8,128)(2,1)S(1)}, bf16[128,2176]{1,0:T(8,128)(2,1)}, u32[]{:S(2)}, u32[]{:S(2)}) collective-permute-start(bf16[128,2176]{1,0:T(8,128)(2,1)S(1)} %collective-permute-done.8.refs_2_.refs_4_), channel_id=1, source_target_pairs={{0,4},{1,5},{2,6},{3,7},{4,8},{5,9},{6,10},{7,11},{8,12},{9,13},{1... | collective-permute-start | bytes 1671176 | tf_op jit(solution)/shard_map/ppermute | solution.py:240
  40.8 25.3 %collective-permute-start.29 = (bf16[128,2048]{1,0:T(8,128)(2,1)}, bf16[128,2048]{1,0:T(8,128)(2,1)}, u32[]{:S(2)}, u32[]{:S(2)}) collective-permute-start(bf16[128,2048]{1,0:T(8,128)(2,1)} %collective-permute-done.18.refs_1_), channel_id=1, source_target_pairs={{4,0},{5,1},{6,2},{7,3},{8,4},{9,5},{10,6},{11,7},{12,8},{13,9},{1... | collective-permute-start | bytes 1572872 | tf_op jit(solution)/shard_map/ppermute | solution.py:240
  43.2 23.2 %collective-permute-start.28 = (bf16[128,2048]{1,0:T(8,128)(2,1)}, bf16[128,2048]{1,0:T(8,128)(2,1)}, u32[]{:S(2)}, u32[]{:S(2)}) collective-permute-start(bf16[128,2048]{1,0:T(8,128)(2,1)} %collective-permute-done.17.refs_0_), channel_id=1, source_target_pairs={{0,4},{1,5},{2,6},{3,7},{4,8},{5,9},{6,10},{7,11},{8,12},{9,13},{1... | collective-permute-start | bytes 1572872 | tf_op jit(solution)/shard_map/ppermute | solution.py:240
  52.8 22.0 %collective-permute-start.31 = (bf16[128,2176]{1,0:T(8,128)(2,1)}, bf16[128,2176]{1,0:T(8,128)(2,1)}, u32[]{:S(2)}, u32[]{:S(2)}) collective-permute-start(bf16[128,2176]{1,0:T(8,128)(2,1)} %collective-permute-done.20.refs_3_), channel_id=1, source_target_pairs={{4,0},{5,1},{6,2},{7,3},{8,4},{9,5},{10,6},{11,7},{12,8},{13,9},{1... | collective-permute-start | bytes 1671176 | tf_op jit(solution)/shard_map/ppermute | solution.py:240
  55.2 21.7 %collective-permute-start.30 = (bf16[128,2176]{1,0:T(8,128)(2,1)}, bf16[128,2176]{1,0:T(8,128)(2,1)}, u32[]{:S(2)}, u32[]{:S(2)}) collective-permute-start(bf16[128,2176]{1,0:T(8,128)(2,1)} %collective-permute-done.19.refs_2_), channel_id=1, source_target_pairs={{0,4},{1,5},{2,6},{3,7},{4,8},{5,9},{6,10},{7,11},{8,12},{9,13},{1... | collective-permute-start | bytes 1671176 | tf_op jit(solution)/shard_map/ppermute | solution.py:240
  64.6 18.2 %collective-permute-start.11 = (bf16[40,4224]{1,0:T(8,128)(2,1)}, bf16[40,4224]{1,0:T(8,128)(2,1)}, u32[]{:S(2)}, u32[]{:S(2)}) collective-permute-start(bf16[40,4224]{1,0:T(8,128)(2,1)} %copy-done.69), channel_id=1, source_target_pairs={{0,2},{1,3},{2,0},{3,1},{4,6},{5,7},{6,4},{7,5},{8,10},{9,11},{10,... | collective-permute-start | bytes 1013768 | tf_op jit(solution)/shard_map/ppermute | solution.py:243
  66.1 18.4 %collective-permute-start.12 = (bf16[40,4224]{1,0:T(8,128)(2,1)}, bf16[40,4224]{1,0:T(8,128)(2,1)}, u32[]{:S(2)}, u32[]{:S(2)}) collective-permute-start(bf16[40,4224]{1,0:T(8,128)(2,1)} %copy-done.68), channel_id=1, source_target_pairs={{0,3},{1,2},{2,1},{3,0},{4,7},{5,6},{6,5},{7,4},{8,11},{9,10},{10,... | collective-permute-start | bytes 1013768 | tf_op jit(solution)/shard_map/ppermute | solution.py:243
  66.4 18.6 %collective-permute-start.21 = (bf16[40,4224]{1,0:T(8,128)(2,1)}, bf16[40,4224]{1,0:T(8,128)(2,1)}, u32[]{:S(2)}, u32[]{:S(2)}) collective-permute-start(bf16[40,4224]{1,0:T(8,128)(2,1)} %get-tuple-element.80), channel_id=1, source_target_pairs={{0,1},{1,0},{2,3},{3,2},{4,5},{5,4},{6,7},{7,6},{8,9},{9,8},{10,11... | collective-permute-start | bytes 1013768 | tf_op jit(solution)/shard_map/ppermute | solution.py:243
  74.8 23.9 %collective-permute-start.22 = (bf16[40,4224]{1,0:T(8,128)(2,1)}, bf16[40,4224]{1,0:T(8,128)(2,1)}, u32[]{:S(2)}, u32[]{:S(2)}) collective-permute-start(bf16[40,4224]{1,0:T(8,128)(2,1)} %get-tuple-element.81), channel_id=1, source_target_pairs={{0,2},{1,3},{2,0},{3,1},{4,6},{5,7},{6,4},{7,5},{8,10},{9,11},{10,... | collective-permute-start | bytes 1013768 | tf_op jit(solution)/shard_map/ppermute | solution.py:243
  76.9 22.5 %collective-permute-start.23 = (bf16[40,4224]{1,0:T(8,128)(2,1)}, bf16[40,4224]{1,0:T(8,128)(2,1)}, u32[]{:S(2)}, u32[]{:S(2)}) collective-permute-start(bf16[40,4224]{1,0:T(8,128)(2,1)} %get-tuple-element.82), channel_id=1, source_target_pairs={{0,3},{1,2},{2,1},{3,0},{4,7},{5,6},{6,5},{7,4},{8,11},{9,10},{10,... | collective-permute-start | bytes 1013768 | tf_op jit(solution)/shard_map/ppermute | solution.py:243
  82.8 27.0 %collective-permute-start.32 = (bf16[40,4224]{1,0:T(8,128)(2,1)S(1)}, bf16[40,4224]{1,0:T(8,128)(2,1)S(1)}, u32[]{:S(2)}, u32[]{:S(2)}) collective-permute-start(bf16[40,4224]{1,0:T(8,128)(2,1)S(1)} %get-tuple-element.89), channel_id=1, source_target_pairs={{0,1},{1,0},{2,3},{3,2},{4,5},{5,4},{6,7},{7,6},{8,9},{9,8},{10,11... | collective-permute-start | bytes 1013768 | tf_op jit(solution)/shard_map/ppermute | solution.py:243
  84.5 26.3 %collective-permute-start.33 = (bf16[40,4224]{1,0:T(8,128)(2,1)S(1)}, bf16[40,4224]{1,0:T(8,128)(2,1)S(1)}, u32[]{:S(2)}, u32[]{:S(2)}) collective-permute-start(bf16[40,4224]{1,0:T(8,128)(2,1)S(1)} %get-tuple-element.90), channel_id=1, source_target_pairs={{0,2},{1,3},{2,0},{3,1},{4,6},{5,7},{6,4},{7,5},{8,10},{9,11},{10,... | collective-permute-start | bytes 1013768 | tf_op jit(solution)/shard_map/ppermute | solution.py:243
  85.0 26.5 %collective-permute-start.34 = (bf16[40,4224]{1,0:T(8,128)(2,1)S(1)}, bf16[40,4224]{1,0:T(8,128)(2,1)S(1)}, u32[]{:S(2)}, u32[]{:S(2)}) collective-permute-start(bf16[40,4224]{1,0:T(8,128)(2,1)S(1)} %get-tuple-element.91), channel_id=1, source_target_pairs={{0,3},{1,2},{2,1},{3,0},{4,7},{5,6},{6,5},{7,4},{8,11},{9,10},{10,... | collective-permute-start | bytes 1013768 | tf_op jit(solution)/shard_map/ppermute | solution.py:243
  98.7 23.5 %collective-permute-start.13 = (bf16[40,2176]{1,0:T(8,128)(2,1)S(1)}, bf16[40,2176]{1,0:T(8,128)(2,1)S(1)}, u32[]{:S(2)}, u32[]{:S(2)}) collective-permute-start(bf16[40,2176]{1,0:T(8,128)(2,1)S(1)} %get-tuple-element.75), channel_id=1, source_target_pairs={{0,1},{1,0},{2,3},{3,2},{4,5},{5,4},{6,7},{7,6},{8,9},{9,8},{10,11... | collective-permute-start | bytes 522248 | tf_op jit(solution)/shard_map/ppermute | solution.py:243
  99.4 24.5 %collective-permute-start.14 = (bf16[40,2176]{1,0:T(8,128)(2,1)S(1)}, bf16[40,2176]{1,0:T(8,128)(2,1)S(1)}, u32[]{:S(2)}, u32[]{:S(2)}) collective-permute-start(bf16[40,2176]{1,0:T(8,128)(2,1)S(1)} %get-tuple-element.76), channel_id=1, source_target_pairs={{0,2},{1,3},{2,0},{3,1},{4,6},{5,7},{6,4},{7,5},{8,10},{9,11},{10,... | collective-permute-start | bytes 522248 | tf_op jit(solution)/shard_map/ppermute | solution.py:243
  109.8 18.9 %collective-permute-start.15 = (bf16[40,2176]{1,0:T(8,128)(2,1)}, bf16[40,2176]{1,0:T(8,128)(2,1)}, u32[]{:S(2)}, u32[]{:S(2)}) collective-permute-start(bf16[40,2176]{1,0:T(8,128)(2,1)} %get-tuple-element.77), channel_id=1, source_target_pairs={{0,3},{1,2},{2,1},{3,0},{4,7},{5,6},{6,5},{7,4},{8,11},{9,10},{10,... | collective-permute-start | bytes 522248 | tf_op jit(solution)/shard_map/ppermute | solution.py:243
  110.7 18.1 %collective-permute-start.24 = (bf16[40,2176]{1,0:T(8,128)(2,1)}, bf16[40,2176]{1,0:T(8,128)(2,1)}, u32[]{:S(2)}, u32[]{:S(2)}) collective-permute-start(bf16[40,2176]{1,0:T(8,128)(2,1)} %get-tuple-element.84), channel_id=1, source_target_pairs={{0,1},{1,0},{2,3},{3,2},{4,5},{5,4},{6,7},{7,6},{8,9},{9,8},{10,11... | collective-permute-start | bytes 522248 | tf_op jit(solution)/shard_map/ppermute | solution.py:243
  111.5 18.8 %collective-permute-start.25 = (bf16[40,2176]{1,0:T(8,128)(2,1)}, bf16[40,2176]{1,0:T(8,128)(2,1)}, u32[]{:S(2)}, u32[]{:S(2)}) collective-permute-start(bf16[40,2176]{1,0:T(8,128)(2,1)} %get-tuple-element.85), channel_id=1, source_target_pairs={{0,2},{1,3},{2,0},{3,1},{4,6},{5,7},{6,4},{7,5},{8,10},{9,11},{10,... | collective-permute-start | bytes 522248 | tf_op jit(solution)/shard_map/ppermute | solution.py:243
  128.8 28.6 %collective-permute-start = (bf16[40,4224]{1,0:T(8,128)(2,1)S(1)}, bf16[40,4224]{1,0:T(8,128)(2,1)S(1)}, u32[]{:S(2)}, u32[]{:S(2)}) collective-permute-start(bf16[40,4224]{1,0:T(8,128)(2,1)S(1)} %get-tuple-element.62), channel_id=1, source_target_pairs={{0,1},{1,0},{2,3},{3,2},{4,5},{5,4},{6,7},{7,6},{8,9},{9,8},{10,11... | collective-permute-start | bytes 1013768 | tf_op jit(solution)/shard_map/ppermute | solution.py:243
  128.8 32.3 %collective-permute-start.1 = (bf16[40,4224]{1,0:T(8,128)(2,1)S(1)}, bf16[40,4224]{1,0:T(8,128)(2,1)S(1)}, u32[]{:S(2)}, u32[]{:S(2)}) collective-permute-start(bf16[40,4224]{1,0:T(8,128)(2,1)S(1)} %get-tuple-element.63), channel_id=1, source_target_pairs={{0,2},{1,3},{2,0},{3,1},{4,6},{5,7},{6,4},{7,5},{8,10},{9,11},{10,... | collective-permute-start | bytes 1013768 | tf_op jit(solution)/shard_map/ppermute | solution.py:243
  130.3 30.8 %collective-permute-start.2 = (bf16[40,4224]{1,0:T(8,128)(2,1)S(1)}, bf16[40,4224]{1,0:T(8,128)(2,1)S(1)}, u32[]{:S(2)}, u32[]{:S(2)}) collective-permute-start(bf16[40,4224]{1,0:T(8,128)(2,1)S(1)} %get-tuple-element.64), channel_id=1, source_target_pairs={{0,3},{1,2},{2,1},{3,0},{4,7},{5,6},{6,5},{7,4},{8,11},{9,10},{10,... | collective-permute-start | bytes 1013768 | tf_op jit(solution)/shard_map/ppermute | solution.py:243
  130.7 19.9 %collective-permute-start.36 = (bf16[40,2176]{1,0:T(8,128)(2,1)}, bf16[40,2176]{1,0:T(8,128)(2,1)S(1)}, u32[]{:S(2)}, u32[]{:S(2)}) collective-permute-start(bf16[40,2176]{1,0:T(8,128)(2,1)} %copy-done.71), channel_id=1, source_target_pairs={{0,2},{1,3},{2,0},{3,1},{4,6},{5,7},{6,4},{7,5},{8,10},{9,11},{10,... | collective-permute-start | bytes 522248 | tf_op jit(solution)/shard_map/ppermute | solution.py:243
  131.8 21.8 %collective-permute-start.37 = (bf16[40,2176]{1,0:T(8,128)(2,1)}, bf16[40,2176]{1,0:T(8,128)(2,1)S(1)}, u32[]{:S(2)}, u32[]{:S(2)}) collective-permute-start(bf16[40,2176]{1,0:T(8,128)(2,1)} %copy-done.70), channel_id=1, source_target_pairs={{0,3},{1,2},{2,1},{3,0},{4,7},{5,6},{6,5},{7,4},{8,11},{9,10},{10,... | collective-permute-start | bytes 522248 | tf_op jit(solution)/shard_map/ppermute | solution.py:243
  150.6 33.9 %collective-permute-start.16 = (bf16[128,2176]{1,0:T(8,128)(2,1)S(1)}, bf16[128,2176]{1,0:T(8,128)(2,1)S(1)}, u32[]{:S(2)}, u32[]{:S(2)}) collective-permute-start(bf16[128,2176]{1,0:T(8,128)(2,1)S(1)} %combine.5), channel_id=1, source_target_pairs={{0,4},{1,5},{2,6},{3,7},{4,0},{5,1},{6,2},{7,3},{8,12},{9,13},{10,... | collective-permute-start | bytes 1671176 | tf_op jit(solution)/shard_map/ppermute | solution.py:243
  153.5 37.5 %collective-permute-start.27 = (bf16[128,2176]{1,0:T(8,128)(2,1)S(1)}, bf16[128,2176]{1,0:T(8,128)(2,1)S(1)}, u32[]{:S(2)}, u32[]{:S(2)}) collective-permute-start(bf16[128,2176]{1,0:T(8,128)(2,1)S(1)} %combine.6), channel_id=1, source_target_pairs={{0,8},{1,9},{2,10},{3,11},{4,12},{5,13},{6,14},{7,15},{8,0},{9,1},... | collective-permute-start | bytes 1671176 | tf_op jit(solution)/shard_map/ppermute | solution.py:243
  157.4 49.1 %collective-permute-start.38 = (bf16[128,2176]{1,0:T(8,128)(2,1)S(1)}, bf16[128,2176]{1,0:T(8,128)(2,1)S(1)}, u32[]{:S(2)}, u32[]{:S(2)}) collective-permute-start(bf16[128,2176]{1,0:T(8,128)(2,1)S(1)} %combine.7), channel_id=1, source_target_pairs={{0,12},{1,13},{2,14},{3,15},{4,8},{5,9},{6,10},{7,11},{8,4},{9,5},... | collective-permute-start | bytes 1671176 | tf_op jit(solution)/shard_map/ppermute | solution.py:243
  (79 other events, 814.1 us)

commit v2 on v1

v2 whole, which is shorter than its diff:
```python
import functools

import jax
import jax.numpy as jnp
from jax import lax
from jax.experimental import pallas as pl
from jax.experimental.pallas import tpu as pltpu
from jax.sharding import PartitionSpec as P

SCALE = 2.0
PLANE = 4
LANES = 128
F32 = jnp.float32
BF16 = jnp.bfloat16
MIB = 1024 * 1024
RATE = 3000000


def nn(a, b):
    return lax.dot_general(a, b, (((1,), (0,)), ((), ())), preferred_element_type=F32)


def nt(a, b):
    return lax.dot_general(a, b, (((1,), (1,)), ((), ())), preferred_element_type=F32)


def two_parts(value):
    high = value.astype(BF16).astype(F32)
    return high, value - high


def smem():
    return pl.BlockSpec(memory_space=pltpu.SMEM)


def one_hots(names, slots, side, routes):
    turned = side.T
    tokens = side.shape[0]
    earlier = lax.broadcasted_iota(jnp.int32, (tokens, tokens), 0)
    later = lax.broadcasted_iota(jnp.int32, (tokens, tokens), 1)
    ahead = jnp.where(earlier < later, 1.0, 0.0).astype(BF16)
    place = lax.broadcasted_iota(jnp.int32, (slots, tokens), 0).astype(F32)
    found = []
    for name in names:
        hits = [jnp.where(turned[k : k + 1, :] == name, 1.0, 0.0) for k in range(routes)]
        member = sum(hits)
        wide = jnp.broadcast_to(member, (8, tokens)).astype(BF16)
        slot = nn(wide, ahead)[0:1, :]
        found.append((jnp.where((place == slot) & (member > 0.0), 1.0, 0.0), hits))
    return turned, found


def pack_kernel(routes, x_ref, grad_ref, ids_ref, weight_ref, out_ref):
    tokens, width = grad_ref.shape
    out_ref[:, :width] = x_ref[...]
    out_ref[:, width : 2 * width] = grad_ref[...]
    names = ids_ref[...].astype(F32) + 1.0
    high, low = two_parts(weight_ref[...])
    row = lax.broadcasted_iota(jnp.int32, (LANES, tokens), 0)
    side = jnp.zeros((LANES, tokens), F32)
    for group, values in enumerate((names, names, high, low)):
        for k in range(routes):
            side = jnp.where(row == group * routes + k, values[k : k + 1, :], side)
    out_ref[:, 2 * width :] = side.T.astype(BF16)


def select_kernel(routes, slots, choices, stage, info_ref, *refs):
    blocks, outs, side_ref = refs[:choices], refs[choices:-1], refs[-1]
    block = blocks[0]
    for i in range(1, choices):

        @pl.when(info_ref[PLANE + stage] == i)
        def _():
            block[...] = blocks[i][...]

    width = (block.shape[1] - LANES) // 2
    side_ref[...] = block[:, 2 * width :]
    side = block[:, 2 * width :].astype(F32)
    names = [info_ref[m].astype(F32) + 1.0 for m in range(PLANE)]
    turned, found = one_hots(names, slots, side, routes)
    lane = lax.broadcasted_iota(jnp.int32, (slots, LANES), 1)
    picks = jnp.concatenate([hot for hot, _ in found], axis=0).astype(BF16)
    chosen = nn(picks, block[:, : 2 * width])
    tails = []
    for hot, hits in found:
        parts = []
        for group in (2, 3):
            weight = sum(hits[k] * turned[group * routes + k : group * routes + k + 1, :] for k in range(routes))
            parts.append(jnp.sum(hot * weight, axis=1, keepdims=True))
        tails.append(jnp.where(lane == 0, parts[0], jnp.where(lane == 1, parts[1], 0.0)))
    for out, low, high in ((outs[0], 0, 1), (outs[1], 1, 2), (outs[2], 2, 4)):
        out[:, : 2 * width] = chosen[low * slots : high * slots].astype(BF16)
        out[:, 2 * width :] = jnp.concatenate(tails[low:high], axis=0).astype(BF16)


def stacked(refs, low, high):
    own, near, across, around = (r[:, low:high].astype(F32) for r in refs)
    half = own.shape[0]
    return jnp.concatenate([own, near, across[:half], around[half:]], axis=0)


def prepare_kernel(gate_a, gate_b, up_a, up_b, down_a, down_b, *refs):
    def padded(*parts):
        rows, columns = sum(p.shape[0] for p in parts), parts[0].shape[1]
        return jnp.concatenate([*(p.astype(F32) for p in parts), jnp.zeros((LANES - rows, columns), F32)], axis=0)

    in_t, in_s, back_t, out_s, down_t, down_s, last_t = refs
    rank = gate_a.shape[0]
    both = padded(gate_a[...], up_a[...])
    in_t[...] = both.T.astype(BF16)
    in_s[...] = both.astype(BF16)
    gate = padded(gate_b[...])
    up = padded(jnp.zeros((rank, up_b.shape[1]), F32), up_b[...])
    out_s[0] = gate.astype(BF16)
    out_s[1] = up.astype(BF16)
    back_t[0] = gate.T.astype(BF16)
    back_t[1] = up.T.astype(BF16)
    down = padded(down_a[...])
    down_s[...] = down.astype(BF16)
    down_t[...] = down.T.astype(BF16)
    last_t[...] = padded(down_b[...]).T.astype(BF16)


def expert_kernel(routes, slots, *refs):
    rows_in = refs[:PLANE]
    in_t, in_s, back_t, out_s, down_t, down_s, last_t, gate_w, up_w, down_w = refs[PLANE : PLANE + 10]
    *outs, acts_ref, lows_ref = refs[PLANE + 10 :]
    width, hidden_units = gate_w.shape
    x = stacked(rows_in, 0, width).astype(BF16)
    g = stacked(rows_in, width, 2 * width).astype(BF16)
    side = stacked(rows_in, 2 * width, 2 * width + LANES)
    weight = side[:, 0:1] + side[:, 1:2]

    low = nn(x, in_t[...]).astype(BF16)
    g_low = nn(g, last_t[...])
    down_back = (weight * g_low).astype(BF16)
    gate_pre = nn(x, gate_w[...]) + SCALE * nn(low, out_s[0])
    up_pre = nn(x, up_w[...]) + SCALE * nn(low, out_s[1])
    q = jax.nn.sigmoid(gate_pre)
    silu = gate_pre * q
    hidden = (silu * up_pre).astype(BF16)
    low_down = nn(hidden, down_t[...]).astype(BF16).astype(F32)
    g_hidden = nt(g, down_w[...])
    dots = jnp.sum(hidden.astype(F32) * g_hidden, axis=1, keepdims=True)
    dots = dots + SCALE * jnp.sum(low_down * g_low, axis=1, keepdims=True)
    grad_hidden = weight * g_hidden + SCALE * nn(down_back, down_s[...])
    gate_grad = (grad_hidden * up_pre * q * (1.0 + gate_pre * (1.0 - q))).astype(BF16)
    up_grad = (grad_hidden * silu).astype(BF16)
    back = (nn(gate_grad, back_t[0]) + nn(up_grad, back_t[1])).astype(BF16)
    input_grad = nt(gate_grad, gate_w[...]) + nt(up_grad, up_w[...]) + SCALE * nn(back, in_s[...])
    high, lesser = two_parts(dots)
    lane = lax.broadcasted_iota(jnp.int32, (PLANE * slots, LANES), 1)
    side_back = jnp.where(lane < routes, high, jnp.where(lane < 2 * routes, lesser, 0.0))
    for out, first, end in ((outs[0], 0, 1), (outs[1], 1, 2), (outs[2], 2, 4)):
        out[:, :width] = input_grad[first * slots : end * slots].astype(BF16)
        out[:, width:] = side_back[first * slots : end * slots].astype(BF16)
    acts_ref[:, :hidden_units] = hidden
    acts_ref[:, hidden_units : 2 * hidden_units] = gate_grad
    acts_ref[:, 2 * hidden_units :] = up_grad
    for n, value in enumerate((back, low, down_back, (weight * low_down).astype(BF16))):
        lows_ref[:, n * LANES : (n + 1) * LANES] = value


def combine_kernel(routes, slots, info_ref, side_ref, *refs):
    backs, out_ref = refs[:PLANE], refs[PLANE]
    width = out_ref.shape[1] - LANES
    side = side_ref[...].astype(F32)
    names = [info_ref[m].astype(F32) + 1.0 for m in range(PLANE)]
    _, found = one_hots(names, slots, side, routes)
    tails = stacked(backs, width, width + LANES).astype(BF16)
    extra = jnp.zeros((side.shape[0], LANES), F32)
    for m in range(PLANE):
        hot = jnp.concatenate([h if n == m else jnp.zeros_like(h) for n, (h, _) in enumerate(found)], axis=0)
        spread = lax.dot_general(hot.astype(BF16), tails, (((0,), (0,)), ((), ())), preferred_element_type=F32)
        extra = extra + jnp.where(side == names[m], spread, 0.0)
    out_ref[:, width:] = extra.astype(BF16)
    picks = jnp.concatenate([hot for hot, _ in found], axis=0).astype(BF16)
    rows = stacked(backs, 0, width).astype(BF16)
    out_ref[:, :width] = lax.dot_general(
        picks, rows, (((0,), (0,)), ((), ())), preferred_element_type=F32
    ).astype(BF16)


def add_kernel(*refs):
    refs[-1][...] = sum(r[...].astype(F32) for r in refs[:-1])


def finish_kernel(routes, *refs):
    parts, (tokens_ref, combine_ref) = refs[:-2], refs[-2:]
    width = tokens_ref.shape[1]
    tokens_ref[...] = sum(r[:, :width].astype(F32) for r in parts).astype(BF16)
    side = sum(r[:, width:].astype(F32) for r in parts).T
    combine_ref[...] = side[:routes] + side[routes : 2 * routes]


def adapter_kernel(stages, rank, *refs):
    rows_in, refs = refs[: stages * PLANE], refs[stages * PLANE :]
    acts, lows, outs = refs[:stages], refs[stages : 2 * stages], refs[2 * stages :]
    width, hidden_units = outs[0].shape[2], outs[1].shape[2]

    def over_rows(part, other):
        return SCALE * lax.dot_general(part, other, (((0,), (0,)), ((), ())), preferred_element_type=F32)

    def every(low, high):
        pieces = [stacked(rows_in[n * PLANE : (n + 1) * PLANE], low, high) for n in range(stages)]
        return jnp.concatenate(pieces, axis=0).astype(BF16)

    parts = [jnp.concatenate([r[:, n * LANES : (n + 1) * LANES] for r in lows], axis=0) for n in range(4)]
    act = [jnp.concatenate([r[:, n * hidden_units : (n + 1) * hidden_units] for r in acts], axis=0) for n in range(3)]
    by_x = over_rows(parts[0], every(0, width))
    outs[0][0] = by_x[:rank]
    outs[2][0] = by_x[rank : 2 * rank]
    outs[1][0] = over_rows(parts[1], act[1])[:rank]
    outs[3][0] = over_rows(parts[1], act[2])[rank : 2 * rank]
    outs[4][0] = over_rows(parts[2], act[0])[:rank]
    outs[5][0] = over_rows(parts[3], every(width, 2 * width))[:rank]


def on_device(tokens, grad_out, expert_ids, combine, *weights):
    rows, width = tokens.shape
    routes = expert_ids.shape[1]
    experts = lax.axis_size("expert")
    planes = experts // PLANE
    capacity = rows * routes * 9 // (8 * experts)
    slots = -(-capacity // 8) * 8
    matrices = [w[0] for w in weights]
    hidden_units = matrices[0].shape[1]
    rank = matrices[3].shape[0]
    wide = width + LANES
    shape = jax.ShapeDtypeStruct

    me = lax.axis_index("expert").astype(jnp.int32)
    here, seat = me // PLANE, me % PLANE
    if planes == 4:
        end = ((here == 0) | (here == 3)).astype(jnp.int32)
        choice = [0 * end, 0 * end, end, end]
    else:
        offsets = [sorted({(p ^ n) - p for p in range(planes)}, key=lambda o: (abs(o), o)) for n in range(planes)]
        choice = [sum(jnp.where((here ^ n) - here == o, i, 0) for i, o in enumerate(offsets[n])) for n in range(planes)]
    info = jnp.stack([here * PLANE + (seat ^ m) for m in range(PLANE)] + choice).astype(jnp.int32)

    def along(value, step):
        pairs = [
            (p * PLANE + s, (p + step) * PLANE + s) for p in range(planes) for s in range(PLANE) if 0 <= p + step < planes
        ]
        return lax.ppermute(value, "expert", pairs)

    def flipped(value, mask, sources=range(planes)):
        pairs = [(p * PLANE + n, (p * PLANE + n) ^ mask) for p in sources for n in range(PLANE)]
        return lax.ppermute(value, "expert", pairs)

    def kernel(body, outs, args, micros, name, mib, scalars=0):
        vmem = pl.BlockSpec(memory_space=pltpu.VMEM)

        def run(*refs):
            refs[len(args) + len(last) + len(outs)][...] = jnp.zeros((8, LANES), F32)
            body(*refs[: len(args)], *refs[len(args) + len(last) : -1])

        *result, mark = pl.pallas_call(
            run,
            out_shape=[*outs, shape((8, LANES), F32)],
            in_specs=[smem()] * scalars + [vmem] * (len(args) - scalars + len(last)),
            out_specs=[vmem] * (len(outs) + 1),
            compiler_params=pltpu.CompilerParams(vmem_limit_bytes=mib * MIB),
            cost_estimate=pl.CostEstimate(flops=1, bytes_accessed=micros * RATE, transcendentals=0),
            name=name,
        )(*args, *last)
        last[:] = [mark]
        return result

    last = []
    (packed,) = kernel(
        functools.partial(pack_kernel, routes),
        [shape((rows, 2 * width + LANES), BF16)],
        (tokens, grad_out, expert_ids.T, combine.T),
        2,
        "pack",
        6,
    )

    def expert(got):
        return kernel(
            functools.partial(expert_kernel, routes, slots),
            [shape((n * slots, wide), BF16) for n in (1, 1, 2)]
            + [shape((PLANE * slots, 3 * hidden_units), BF16), shape((PLANE * slots, 4 * LANES), BF16)],
            (*got, *adapters, *matrices[:3]),
            8,
            "expert",
            20,
        )

    def together(*values):
        *values, last[0] = lax.optimization_barrier((*values, last[0]))
        return values

    rows_of, sides, parts, acts, lows = {}, {}, {}, {}, {}

    def halfway(own, near, far, sources):
        return own, flipped(near, 1), flipped(far, 2, sources)

    def arrived(own, near, across):
        (across,) = together(across)
        return own, near, across, flipped(across, 1)

    def begin(stage, *found, sources=range(planes)):
        *picked, sides[stage] = kernel(
            functools.partial(select_kernel, routes, slots, len(found), stage),
            [shape((n * slots, 2 * width + LANES), BF16) for n in (1, 1, 2)] + [shape((rows, LANES), BF16)],
            (info, *found),
            4,
            "select",
            12,
            scalars=1,
        )
        rows_of[stage] = halfway(*picked, sources)

    def middle_of(stage, sources=range(planes)):
        rows_of[stage] = arrived(*rows_of[stage])
        *backs, acts[stage], lows[stage] = expert(rows_of[stage])
        parts[stage] = halfway(*backs, sources)

    def end_of(stage, toward, sources=range(planes)):
        (part,) = kernel(
            functools.partial(combine_kernel, routes, slots),
            [shape((rows, wide), BF16)],
            (info, sides[stage], *arrived(*parts[stage])),
            3,
            "combine",
            8,
            scalars=1,
        )
        parts[stage] = flipped(part, toward * PLANE, sources) if toward else part

    def add(*values):
        return kernel(add_kernel, [shape((rows, wide), F32)], values, 1, "add", 8)[0]

    adapters = []

    def prepare():
        adapters[:] = kernel(
            prepare_kernel,
            [
                shape((width, LANES), BF16),
                shape((LANES, width), BF16),
                shape((2, hidden_units, LANES), BF16),
                shape((2, LANES, hidden_units), BF16),
                shape((hidden_units, LANES), BF16),
                shape((LANES, hidden_units), BF16),
                shape((width, LANES), BF16),
            ],
            tuple(matrices[3:]),
            4,
            "prepare",
            8,
        )

    if planes == 4:
        mids = (1, 2)
        mate, across = flipped(packed, PLANE), flipped(packed, 3 * PLANE, mids)
        begin(0, packed)
        prepare()
        mate, across = together(mate, across)
        mate_across, far = flipped(mate, 3 * PLANE, mids), flipped(across, PLANE)
        begin(1, mate)
        middle_of(0)
        mate_across, far, *rows_of[1] = together(mate_across, far, *rows_of[1])
        farthest = flipped(mate_across, PLANE)
        begin(2, mate_across, far)
        middle_of(1)
        middle_of(2)
        (farthest,) = together(farthest)
        begin(3, across, farthest)
        end_of(2, 2)
        middle_of(3)
        end_of(1, 1)
        (parts[2],) = together(parts[2])
        end_of(3, 3)
        end_of(0, 0)
    else:
        blocks = {0: packed}
        for step in range(1, planes):
            for sign in (1, -1):
                blocks[sign * step] = along(blocks[sign * (step - 1)], -sign)
        prepare()
        for stage in range(planes):
            begin(stage, *(blocks[o] for o in offsets[stage]))
            middle_of(stage)
            end_of(stage, stage)
    order = sorted(rows_of)
    total = add(*(parts[n] for n in order[:-1]))

    grads = kernel(
        functools.partial(adapter_kernel, len(order), rank),
        [shape((1, rank, n), F32) for n in (width, hidden_units, width, hidden_units, hidden_units, width)],
        (*(r for n in order for r in rows_of[n]), *(acts[n] for n in order), *(lows[n] for n in order)),
        5,
        "adapter_grads",
        24,
    )
    grad_tokens, grad_combine = kernel(
        functools.partial(finish_kernel, routes),
        [shape((rows, width), BF16), shape((routes, rows), F32)],
        (total, parts[order[-1]]),
        3,
        "finish",
        8,
    )
    return (grad_tokens, grad_combine.T, *grads)


def solution(mesh):
    by_token = P(("groups", "expert"), None)
    by_part = P(("groups", "expert"), None, None)
    return jax.shard_map(
        on_device,
        mesh=mesh,
        in_specs=(by_token,) * 4 + (P("expert", None, None),) * 9,
        out_specs=(by_token,) * 2 + (by_part,) * 6,
        check_vma=False,
    )
```

time: 210 us -> 174 us (0.83)
  starting transfers between devices: 61.5 us -> 25.3 us
  waiting for transfers between devices: 61.7 us -> 94.9 us
  local copies, waits for them, and re-layouts: 36 us -> 12.4 us
  Pallas kernels: 47.9 us -> 38.6 us
    ppermute x39 -> x32, starting transfers between devices: 61.5 us -> 25.3 us  [flipped(): return lax.ppermute(value, 'expert', pairs)]
    ppermute x39 -> x32, waiting for transfers between devices: 61.7 us -> 94.9 us  [flipped(): return lax.ppermute(value, 'expert', pairs)]
    unnamed x147 -> x26, local copies, waits for them, and re-layouts: 35.6 us -> 12.3 us
    pallas_call x15 -> x17, Pallas kernels: 47.9 us -> 38.6 us  [kernel(): pl.pallas_call(run, out_shape=[*outs, shape((8, LANES), F32)], in_specs=[...]
  transfers between devices with their start and end apart: 39 -> 32, of which waited for: 14 -> 21; matrix products, arithmetic and copies ran while one was open for 1% -> 0% of each run, Pallas kernels for 22% -> 20%
where the time goes in v2:
time: 174 us; the launch traced here: 172 us
  waiting for transfers between devices  94.9 us (55%)
  Pallas kernels  38.6 us (22%)
  starting transfers between devices  25.3 us (15%)
  local copies, waits for them, and re-layouts  12.4 us (7%)
    ppermute x32, waiting for transfers between devices, flipped(): return lax.ppermute(value, 'expert', pairs)  94.9 us
    pallas_call x17, Pallas kernels, kernel(): pl.pallas_call(run, out_shape=[*outs, shape((8, LANES), F32)], in_specs=[...  38.6 us
    ppermute x32, starting transfers between devices, flipped(): return lax.ppermute(value, 'expert', pairs)  25.3 us
    unnamed x26, local copies, waits for them, and re-layouts  12.3 us
  transfers between devices with their start and end apart: 32, of which 21 were waited for; matrix products, arithmetic and copies ran while one was open for 0% of the time, Pallas kernels for 20%

profile of v2, /device:TPU:16, one launch (start us, length us, event | category | flops | bytes accessed | tf_op | source)
XLA Modules:
  0.0 172.0 jit_solution(12671702068259174073)
XLA Ops:
  5.2 2.5 %collective-permute-start.3 = (bf16[128,4224]{1,0:T(8,128)(2,1)}, bf16[128,4224]{1,0:T(8,128)(2,1)}, u32[]{:S(2)}, u32[]{:S(2)}) collective-permute-start(bf16[128,4224]{1,0:T(8,128)(2,1)} %get-tuple-element.110.refs_1_), channel_id=1, source_target_pairs={{4,8},{5,9},{6,10},{7,11},{8,4},{9,5},{10,6},{11,7},{20,24},{21,25... | collective-permute-start | bytes 3244040 | tf_op jit(solution)/shard_map/ppermute | solution.py:250
  8.7 1.9 %select.10 = (bf16[40,4224]{1,0:T(8,128)(2,1)S(1)}, bf16[40,4224]{1,0:T(8,128)(2,1)S(1)}, bf16[80,4224]{1,0:T(8,128)(2,1)S(1)}, bf16[128,128]{1,0:T(8,128)(2,1)S(1)}, f32[8,128]{1,0:T(8,128)S(1)}) custom-call(s32[8]{0:T(128)S(1)} %stack.28.refs_0_, bf16[128,4224]{1,0:T(8,128)(2,1)} %get-tuple-element.110.refs_1_, f32[8,128]{1,0:T(8,128)S(1)} %get-tuple-element.111.refs_2_), custom_call_target="tpu_custom_call" | custom-call | flops 1 | bytes 12000000 | tf_op jit(solution)/shard_map/select/pallas_call | solution.py:259
  10.6 1.6 collective-permute-start.1
  17.8 15.3 %collective-permute-done.3.refs_1_ = bf16[128,4224]{1,0:T(8,128)(2,1)} collective-permute-done((bf16[128,4224]{1,0:T(8,128)(2,1)}, bf16[128,4224]{1,0:T(8,128)(2,1)}, u32[]{:S(2)}, u32[]{:S(2)}) %collective-permute-start.3) | collective-permute-done | bytes 1081376 | tf_op jit(solution)/shard_map/ppermute | solution.py:250
  33.4 3.5 %collective-permute-start.7 = (bf16[128,4224]{1,0:T(8,128)(2,1)}, bf16[128,4224]{1,0:T(8,128)(2,1)S(1)}, u32[]{:S(2)}, u32[]{:S(2)}) collective-permute-start(bf16[128,4224]{1,0:T(8,128)(2,1)} %collective-permute-done.2.refs_1_), channel_id=1, source_target_pairs={{4,8},{5,9},{6,10},{7,11},{8,4},{9,5},{10,6},{11,7},{20,24},{21,25... | collective-permute-start | bytes 3244040 | tf_op jit(solution)/shard_map/ppermute | solution.py:250
  36.9 1.9 %select.11 = (bf16[40,4224]{1,0:T(8,128)(2,1)S(1)}, bf16[40,4224]{1,0:T(8,128)(2,1)S(1)}, bf16[80,4224]{1,0:T(8,128)(2,1)S(1)}, bf16[128,128]{1,0:T(8,128)(2,1)S(1)}, f32[8,128]{1,0:T(8,128)S(1)}) custom-call(s32[8]{0:T(128)S(1)} %stack.28.refs_0_, bf16[128,4224]{1,0:T(8,128)(2,1)} %collective-permute-done.2.refs_1_, f32[8,128]{1,0:T(8,128)S(1)} %get-tuple-element.119.refs_2_), custom_call_target="tpu_custom_call" | custom-call | flops 1 | bytes 12000000 | tf_op jit(solution)/shard_map/select/pallas_call | solution.py:259
  39.5 1.5 collective-permute-start.10
  41.7 1.9 %copy-done.1 = bf16[1,2048,768]{2,1,0:T(8,128)(2,1)S(1)} copy-done((bf16[1,2048,768]{2,1,0:T(8,128)(2,1)S(1)}, bf16[1,2048,768]{2,1,0:T(8,128)(2,1)}, u32[]{:S(2)}) %copy-start.1) | copy-done | bytes 3145752
  43.6 1.9 %copy-done.2 = bf16[1,768,2048]{2,1,0:T(8,128)(2,1)S(1)} copy-done((bf16[1,768,2048]{2,1,0:T(8,128)(2,1)S(1)}, bf16[1,768,2048]{2,1,0:T(8,128)(2,1)}, u32[]{:S(2)}) %copy-start.2) | copy-done | bytes 3145752
  45.5 5.4 %expert.4 = (bf16[40,2176]{1,0:T(8,128)(2,1)S(1)}, bf16[40,2176]{1,0:T(8,128)(2,1)S(1)}, bf16[80,2176]{1,0:T(8,128)(2,1)S(1)}, bf16[160,2304]{1,0:T(8,128)(2,1)S...) custom-call(bf16[40,4224]{1,0:T(8,128)(2,1)S(1)} %get-tuple-element.113.refs_0_, ...), custom_call_target="tpu_custom_call" | custom-call | flops 1 | bytes 24000000 | tf_op jit(solution)/shard_map/expert/pallas_call | solution.py:259
  50.9 5.7 %collective-permute-done.10.refs_2_.refs_6_ = bf16[80,4224]{1,0:T(8,128)(2,1)S(1)} collective-permute-done((bf16[80,4224]{1,0:T(8,128)(2,1)S(1)}, bf16[80,4224]{1,0:T(8,128)(2,1)S(1)}, u32[]{:S(2)}, u32[]{:S(2)}) %collective-permute-start.10) | collective-permute-done | bytes 675872 | tf_op jit(solution)/shard_map/ppermute | solution.py:250
  56.6 3.3 %collective-permute-done.7.refs_1_ = bf16[128,4224]{1,0:T(8,128)(2,1)S(1)} collective-permute-done((bf16[128,4224]{1,0:T(8,128)(2,1)}, bf16[128,4224]{1,0:T(8,128)(2,1)S(1)}, u32[]{:S(2)}, u32[]{:S(2)}) %collective-permute-start.7) | collective-permute-done | bytes 1081376 | tf_op jit(solution)/shard_map/ppermute | solution.py:250
  61.3 1.4 select.12
  62.8 1.6 collective-permute-start.13
  64.9 5.4 %expert.5 = (bf16[40,2176]{1,0:T(8,128)(2,1)S(1)}, bf16[40,2176]{1,0:T(8,128)(2,1)S(1)}, bf16[80,2176]{1,0:T(8,128)(2,1)S(1)}, bf16[160,2304]{1,0:T(8,128)(2,1)S...) custom-call(bf16[40,4224]{1,0:T(8,128)(2,1)S(1)} %get-tuple-element.144.refs_0_.refs_4_, ...), custom_call_target="tpu_custom_call" | custom-call | flops 1 | bytes 24000000 | tf_op jit(solution)/shard_map/expert/pallas_call | solution.py:259
  70.2 10.1 %collective-permute-done.13.refs_2_.refs_10_ = bf16[80,4224]{1,0:T(8,128)(2,1)S(1)} collective-permute-done((bf16[80,4224]{1,0:T(8,128)(2,1)S(1)}, bf16[80,4224]{1,0:T(8,128)(2,1)S(1)}, u32[]{:S(2)}, u32[]{:S(2)}) %collective-permute-start.13) | collective-permute-done | bytes 675872 | tf_op jit(solution)/shard_map/ppermute | solution.py:250
  80.9 2.1 %collective-permute-done.12.refs_1_.refs_9_ = bf16[40,4224]{1,0:T(8,128)(2,1)S(1)} collective-permute-done((bf16[40,4224]{1,0:T(8,128)(2,1)S(1)}, bf16[40,4224]{1,0:T(8,128)(2,1)S(1)}, u32[]{:S(2)}, u32[]{:S(2)}) %collective-permute-start.12) | collective-permute-done | bytes 337952 | tf_op jit(solution)/shard_map/ppermute | solution.py:250
  83.0 5.4 %expert.6 = (bf16[40,2176]{1,0:T(8,128)(2,1)S(1)}, bf16[40,2176]{1,0:T(8,128)(2,1)S(1)}, bf16[80,2176]{1,0:T(8,128)(2,1)S(1)}, bf16[160,2304]{1,0:T(8,128)(2,1)S...) custom-call(bf16[40,4224]{1,0:T(8,128)(2,1)S(1)} %get-tuple-element.141.refs_0_.refs_8_, ...), custom_call_target="tpu_custom_call" | custom-call | flops 1 | bytes 24000000 | tf_op jit(solution)/shard_map/expert/pallas_call | solution.py:259
  88.4 1.6 collective-permute-start.19
  90.3 2.1 %select.13 = (bf16[40,4224]{1,0:T(8,128)(2,1)S(1)}, bf16[40,4224]{1,0:T(8,128)(2,1)S(1)}, bf16[80,4224]{1,0:T(8,128)(2,1)S(1)}, bf16[128,128]{1,0:T(8,128)(2,1)S(1)}, f32[8,128]{1,0:T(8,128)S(1)}) custom-call(s32[8]{0:T(128)S(1)} %stack.28.refs_0_, bf16[128,4224]{1,0:T(8,128)(2,1)} %collective-permute-done.3.refs_1_, ...), custom_call_target="tpu_custom_call" | custom-call | flops 1 | bytes 12000000 | tf_op jit(solution)/shard_map/select/pallas_call | solution.py:259
  93.0 6.4 %collective-permute-done.19.refs_4_ = bf16[80,2176]{1,0:T(8,128)(2,1)S(1)} collective-permute-done((bf16[80,2176]{1,0:T(8,128)(2,1)S(1)}, bf16[80,2176]{1,0:T(8,128)(2,1)S(1)}, u32[]{:S(2)}, u32[]{:S(2)}) %collective-permute-start.19) | collective-permute-done | bytes 348192 | tf_op jit(solution)/shard_map/ppermute | solution.py:250
  102.5 10.6 %collective-permute-done.17.refs_2_.refs_14_ = bf16[80,4224]{1,0:T(8,128)(2,1)S(1)} collective-permute-done((bf16[80,4224]{1,0:T(8,128)(2,1)S(1)}, bf16[80,4224]{1,0:T(8,128)(2,1)S(1)}, u32[]{:S(2)}, u32[]{:S(2)}) %collective-permute-start.17) | collective-permute-done | bytes 675872 | tf_op jit(solution)/shard_map/ppermute | solution.py:250
  113.1 1.5 collective-permute-start.26
  116.3 5.4 %expert.7 = (bf16[40,2176]{1,0:T(8,128)(2,1)S(1)}, bf16[40,2176]{1,0:T(8,128)(2,1)S(1)}, bf16[80,2176]{1,0:T(8,128)(2,1)S(1)}, bf16[160,2304]{1,0:T(8,128)(2,1)S...) custom-call(bf16[40,4224]{1,0:T(8,128)(2,1)S(1)} %get-tuple-element.157.refs_0_.refs_12_, ...), custom_call_target="tpu_custom_call" | custom-call | flops 1 | bytes 24000000 | tf_op jit(solution)/shard_map/expert/pallas_call | solution.py:259
  121.6 2.0 %collective-permute-done.26.refs_4_ = bf16[80,2176]{1,0:T(8,128)(2,1)S(1)} collective-permute-done((bf16[80,2176]{1,0:T(8,128)(2,1)S(1)}, bf16[80,2176]{1,0:T(8,128)(2,1)S(1)}, u32[]{:S(2)}, u32[]{:S(2)}) %collective-permute-start.26) | collective-permute-done | bytes 348192 | tf_op jit(solution)/shard_map/ppermute | solution.py:250
  123.7 1.5 collective-permute-start.23
  127.7 11.7 %collective-permute-done.24.refs_2_ = bf16[128,2176]{1,0:T(8,128)(2,1)S(1)} collective-permute-done((bf16[128,2176]{1,0:T(8,128)(2,1)S(1)}, bf16[128,2176]{1,0:T(8,128)(2,1)S(1)}, u32[]{:S(2)}, u32[]{:S(2)}) %collective-permute-start.24) | collective-permute-done | bytes 557088 | tf_op jit(solution)/shard_map/ppermute | solution.py:250
  140.4 3.4 %collective-permute-start.30 = (bf16[128,2176]{1,0:T(8,128)(2,1)S(1)}, bf16[128,2176]{1,0:T(8,128)(2,1)S(1)}, u32[]{:S(2)}, u32[]{:S(2)}) collective-permute-start(bf16[128,2176]{1,0:T(8,128)(2,1)S(1)} %get-tuple-element.189), channel_id=1, source_target_pairs={{0,4},{1,5},{2,6},{3,7},{4,0},{5,1},{6,2},{7,3},{8,12},{9,13},{10,... | collective-permute-start | bytes 1671176 | tf_op jit(solution)/shard_map/ppermute | solution.py:250
  145.6 4.4 %collective-permute-done.6.refs_4_ = bf16[80,2176]{1,0:T(8,128)(2,1)S(1)} collective-permute-done((bf16[80,2176]{1,0:T(8,128)(2,1)S(1)}, bf16[80,2176]{1,0:T(8,128)(2,1)S(1)}, u32[]{:S(2)}, u32[]{:S(2)}) %collective-permute-start.6) | collective-permute-done | bytes 348192 | tf_op jit(solution)/shard_map/ppermute | solution.py:250
  153.0 4.3 %collective-permute-done.30.refs_1_ = bf16[128,2176]{1,0:T(8,128)(2,1)S(1)} collective-permute-done((bf16[128,2176]{1,0:T(8,128)(2,1)S(1)}, bf16[128,2176]{1,0:T(8,128)(2,1)S(1)}, u32[]{:S(2)}, u32[]{:S(2)}) %collective-permute-start.30) | collective-permute-done | bytes 557088 | tf_op jit(solution)/shard_map/ppermute | solution.py:250
  157.6 2.4 %adapter_grads.1 = (f32[1,32,2048]{2,1,0:T(8,128)}, f32[1,32,768]{2,1,0:T(8,128)}, f32[1,32,2048]{2,1,0:T(8,128)}, f32[1,32,768]{2,1,0:T(8,128)}, f32[1,32,768]{...) custom-call(bf16[40,4224]{1,0:T(8,128)(2,1)S(1)} %get-tuple-element.113.refs_0_, ...), custom_call_target="tpu_custom_call" | custom-call | flops 1 | bytes 15000000 | tf_op jit(solution)/shard_map/adapter_grads/pallas_call | solution.py:259
  159.9 11.1 %collective-permute-done.31.refs_1_ = bf16[128,2176]{1,0:T(8,128)(2,1)S(1)} collective-permute-done((bf16[128,2176]{1,0:T(8,128)(2,1)S(1)}, bf16[128,2176]{1,0:T(8,128)(2,1)S(1)}, u32[]{:S(2)}, u32[]{:S(2)}) %collective-permute-start.31) | collective-permute-done | bytes 557088 | tf_op jit(solution)/shard_map/ppermute | solution.py:250
  (77 shorter events, 30.4 us)
Async XLA Ops:
  5.2 27.9 %collective-permute-start.3 = (bf16[128,4224]{1,0:T(8,128)(2,1)}, bf16[128,4224]{1,0:T(8,128)(2,1)}, u32[]{:S(2)}, u32[]{:S(2)}) collective-permute-start(bf16[128,4224]{1,0:T(8,128)(2,1)} %get-tuple-element.110.refs_1_), channel_id=1, source_target_pairs={{4,8},{5,9},{6,10},{7,11},{8,4},{9,5},{10,6},{11,7},{20,24},{21,25... | collective-permute-start | bytes 3244040 | tf_op jit(solution)/shard_map/ppermute | solution.py:250
  7.7 25.7 %collective-permute-start.2 = (bf16[128,4224]{1,0:T(8,128)(2,1)}, bf16[128,4224]{1,0:T(8,128)(2,1)}, u32[]{:S(2)}, u32[]{:S(2)}) collective-permute-start(bf16[128,4224]{1,0:T(8,128)(2,1)} %get-tuple-element.110.refs_1_), channel_id=1, source_target_pairs={{0,4},{1,5},{2,6},{3,7},{4,0},{5,1},{6,2},{7,3},{8,12},{9,13},{10,... | collective-permute-start | bytes 3244040 | tf_op jit(solution)/shard_map/ppermute | solution.py:250
  10.6 28.3 %collective-permute-start.1 = (bf16[80,4224]{1,0:T(8,128)(2,1)S(1)}, bf16[80,4224]{1,0:T(8,128)(2,1)S(1)}, u32[]{:S(2)}, u32[]{:S(2)}) collective-permute-start(bf16[80,4224]{1,0:T(8,128)(2,1)S(1)} %get-tuple-element.115), channel_id=1, source_target_pairs={{0,2},{1,3},{2,0},{3,1},{4,6},{5,7},{6,4},{7,5},{8,10},{9,11},{10,... | collective-permute-start | bytes 2027528 | tf_op jit(solution)/shard_map/ppermute | solution.py:250
  33.4 26.6 %collective-permute-start.7 = (bf16[128,4224]{1,0:T(8,128)(2,1)}, bf16[128,4224]{1,0:T(8,128)(2,1)S(1)}, u32[]{:S(2)}, u32[]{:S(2)}) collective-permute-start(bf16[128,4224]{1,0:T(8,128)(2,1)} %collective-permute-done.2.refs_1_), channel_id=1, source_target_pairs={{4,8},{5,9},{6,10},{7,11},{8,4},{9,5},{10,6},{11,7},{20,24},{21,25... | collective-permute-start | bytes 3244040 | tf_op jit(solution)/shard_map/ppermute | solution.py:250
  36.9 24.4 %collective-permute-start.8 = (bf16[128,4224]{1,0:T(8,128)(2,1)}, bf16[128,4224]{1,0:T(8,128)(2,1)S(1)}, u32[]{:S(2)}, u32[]{:S(2)}) collective-permute-start(bf16[128,4224]{1,0:T(8,128)(2,1)} %collective-permute-done.3.refs_1_), channel_id=1, source_target_pairs={{0,4},{1,5},{2,6},{3,7},{4,0},{5,1},{6,2},{7,3},{8,12},{9,13},{10,... | collective-permute-start | bytes 3244040 | tf_op jit(solution)/shard_map/ppermute | solution.py:250
  38.9 2.8 %collective-permute-start.4 = (bf16[80,4224]{1,0:T(8,128)(2,1)S(1)}, bf16[80,4224]{1,0:T(8,128)(2,1)S(1)}, u32[]{:S(2)}, u32[]{:S(2)}) collective-permute-start(bf16[80,4224]{1,0:T(8,128)(2,1)S(1)} %collective-permute-done.1.refs_2_), channel_id=1, source_target_pairs={{0,1},{1,0},{2,3},{3,2},{4,5},{5,4},{6,7},{7,6},{8,9},{9,8},{10,11... | collective-permute-start | bytes 2027528 | tf_op jit(solution)/shard_map/ppermute | solution.py:250
  39.0 2.6 %collective-permute-start = (bf16[40,4224]{1,0:T(8,128)(2,1)S(1)}, bf16[40,4224]{1,0:T(8,128)(2,1)S(1)}, u32[]{:S(2)}, u32[]{:S(2)}) collective-permute-start(bf16[40,4224]{1,0:T(8,128)(2,1)S(1)} %get-tuple-element.114), channel_id=1, source_target_pairs={{0,1},{1,0},{2,3},{3,2},{4,5},{5,4},{6,7},{7,6},{8,9},{9,8},{10,11... | collective-permute-start | bytes 1013768 | tf_op jit(solution)/shard_map/ppermute | solution.py:250
  39.5 17.2 %collective-permute-start.10 = (bf16[80,4224]{1,0:T(8,128)(2,1)S(1)}, bf16[80,4224]{1,0:T(8,128)(2,1)S(1)}, u32[]{:S(2)}, u32[]{:S(2)}) collective-permute-start(bf16[80,4224]{1,0:T(8,128)(2,1)S(1)} %get-tuple-element.136), channel_id=1, source_target_pairs={{0,2},{1,3},{2,0},{3,1},{4,6},{5,7},{6,4},{7,5},{8,10},{9,11},{10,... | collective-permute-start | bytes 2027528 | tf_op jit(solution)/shard_map/ppermute | solution.py:250
  41.6 9.3 %collective-permute-start.9 = (bf16[40,4224]{1,0:T(8,128)(2,1)S(1)}, bf16[40,4224]{1,0:T(8,128)(2,1)S(1)}, u32[]{:S(2)}, u32[]{:S(2)}) collective-permute-start(bf16[40,4224]{1,0:T(8,128)(2,1)S(1)} %get-tuple-element.135), channel_id=1, source_target_pairs={{0,1},{1,0},{2,3},{3,2},{4,5},{5,4},{6,7},{7,6},{8,9},{9,8},{10,11... | collective-permute-start | bytes 1013768 | tf_op jit(solution)/shard_map/ppermute | solution.py:250
  62.7 2.2 %collective-permute-start.14 = (bf16[80,4224]{1,0:T(8,128)(2,1)S(1)}, bf16[80,4224]{1,0:T(8,128)(2,1)S(1)}, u32[]{:S(2)}, u32[]{:S(2)}) collective-permute-start(bf16[80,4224]{1,0:T(8,128)(2,1)S(1)} %collective-permute-done.10.refs_2_.refs_6_), channel_id=1, source_target_pairs={{0,1},{1,0},{2,3},{3,2},{4,5},{5,4},{6,7},{7,6},{8,9},{9,8},{10,11... | collective-permute-start | bytes 2027528 | tf_op jit(solution)/shard_map/ppermute | solution.py:250
  62.8 17.6 %collective-permute-start.13 = (bf16[80,4224]{1,0:T(8,128)(2,1)S(1)}, bf16[80,4224]{1,0:T(8,128)(2,1)S(1)}, u32[]{:S(2)}, u32[]{:S(2)}) collective-permute-start(bf16[80,4224]{1,0:T(8,128)(2,1)S(1)} %get-tuple-element.143), channel_id=1, source_target_pairs={{0,2},{1,3},{2,0},{3,1},{4,6},{5,7},{6,4},{7,5},{8,10},{9,11},{10,... | collective-permute-start | bytes 2027528 | tf_op jit(solution)/shard_map/ppermute | solution.py:250
  64.3 25.9 %collective-permute-start.11 = (bf16[128,4224]{1,0:T(8,128)(2,1)S(1)}, bf16[128,4224]{1,0:T(8,128)(2,1)S(1)}, u32[]{:S(2)}, u32[]{:S(2)}) collective-permute-start(bf16[128,4224]{1,0:T(8,128)(2,1)S(1)} %collective-permute-done.7.refs_1_), channel_id=1, source_target_pairs={{0,4},{1,5},{2,6},{3,7},{4,0},{5,1},{6,2},{7,3},{8,12},{9,13},{10,... | collective-permute-start | bytes 3244040 | tf_op jit(solution)/shard_map/ppermute | solution.py:250
  80.3 2.6 %collective-permute-start.15 = (bf16[80,4224]{1,0:T(8,128)(2,1)S(1)}, bf16[80,4224]{1,0:T(8,128)(2,1)S(1)}, u32[]{:S(2)}, u32[]{:S(2)}) collective-permute-start(bf16[80,4224]{1,0:T(8,128)(2,1)S(1)} %collective-permute-done.13.refs_2_.refs_10_), channel_id=1, source_target_pairs={{0,1},{1,0},{2,3},{3,2},{4,5},{5,4},{6,7},{7,6},{8,9},{9,8},{10,11... | collective-permute-start | bytes 2027528 | tf_op jit(solution)/shard_map/ppermute | solution.py:250
  80.3 2.6 %collective-permute-start.12 = (bf16[40,4224]{1,0:T(8,128)(2,1)S(1)}, bf16[40,4224]{1,0:T(8,128)(2,1)S(1)}, u32[]{:S(2)}, u32[]{:S(2)}) collective-permute-start(bf16[40,4224]{1,0:T(8,128)(2,1)S(1)} %get-tuple-element.142), channel_id=1, source_target_pairs={{0,1},{1,0},{2,3},{3,2},{4,5},{5,4},{6,7},{7,6},{8,9},{9,8},{10,11... | collective-permute-start | bytes 1013768 | tf_op jit(solution)/shard_map/ppermute | solution.py:250
  88.4 11.1 %collective-permute-start.19 = (bf16[80,2176]{1,0:T(8,128)(2,1)S(1)}, bf16[80,2176]{1,0:T(8,128)(2,1)S(1)}, u32[]{:S(2)}, u32[]{:S(2)}) collective-permute-start(bf16[80,2176]{1,0:T(8,128)(2,1)S(1)} %get-tuple-element.163), channel_id=1, source_target_pairs={{0,2},{1,3},{2,0},{3,1},{4,6},{5,7},{6,4},{7,5},{8,10},{9,11},{10,... | collective-permute-start | bytes 1044488 | tf_op jit(solution)/shard_map/ppermute | solution.py:250
  92.4 20.7 %collective-permute-start.17 = (bf16[80,4224]{1,0:T(8,128)(2,1)S(1)}, bf16[80,4224]{1,0:T(8,128)(2,1)S(1)}, u32[]{:S(2)}, u32[]{:S(2)}) collective-permute-start(bf16[80,4224]{1,0:T(8,128)(2,1)S(1)} %get-tuple-element.159), channel_id=1, source_target_pairs={{0,2},{1,3},{2,0},{3,1},{4,6},{5,7},{6,4},{7,5},{8,10},{9,11},{10,... | collective-permute-start | bytes 2027528 | tf_op jit(solution)/shard_map/ppermute | solution.py:250
  99.4 1.9 %collective-permute-start.20 = (bf16[80,2176]{1,0:T(8,128)(2,1)S(1)}, bf16[80,2176]{1,0:T(8,128)(2,1)S(1)}, u32[]{:S(2)}, u32[]{:S(2)}) collective-permute-start(bf16[80,2176]{1,0:T(8,128)(2,1)S(1)} %collective-permute-done.19.refs_4_), channel_id=1, source_target_pairs={{0,1},{1,0},{2,3},{3,2},{4,5},{5,4},{6,7},{7,6},{8,9},{9,8},{10,11... | collective-permute-start | bytes 1044488 | tf_op jit(solution)/shard_map/ppermute | solution.py:250
  99.4 1.9 %collective-permute-start.18 = (bf16[40,2176]{1,0:T(8,128)(2,1)S(1)}, bf16[40,2176]{1,0:T(8,128)(2,1)S(1)}, u32[]{:S(2)}, u32[]{:S(2)}) collective-permute-start(bf16[40,2176]{1,0:T(8,128)(2,1)S(1)} %get-tuple-element.162), channel_id=1, source_target_pairs={{0,1},{1,0},{2,3},{3,2},{4,5},{5,4},{6,7},{7,6},{8,9},{9,8},{10,11... | collective-permute-start | bytes 522248 | tf_op jit(solution)/shard_map/ppermute | solution.py:250
  113.1 3.2 %collective-permute-start.21 = (bf16[80,4224]{1,0:T(8,128)(2,1)S(1)}, bf16[80,4224]{1,0:T(8,128)(2,1)S(1)}, u32[]{:S(2)}, u32[]{:S(2)}) collective-permute-start(bf16[80,4224]{1,0:T(8,128)(2,1)S(1)} %collective-permute-done.17.refs_2_.refs_14_), channel_id=1, source_target_pairs={{0,1},{1,0},{2,3},{3,2},{4,5},{5,4},{6,7},{7,6},{8,9},{9,8},{10,11... | collective-permute-start | bytes 2027528 | tf_op jit(solution)/shard_map/ppermute | solution.py:250
  113.1 10.6 %collective-permute-start.26 = (bf16[80,2176]{1,0:T(8,128)(2,1)S(1)}, bf16[80,2176]{1,0:T(8,128)(2,1)S(1)}, u32[]{:S(2)}, u32[]{:S(2)}) collective-permute-start(bf16[80,2176]{1,0:T(8,128)(2,1)S(1)} %get-tuple-element.177), channel_id=1, source_target_pairs={{0,2},{1,3},{2,0},{3,1},{4,6},{5,7},{6,4},{7,5},{8,10},{9,11},{10,... | collective-permute-start | bytes 1044488 | tf_op jit(solution)/shard_map/ppermute | solution.py:250
  114.6 1.6 collective-permute-start.16
  114.8 24.6 %collective-permute-start.24 = (bf16[128,2176]{1,0:T(8,128)(2,1)S(1)}, bf16[128,2176]{1,0:T(8,128)(2,1)S(1)}, u32[]{:S(2)}, u32[]{:S(2)}) collective-permute-start(bf16[128,2176]{1,0:T(8,128)(2,1)S(1)} %get-tuple-element.173), channel_id=1, source_target_pairs={{0,8},{1,9},{2,10},{3,11},{4,12},{5,13},{6,14},{7,15},{8,0},{9,1},... | collective-permute-start | bytes 1671176 | tf_op jit(solution)/shard_map/ppermute | solution.py:250
  123.7 2.9 %collective-permute-start.27 = (bf16[80,2176]{1,0:T(8,128)(2,1)S(1)}, bf16[80,2176]{1,0:T(8,128)(2,1)S(1)}, u32[]{:S(2)}, u32[]{:S(2)}) collective-permute-start(bf16[80,2176]{1,0:T(8,128)(2,1)S(1)} %collective-permute-done.26.refs_4_), channel_id=1, source_target_pairs={{0,1},{1,0},{2,3},{3,2},{4,5},{5,4},{6,7},{7,6},{8,9},{9,8},{10,11... | collective-permute-start | bytes 1044488 | tf_op jit(solution)/shard_map/ppermute | solution.py:250
  123.7 15.8 %collective-permute-start.23 = (bf16[80,2176]{1,0:T(8,128)(2,1)S(1)}, bf16[80,2176]{1,0:T(8,128)(2,1)S(1)}, u32[]{:S(2)}, u32[]{:S(2)}) collective-permute-start(bf16[80,2176]{1,0:T(8,128)(2,1)S(1)} %get-tuple-element.172), channel_id=1, source_target_pairs={{0,2},{1,3},{2,0},{3,1},{4,6},{5,7},{6,4},{7,5},{8,10},{9,11},{10,... | collective-permute-start | bytes 1044488 | tf_op jit(solution)/shard_map/ppermute | solution.py:250
  125.2 1.4 collective-permute-start.25
  139.4 4.5 %collective-permute-start.28 = (bf16[80,2176]{1,0:T(8,128)(2,1)S(1)}, bf16[80,2176]{1,0:T(8,128)(2,1)S(1)}, u32[]{:S(2)}, u32[]{:S(2)}) collective-permute-start(bf16[80,2176]{1,0:T(8,128)(2,1)S(1)} %collective-permute-done.23.refs_4_), channel_id=1, source_target_pairs={{0,1},{1,0},{2,3},{3,2},{4,5},{5,4},{6,7},{7,6},{8,9},{9,8},{10,11... | collective-permute-start | bytes 1044488 | tf_op jit(solution)/shard_map/ppermute | solution.py:250
  139.4 4.4 %collective-permute-start.22 = (bf16[40,2176]{1,0:T(8,128)(2,1)S(1)}, bf16[40,2176]{1,0:T(8,128)(2,1)S(1)}, u32[]{:S(2)}, u32[]{:S(2)}) collective-permute-start(bf16[40,2176]{1,0:T(8,128)(2,1)S(1)} %get-tuple-element.171), channel_id=1, source_target_pairs={{0,1},{1,0},{2,3},{3,2},{4,5},{5,4},{6,7},{7,6},{8,9},{9,8},{10,11... | collective-permute-start | bytes 522248 | tf_op jit(solution)/shard_map/ppermute | solution.py:250
  139.9 10.1 %collective-permute-start.6 = (bf16[80,2176]{1,0:T(8,128)(2,1)S(1)}, bf16[80,2176]{1,0:T(8,128)(2,1)S(1)}, u32[]{:S(2)}, u32[]{:S(2)}) collective-permute-start(bf16[80,2176]{1,0:T(8,128)(2,1)S(1)} %get-tuple-element.132), channel_id=1, source_target_pairs={{0,2},{1,3},{2,0},{3,1},{4,6},{5,7},{6,4},{7,5},{8,10},{9,11},{10,... | collective-permute-start | bytes 1044488 | tf_op jit(solution)/shard_map/ppermute | solution.py:250
  140.4 16.9 %collective-permute-start.30 = (bf16[128,2176]{1,0:T(8,128)(2,1)S(1)}, bf16[128,2176]{1,0:T(8,128)(2,1)S(1)}, u32[]{:S(2)}, u32[]{:S(2)}) collective-permute-start(bf16[128,2176]{1,0:T(8,128)(2,1)S(1)} %get-tuple-element.189), channel_id=1, source_target_pairs={{0,4},{1,5},{2,6},{3,7},{4,0},{5,1},{6,2},{7,3},{8,12},{9,13},{10,... | collective-permute-start | bytes 1671176 | tf_op jit(solution)/shard_map/ppermute | solution.py:250
  145.0 26.0 %collective-permute-start.31 = (bf16[128,2176]{1,0:T(8,128)(2,1)S(1)}, bf16[128,2176]{1,0:T(8,128)(2,1)S(1)}, u32[]{:S(2)}, u32[]{:S(2)}) collective-permute-start(bf16[128,2176]{1,0:T(8,128)(2,1)S(1)} %get-tuple-element.193), channel_id=1, source_target_pairs={{0,12},{1,13},{2,14},{3,15},{4,8},{5,9},{6,10},{7,11},{8,4},{9,5},... | collective-permute-start | bytes 1671176 | tf_op jit(solution)/shard_map/ppermute | solution.py:250
  150.0 1.9 %collective-permute-start.29 = (bf16[80,2176]{1,0:T(8,128)(2,1)S(1)}, bf16[80,2176]{1,0:T(8,128)(2,1)S(1)}, u32[]{:S(2)}, u32[]{:S(2)}) collective-permute-start(bf16[80,2176]{1,0:T(8,128)(2,1)S(1)} %collective-permute-done.6.refs_4_), channel_id=1, source_target_pairs={{0,1},{1,0},{2,3},{3,2},{4,5},{5,4},{6,7},{7,6},{8,9},{9,8},{10,11... | collective-permute-start | bytes 1044488 | tf_op jit(solution)/shard_map/ppermute | solution.py:250
  150.0 1.9 %collective-permute-start.5 = (bf16[40,2176]{1,0:T(8,128)(2,1)S(1)}, bf16[40,2176]{1,0:T(8,128)(2,1)S(1)}, u32[]{:S(2)}, u32[]{:S(2)}) collective-permute-start(bf16[40,2176]{1,0:T(8,128)(2,1)S(1)} %get-tuple-element.131), channel_id=1, source_target_pairs={{0,1},{1,0},{2,3},{3,2},{4,5},{5,4},{6,7},{7,6},{8,9},{9,8},{10,11... | collective-permute-start | bytes 522248 | tf_op jit(solution)/shard_map/ppermute | solution.py:250
  (13 other events, 50.0 us)

commit v3 on v2

--- a/solution.py
+++ b/solution.py
@@ -50,18 +50,25 @@
     return turned, found
 
 
-def pack_kernel(routes, x_ref, grad_ref, ids_ref, weight_ref, out_ref):
+def pack_kernel(routes, x_ref, grad_ref, ids_ref, weight_ref, out_ref, ids_buf, weight_buf, sems):
     tokens, width = grad_ref.shape
-    out_ref[:, :width] = x_ref[...]
-    out_ref[:, width : 2 * width] = grad_ref[...]
-    names = ids_ref[...].astype(F32) + 1.0
-    high, low = two_parts(weight_ref[...])
+    targets = (out_ref.at[:, :width], out_ref.at[:, width : 2 * width], ids_buf, weight_buf)
+    sources = (x_ref, grad_ref, ids_ref, weight_ref)
+    copies = [pltpu.make_async_copy(a, b, sems.at[n]) for n, (a, b) in enumerate(zip(sources, targets))]
+    for copy in copies:
+        copy.start()
+    copies[2].wait()
+    copies[3].wait()
+    names = ids_buf[...].astype(F32) + 1.0
+    high, low = two_parts(weight_buf[...])
     row = lax.broadcasted_iota(jnp.int32, (LANES, tokens), 0)
     side = jnp.zeros((LANES, tokens), F32)
     for group, values in enumerate((names, names, high, low)):
         for k in range(routes):
             side = jnp.where(row == group * routes + k, values[k : k + 1, :], side)
     out_ref[:, 2 * width :] = side.T.astype(BF16)
+    copies[0].wait()
+    copies[1].wait()
 
 
 def select_kernel(routes, slots, choices, stage, info_ref, *refs):
@@ -162,8 +169,8 @@
 
 
 def combine_kernel(routes, slots, info_ref, side_ref, *refs):
-    backs, out_ref = refs[:PLANE], refs[PLANE]
-    width = out_ref.shape[1] - LANES
+    backs, outs = refs[:PLANE], refs[PLANE:]
+    width = backs[0].shape[1] - LANES
     side = side_ref[...].astype(F32)
     names = [info_ref[m].astype(F32) + 1.0 for m in range(PLANE)]
     _, found = one_hots(names, slots, side, routes)
@@ -173,16 +180,26 @@
         hot = jnp.concatenate([h if n == m else jnp.zeros_like(h) for n, (h, _) in enumerate(found)], axis=0)
         spread = lax.dot_general(hot.astype(BF16), tails, (((0,), (0,)), ((), ())), preferred_element_type=F32)
         extra = extra + jnp.where(side == names[m], spread, 0.0)
-    out_ref[:, width:] = extra.astype(BF16)
     picks = jnp.concatenate([hot for hot, _ in found], axis=0).astype(BF16)
     rows = stacked(backs, 0, width).astype(BF16)
-    out_ref[:, :width] = lax.dot_general(
-        picks, rows, (((0,), (0,)), ((), ())), preferred_element_type=F32
-    ).astype(BF16)
+    total = lax.dot_general(picks, rows, (((0,), (0,)), ((), ())), preferred_element_type=F32)
+    low = 0
+    for out in outs:
+        end = min(low + out.shape[1], width)
+        out[:, : end - low] = total[:, low:end].astype(BF16)
+        low = end
+    outs[-1][:, outs[-1].shape[1] - LANES :] = extra.astype(BF16)
 
 
 def add_kernel(*refs):
-    refs[-1][...] = sum(r[...].astype(F32) for r in refs[:-1])
+    out_ref, width, low, total = refs[-1], refs[-1].shape[1], 0, {}
+    for r in refs[:-1]:
+        total.setdefault((low, low + r.shape[1]), []).append(r[...].astype(F32))
+        low = (low + r.shape[1]) % width
+    whole = sum(total.pop((0, width)))
+    out_ref[...] = whole
+    for (low, end), values in total.items():
+        out_ref[:, low:end] = whole[:, low:end] + sum(values)
 
 
 def finish_kernel(routes, *refs):
@@ -249,18 +266,22 @@
         pairs = [(p * PLANE + n, (p * PLANE + n) ^ mask) for p in sources for n in range(PLANE)]
         return lax.ppermute(value, "expert", pairs)
 
-    def kernel(body, outs, args, micros, name, mib, scalars=0):
+    def kernel(body, outs, args, micros, name, mib, scalars=0, where=pltpu.VMEM, scratch=()):
         vmem = pl.BlockSpec(memory_space=pltpu.VMEM)
 
         def run(*refs):
-            refs[len(args) + len(last) + len(outs)][...] = jnp.zeros((8, LANES), F32)
-            body(*refs[: len(args)], *refs[len(args) + len(last) : -1])
+            given, rest = refs[: len(args)], refs[len(args) + len(last) :]
+            rest[len(outs)][...] = jnp.zeros((8, LANES), F32)
+            body(*given, *rest[: len(outs)], *rest[len(outs) + 1 :])
 
         *result, mark = pl.pallas_call(
             run,
             out_shape=[*outs, shape((8, LANES), F32)],
-            in_specs=[smem()] * scalars + [vmem] * (len(args) - scalars + len(last)),
+            in_specs=[smem()] * scalars
+            + [pl.BlockSpec(memory_space=where)] * (len(args) - scalars)
+            + [vmem] * len(last),
             out_specs=[vmem] * (len(outs) + 1),
+            scratch_shapes=list(scratch),
             compiler_params=pltpu.CompilerParams(vmem_limit_bytes=mib * MIB),
             cost_estimate=pl.CostEstimate(flops=1, bytes_accessed=micros * RATE, transcendentals=0),
             name=name,
@@ -275,7 +296,13 @@
         (tokens, grad_out, expert_ids.T, combine.T),
         2,
         "pack",
-        6,
+        60,
+        where=pltpu.HBM,
+        scratch=(
+            pltpu.VMEM((routes, rows), jnp.int32),
+            pltpu.VMEM((routes, rows), F32),
+            pltpu.SemaphoreType.DMA((4,)),
+        ),
     )
 
     def expert(got):
@@ -295,14 +322,14 @@
 
     rows_of, sides, parts, acts, lows = {}, {}, {}, {}, {}
 
-    def halfway(own, near, far, sources):
-        return own, flipped(near, 1), flipped(far, 2, sources)
+    def halfway(own, near, far):
+        return own, flipped(near, 1), flipped(far, 2)
 
     def arrived(own, near, across):
         (across,) = together(across)
         return own, near, across, flipped(across, 1)
 
-    def begin(stage, *found, sources=range(planes)):
+    def begin(stage, *found):
         *picked, sides[stage] = kernel(
             functools.partial(select_kernel, routes, slots, len(found), stage),
             [shape((n * slots, 2 * width + LANES), BF16) for n in (1, 1, 2)] + [shape((rows, LANES), BF16)],
@@ -312,24 +339,24 @@
             12,
             scalars=1,
         )
-        rows_of[stage] = halfway(*picked, sources)
-
-    def middle_of(stage, sources=range(planes)):
+        rows_of[stage] = halfway(*picked)
+
+    def middle_of(stage):
         rows_of[stage] = arrived(*rows_of[stage])
         *backs, acts[stage], lows[stage] = expert(rows_of[stage])
-        parts[stage] = halfway(*backs, sources)
-
-    def end_of(stage, toward, sources=range(planes)):
-        (part,) = kernel(
+        parts[stage] = halfway(*backs)
+
+    def end_of(stage, *columns):
+        found = kernel(
             functools.partial(combine_kernel, routes, slots),
-            [shape((rows, wide), BF16)],
+            [shape((rows, c), BF16) for c in columns or (wide,)],
             (info, sides[stage], *arrived(*parts[stage])),
             3,
             "combine",
             8,
             scalars=1,
         )
-        parts[stage] = flipped(part, toward * PLANE, sources) if toward else part
+        parts[stage] = [flipped(part, stage * PLANE) if stage else part for part in found]
 
     def add(*values):
         return kernel(add_kernel, [shape((rows, wide), F32)], values, 1, "add", 8)[0]
@@ -370,12 +397,13 @@
         middle_of(2)
         (farthest,) = together(farthest)
         begin(3, across, farthest)
-        end_of(2, 2)
+        end_of(2, 640, wide - 640)
+        (parts[2][0],) = together(parts[2][0])
         middle_of(3)
-        end_of(1, 1)
-        (parts[2],) = together(parts[2])
-        end_of(3, 3)
-        end_of(0, 0)
+        end_of(1)
+        (parts[2][1],) = together(parts[2][1])
+        end_of(3)
+        end_of(0)
     else:
         blocks = {0: packed}
         for step in range(1, planes):
@@ -385,9 +413,9 @@
         for stage in range(planes):
             begin(stage, *(blocks[o] for o in offsets[stage]))
             middle_of(stage)
-            end_of(stage, stage)
+            end_of(stage)
     order = sorted(rows_of)
-    total = add(*(parts[n] for n in order[:-1]))
+    total = add(*(part for n in order[:-1] for part in parts[n]))
 
     grads = kernel(
         functools.partial(adapter_kernel, len(order), rank),
@@ -400,7 +428,7 @@
     grad_tokens, grad_combine = kernel(
         functools.partial(finish_kernel, routes),
         [shape((rows, width), BF16), shape((routes, rows), F32)],
-        (total, parts[order[-1]]),
+        (total, *parts[order[-1]]),
         3,
         "finish",
         8,

time: 174 us -> 165 us (0.948)
  waiting for transfers between devices: 94.9 us -> 88.3 us
    ppermute x32 -> x33, waiting for transfers between devices: 94.9 us -> 88.3 us  [flipped(): return lax.ppermute(value, 'expert', pairs)]
    unnamed x26 -> x22, local copies, waits for them, and re-layouts: 12.3 us -> 10.8 us
    ppermute x32 -> x33, starting transfers between devices: 25.3 us -> 23.9 us  [flipped(): return lax.ppermute(value, 'expert', pairs)]
  transfers between devices with their start and end apart: 32 -> 33, of which waited for: 21 -> 23; matrix products, arithmetic and copies ran while one was open for 0% -> 0% of each run, Pallas kernels for 20% -> 21%
where the time goes in v3:
time: 165 us; the launch traced here: 163 us
  waiting for transfers between devices  88.3 us (54%)
  Pallas kernels  38.9 us (24%)
  starting transfers between devices  23.9 us (14%)
  local copies, waits for them, and re-layouts  10.9 us (7%)
    ppermute x33, waiting for transfers between devices, flipped(): return lax.ppermute(value, 'expert', pairs)  88.3 us
    pallas_call x17, Pallas kernels, kernel(): pl.pallas_call(run, out_shape=[*outs, shape((8, LANES), F32)], in_specs=[...  38.9 us
    ppermute x33, starting transfers between devices, flipped(): return lax.ppermute(value, 'expert', pairs)  23.9 us
    unnamed x22, local copies, waits for them, and re-layouts  10.8 us
  transfers between devices with their start and end apart: 33, of which 23 were waited for; matrix products, arithmetic and copies ran while one was open for 0% of the time, Pallas kernels for 21%

profile of v3, /device:TPU:16, one launch (start us, length us, event | category | flops | bytes accessed | tf_op | source)
XLA Modules:
  0.0 162.7 jit_solution(3710669540626708992)
XLA Ops:
  0.6 2.4 %pack.1 = (bf16[128,4224]{1,0:T(8,128)(2,1)}, f32[8,128]{1,0:T(8,128)}) custom-call(bf16[128,2048]{1,0:T(8,128)(2,1)} %refs_0_.1, bf16[128,2048]{1,0:T(8,128)(2,1)} %refs_1_.1, s32[4,128]{1,0:T(4,128)} %bitcast.35, f32[4,128]{1,0:T(4,128)} %bitcast.36), custom_call_target="tpu_custom_call" | custom-call | flops 1 | bytes 6000000 | tf_op jit(solution)/shard_map/pack/pallas_call | solution.py:277
  3.0 2.4 %collective-permute-start.3 = (bf16[128,4224]{1,0:T(8,128)(2,1)}, bf16[128,4224]{1,0:T(8,128)(2,1)}, u32[]{:S(2)}, u32[]{:S(2)}) collective-permute-start(bf16[128,4224]{1,0:T(8,128)(2,1)} %get-tuple-element.113.refs_1_), channel_id=1, source_target_pairs={{4,8},{5,9},{6,10},{7,11},{8,4},{9,5},{10,6},{11,7},{20,24},{21,25... | collective-permute-start | bytes 3244040 | tf_op jit(solution)/shard_map/ppermute | solution.py:267
  9.6 1.6 collective-permute-start.1
  16.8 14.1 %collective-permute-done.3.refs_1_ = bf16[128,4224]{1,0:T(8,128)(2,1)} collective-permute-done((bf16[128,4224]{1,0:T(8,128)(2,1)}, bf16[128,4224]{1,0:T(8,128)(2,1)}, u32[]{:S(2)}, u32[]{:S(2)}) %collective-permute-start.3) | collective-permute-done | bytes 1081376 | tf_op jit(solution)/shard_map/ppermute | solution.py:267
  31.1 3.5 %collective-permute-start.7 = (bf16[128,4224]{1,0:T(8,128)(2,1)}, bf16[128,4224]{1,0:T(8,128)(2,1)S(1)}, u32[]{:S(2)}, u32[]{:S(2)}) collective-permute-start(bf16[128,4224]{1,0:T(8,128)(2,1)} %collective-permute-done.2.refs_1_), channel_id=1, source_target_pairs={{4,8},{5,9},{6,10},{7,11},{8,4},{9,5},{10,6},{11,7},{20,24},{21,25... | collective-permute-start | bytes 3244040 | tf_op jit(solution)/shard_map/ppermute | solution.py:267
  34.7 1.9 %select.11 = (bf16[40,4224]{1,0:T(8,128)(2,1)S(1)}, bf16[40,4224]{1,0:T(8,128)(2,1)S(1)}, bf16[80,4224]{1,0:T(8,128)(2,1)S(1)}, bf16[128,128]{1,0:T(8,128)(2,1)S(1)}, f32[8,128]{1,0:T(8,128)S(1)}) custom-call(s32[8]{0:T(128)S(1)} %stack.28.refs_0_, bf16[128,4224]{1,0:T(8,128)(2,1)} %collective-permute-done.2.refs_1_, f32[8,128]{1,0:T(8,128)S(1)} %get-tuple-element.122.refs_2_), custom_call_target="tpu_custom_call" | custom-call | flops 1 | bytes 12000000 | tf_op jit(solution)/shard_map/select/pallas_call | solution.py:277
  37.2 1.5 collective-permute-start.10
  39.4 1.9 %copy-done.1 = bf16[1,2048,768]{2,1,0:T(8,128)(2,1)S(1)} copy-done((bf16[1,2048,768]{2,1,0:T(8,128)(2,1)S(1)}, bf16[1,2048,768]{2,1,0:T(8,128)(2,1)}, u32[]{:S(2)}) %copy-start.1) | copy-done | bytes 3145752
  41.3 1.9 %copy-done.2 = bf16[1,768,2048]{2,1,0:T(8,128)(2,1)S(1)} copy-done((bf16[1,768,2048]{2,1,0:T(8,128)(2,1)S(1)}, bf16[1,768,2048]{2,1,0:T(8,128)(2,1)}, u32[]{:S(2)}) %copy-start.2) | copy-done | bytes 3145752
  43.2 5.3 %expert.4 = (bf16[40,2176]{1,0:T(8,128)(2,1)S(1)}, bf16[40,2176]{1,0:T(8,128)(2,1)S(1)}, bf16[80,2176]{1,0:T(8,128)(2,1)S(1)}, bf16[160,2304]{1,0:T(8,128)(2,1)S...) custom-call(bf16[40,4224]{1,0:T(8,128)(2,1)S(1)} %get-tuple-element.116.refs_0_, ...), custom_call_target="tpu_custom_call" | custom-call | flops 1 | bytes 24000000 | tf_op jit(solution)/shard_map/expert/pallas_call | solution.py:277
  48.5 5.8 %collective-permute-done.10.refs_2_.refs_6_ = bf16[80,4224]{1,0:T(8,128)(2,1)S(1)} collective-permute-done((bf16[80,4224]{1,0:T(8,128)(2,1)S(1)}, bf16[80,4224]{1,0:T(8,128)(2,1)S(1)}, u32[]{:S(2)}, u32[]{:S(2)}) %collective-permute-start.10) | collective-permute-done | bytes 675872 | tf_op jit(solution)/shard_map/ppermute | solution.py:267
  54.3 3.3 %collective-permute-done.7.refs_1_ = bf16[128,4224]{1,0:T(8,128)(2,1)S(1)} collective-permute-done((bf16[128,4224]{1,0:T(8,128)(2,1)}, bf16[128,4224]{1,0:T(8,128)(2,1)S(1)}, u32[]{:S(2)}, u32[]{:S(2)}) %collective-permute-start.7) | collective-permute-done | bytes 1081376 | tf_op jit(solution)/shard_map/ppermute | solution.py:267
  60.5 1.6 collective-permute-start.13
  62.6 5.3 %expert.5 = (bf16[40,2176]{1,0:T(8,128)(2,1)S(1)}, bf16[40,2176]{1,0:T(8,128)(2,1)S(1)}, bf16[80,2176]{1,0:T(8,128)(2,1)S(1)}, bf16[160,2304]{1,0:T(8,128)(2,1)S...) custom-call(bf16[40,4224]{1,0:T(8,128)(2,1)S(1)} %get-tuple-element.147.refs_0_.refs_4_, ...), custom_call_target="tpu_custom_call" | custom-call | flops 1 | bytes 24000000 | tf_op jit(solution)/shard_map/expert/pallas_call | solution.py:277
  67.9 10.2 %collective-permute-done.13.refs_2_.refs_10_ = bf16[80,4224]{1,0:T(8,128)(2,1)S(1)} collective-permute-done((bf16[80,4224]{1,0:T(8,128)(2,1)S(1)}, bf16[80,4224]{1,0:T(8,128)(2,1)S(1)}, u32[]{:S(2)}, u32[]{:S(2)}) %collective-permute-start.13) | collective-permute-done | bytes 675872 | tf_op jit(solution)/shard_map/ppermute | solution.py:267
  78.6 2.1 %collective-permute-done.12.refs_1_.refs_9_ = bf16[40,4224]{1,0:T(8,128)(2,1)S(1)} collective-permute-done((bf16[40,4224]{1,0:T(8,128)(2,1)S(1)}, bf16[40,4224]{1,0:T(8,128)(2,1)S(1)}, u32[]{:S(2)}, u32[]{:S(2)}) %collective-permute-start.12) | collective-permute-done | bytes 337952 | tf_op jit(solution)/shard_map/ppermute | solution.py:267
  80.7 5.3 %expert.6 = (bf16[40,2176]{1,0:T(8,128)(2,1)S(1)}, bf16[40,2176]{1,0:T(8,128)(2,1)S(1)}, bf16[80,2176]{1,0:T(8,128)(2,1)S(1)}, bf16[160,2304]{1,0:T(8,128)(2,1)S...) custom-call(bf16[40,4224]{1,0:T(8,128)(2,1)S(1)} %get-tuple-element.144.refs_0_.refs_8_, ...), custom_call_target="tpu_custom_call" | custom-call | flops 1 | bytes 24000000 | tf_op jit(solution)/shard_map/expert/pallas_call | solution.py:277
  86.0 1.6 collective-permute-start.19
  88.0 2.1 %select.13 = (bf16[40,4224]{1,0:T(8,128)(2,1)S(1)}, bf16[40,4224]{1,0:T(8,128)(2,1)S(1)}, bf16[80,4224]{1,0:T(8,128)(2,1)S(1)}, bf16[128,128]{1,0:T(8,128)(2,1)S(1)}, f32[8,128]{1,0:T(8,128)S(1)}) custom-call(s32[8]{0:T(128)S(1)} %stack.28.refs_0_, bf16[128,4224]{1,0:T(8,128)(2,1)} %collective-permute-done.3.refs_1_, ...), custom_call_target="tpu_custom_call" | custom-call | flops 1 | bytes 12000000 | tf_op jit(solution)/shard_map/select/pallas_call | solution.py:277
  90.7 6.3 %collective-permute-done.19.refs_4_ = bf16[80,2176]{1,0:T(8,128)(2,1)S(1)} collective-permute-done((bf16[80,2176]{1,0:T(8,128)(2,1)S(1)}, bf16[80,2176]{1,0:T(8,128)(2,1)S(1)}, u32[]{:S(2)}, u32[]{:S(2)}) %collective-permute-start.19) | collective-permute-done | bytes 348192 | tf_op jit(solution)/shard_map/ppermute | solution.py:267
  100.5 7.3 %collective-permute-done.21.refs_2_ = bf16[128,640]{1,0:T(8,128)(2,1)S(1)} collective-permute-done((bf16[128,640]{1,0:T(8,128)(2,1)S(1)}, bf16[128,640]{1,0:T(8,128)(2,1)S(1)}, u32[]{:S(2)}, u32[]{:S(2)}) %collective-permute-start.21) | collective-permute-done | bytes 163872 | tf_op jit(solution)/shard_map/ppermute | solution.py:267
  107.8 3.0 %collective-permute-done.17.refs_2_.refs_14_ = bf16[80,4224]{1,0:T(8,128)(2,1)S(1)} collective-permute-done((bf16[80,4224]{1,0:T(8,128)(2,1)S(1)}, bf16[80,4224]{1,0:T(8,128)(2,1)S(1)}, u32[]{:S(2)}, u32[]{:S(2)}) %collective-permute-start.17) | collective-permute-done | bytes 675872 | tf_op jit(solution)/shard_map/ppermute | solution.py:267
  110.8 1.5 collective-permute-start.27
  113.9 5.3 %expert.7 = (bf16[40,2176]{1,0:T(8,128)(2,1)S(1)}, bf16[40,2176]{1,0:T(8,128)(2,1)S(1)}, bf16[80,2176]{1,0:T(8,128)(2,1)S(1)}, bf16[160,2304]{1,0:T(8,128)(2,1)S...) custom-call(bf16[40,4224]{1,0:T(8,128)(2,1)S(1)} %get-tuple-element.160.refs_0_.refs_12_, ...), custom_call_target="tpu_custom_call" | custom-call | flops 1 | bytes 24000000 | tf_op jit(solution)/shard_map/expert/pallas_call | solution.py:277
  119.2 2.1 %collective-permute-done.27.refs_4_ = bf16[80,2176]{1,0:T(8,128)(2,1)S(1)} collective-permute-done((bf16[80,2176]{1,0:T(8,128)(2,1)S(1)}, bf16[80,2176]{1,0:T(8,128)(2,1)S(1)}, u32[]{:S(2)}, u32[]{:S(2)}) %collective-permute-start.27) | collective-permute-done | bytes 348192 | tf_op jit(solution)/shard_map/ppermute | solution.py:267
  121.3 1.5 collective-permute-start.24
  125.4 4.8 %collective-permute-done.25.refs_3_ = bf16[128,1536]{1,0:T(8,128)(2,1)S(1)} collective-permute-done((bf16[128,1536]{1,0:T(8,128)(2,1)S(1)}, bf16[128,1536]{1,0:T(8,128)(2,1)S(1)}, u32[]{:S(2)}, u32[]{:S(2)}) %collective-permute-start.25) | collective-permute-done | bytes 393248 | tf_op jit(solution)/shard_map/ppermute | solution.py:267
  130.2 1.7 %collective-permute-done.24.refs_4_ = bf16[80,2176]{1,0:T(8,128)(2,1)S(1)} collective-permute-done((bf16[80,2176]{1,0:T(8,128)(2,1)S(1)}, bf16[80,2176]{1,0:T(8,128)(2,1)S(1)}, u32[]{:S(2)}, u32[]{:S(2)}) %collective-permute-start.24) | collective-permute-done | bytes 348192 | tf_op jit(solution)/shard_map/ppermute | solution.py:267
  136.3 6.1 %collective-permute-done.6.refs_4_ = bf16[80,2176]{1,0:T(8,128)(2,1)S(1)} collective-permute-done((bf16[80,2176]{1,0:T(8,128)(2,1)S(1)}, bf16[80,2176]{1,0:T(8,128)(2,1)S(1)}, u32[]{:S(2)}, u32[]{:S(2)}) %collective-permute-start.6) | collective-permute-done | bytes 348192 | tf_op jit(solution)/shard_map/ppermute | solution.py:267
  145.5 3.9 %collective-permute-done.31.refs_1_ = bf16[128,2176]{1,0:T(8,128)(2,1)S(1)} collective-permute-done((bf16[128,2176]{1,0:T(8,128)(2,1)S(1)}, bf16[128,2176]{1,0:T(8,128)(2,1)S(1)}, u32[]{:S(2)}, u32[]{:S(2)}) %collective-permute-start.31) | collective-permute-done | bytes 557088 | tf_op jit(solution)/shard_map/ppermute | solution.py:267
  149.6 2.4 %adapter_grads.1 = (f32[1,32,2048]{2,1,0:T(8,128)}, f32[1,32,768]{2,1,0:T(8,128)}, f32[1,32,2048]{2,1,0:T(8,128)}, f32[1,32,768]{2,1,0:T(8,128)}, f32[1,32,768]{...) custom-call(bf16[40,4224]{1,0:T(8,128)(2,1)S(1)} %get-tuple-element.116.refs_0_, ...), custom_call_target="tpu_custom_call" | custom-call | flops 1 | bytes 15000000 | tf_op jit(solution)/shard_map/adapter_grads/pallas_call | solution.py:277
  152.0 9.7 %collective-permute-done.32.refs_1_ = bf16[128,2176]{1,0:T(8,128)(2,1)S(1)} collective-permute-done((bf16[128,2176]{1,0:T(8,128)(2,1)S(1)}, bf16[128,2176]{1,0:T(8,128)(2,1)S(1)}, u32[]{:S(2)}, u32[]{:S(2)}) %collective-permute-start.32) | collective-permute-done | bytes 557088 | tf_op jit(solution)/shard_map/ppermute | solution.py:267
  (75 shorter events, 32.5 us)
Async XLA Ops:
  3.0 27.8 %collective-permute-start.3 = (bf16[128,4224]{1,0:T(8,128)(2,1)}, bf16[128,4224]{1,0:T(8,128)(2,1)}, u32[]{:S(2)}, u32[]{:S(2)}) collective-permute-start(bf16[128,4224]{1,0:T(8,128)(2,1)} %get-tuple-element.113.refs_1_), channel_id=1, source_target_pairs={{4,8},{5,9},{6,10},{7,11},{8,4},{9,5},{10,6},{11,7},{20,24},{21,25... | collective-permute-start | bytes 3244040 | tf_op jit(solution)/shard_map/ppermute | solution.py:267
  5.4 25.7 %collective-permute-start.2 = (bf16[128,4224]{1,0:T(8,128)(2,1)}, bf16[128,4224]{1,0:T(8,128)(2,1)}, u32[]{:S(2)}, u32[]{:S(2)}) collective-permute-start(bf16[128,4224]{1,0:T(8,128)(2,1)} %get-tuple-element.113.refs_1_), channel_id=1, source_target_pairs={{0,4},{1,5},{2,6},{3,7},{4,0},{5,1},{6,2},{7,3},{8,12},{9,13},{10,... | collective-permute-start | bytes 3244040 | tf_op jit(solution)/shard_map/ppermute | solution.py:267
  9.6 27.0 %collective-permute-start.1 = (bf16[80,4224]{1,0:T(8,128)(2,1)S(1)}, bf16[80,4224]{1,0:T(8,128)(2,1)S(1)}, u32[]{:S(2)}, u32[]{:S(2)}) collective-permute-start(bf16[80,4224]{1,0:T(8,128)(2,1)S(1)} %get-tuple-element.118), channel_id=1, source_target_pairs={{0,2},{1,3},{2,0},{3,1},{4,6},{5,7},{6,4},{7,5},{8,10},{9,11},{10,... | collective-permute-start | bytes 2027528 | tf_op jit(solution)/shard_map/ppermute | solution.py:267
  31.1 26.6 %collective-permute-start.7 = (bf16[128,4224]{1,0:T(8,128)(2,1)}, bf16[128,4224]{1,0:T(8,128)(2,1)S(1)}, u32[]{:S(2)}, u32[]{:S(2)}) collective-permute-start(bf16[128,4224]{1,0:T(8,128)(2,1)} %collective-permute-done.2.refs_1_), channel_id=1, source_target_pairs={{4,8},{5,9},{6,10},{7,11},{8,4},{9,5},{10,6},{11,7},{20,24},{21,25... | collective-permute-start | bytes 3244040 | tf_op jit(solution)/shard_map/ppermute | solution.py:267
  34.6 24.4 %collective-permute-start.8 = (bf16[128,4224]{1,0:T(8,128)(2,1)}, bf16[128,4224]{1,0:T(8,128)(2,1)S(1)}, u32[]{:S(2)}, u32[]{:S(2)}) collective-permute-start(bf16[128,4224]{1,0:T(8,128)(2,1)} %collective-permute-done.3.refs_1_), channel_id=1, source_target_pairs={{0,4},{1,5},{2,6},{3,7},{4,0},{5,1},{6,2},{7,3},{8,12},{9,13},{10,... | collective-permute-start | bytes 3244040 | tf_op jit(solution)/shard_map/ppermute | solution.py:267
  36.6 2.8 %collective-permute-start.4 = (bf16[80,4224]{1,0:T(8,128)(2,1)S(1)}, bf16[80,4224]{1,0:T(8,128)(2,1)S(1)}, u32[]{:S(2)}, u32[]{:S(2)}) collective-permute-start(bf16[80,4224]{1,0:T(8,128)(2,1)S(1)} %collective-permute-done.1.refs_2_), channel_id=1, source_target_pairs={{0,1},{1,0},{2,3},{3,2},{4,5},{5,4},{6,7},{7,6},{8,9},{9,8},{10,11... | collective-permute-start | bytes 2027528 | tf_op jit(solution)/shard_map/ppermute | solution.py:267
  36.7 2.6 %collective-permute-start = (bf16[40,4224]{1,0:T(8,128)(2,1)S(1)}, bf16[40,4224]{1,0:T(8,128)(2,1)S(1)}, u32[]{:S(2)}, u32[]{:S(2)}) collective-permute-start(bf16[40,4224]{1,0:T(8,128)(2,1)S(1)} %get-tuple-element.117), channel_id=1, source_target_pairs={{0,1},{1,0},{2,3},{3,2},{4,5},{5,4},{6,7},{7,6},{8,9},{9,8},{10,11... | collective-permute-start | bytes 1013768 | tf_op jit(solution)/shard_map/ppermute | solution.py:267
  37.2 17.2 %collective-permute-start.10 = (bf16[80,4224]{1,0:T(8,128)(2,1)S(1)}, bf16[80,4224]{1,0:T(8,128)(2,1)S(1)}, u32[]{:S(2)}, u32[]{:S(2)}) collective-permute-start(bf16[80,4224]{1,0:T(8,128)(2,1)S(1)} %get-tuple-element.139), channel_id=1, source_target_pairs={{0,2},{1,3},{2,0},{3,1},{4,6},{5,7},{6,4},{7,5},{8,10},{9,11},{10,... | collective-permute-start | bytes 2027528 | tf_op jit(solution)/shard_map/ppermute | solution.py:267
  39.3 9.2 %collective-permute-start.9 = (bf16[40,4224]{1,0:T(8,128)(2,1)S(1)}, bf16[40,4224]{1,0:T(8,128)(2,1)S(1)}, u32[]{:S(2)}, u32[]{:S(2)}) collective-permute-start(bf16[40,4224]{1,0:T(8,128)(2,1)S(1)} %get-tuple-element.138), channel_id=1, source_target_pairs={{0,1},{1,0},{2,3},{3,2},{4,5},{5,4},{6,7},{7,6},{8,9},{9,8},{10,11... | collective-permute-start | bytes 1013768 | tf_op jit(solution)/shard_map/ppermute | solution.py:267
  60.4 2.2 %collective-permute-start.14 = (bf16[80,4224]{1,0:T(8,128)(2,1)S(1)}, bf16[80,4224]{1,0:T(8,128)(2,1)S(1)}, u32[]{:S(2)}, u32[]{:S(2)}) collective-permute-start(bf16[80,4224]{1,0:T(8,128)(2,1)S(1)} %collective-permute-done.10.refs_2_.refs_6_), channel_id=1, source_target_pairs={{0,1},{1,0},{2,3},{3,2},{4,5},{5,4},{6,7},{7,6},{8,9},{9,8},{10,11... | collective-permute-start | bytes 2027528 | tf_op jit(solution)/shard_map/ppermute | solution.py:267
  60.5 17.6 %collective-permute-start.13 = (bf16[80,4224]{1,0:T(8,128)(2,1)S(1)}, bf16[80,4224]{1,0:T(8,128)(2,1)S(1)}, u32[]{:S(2)}, u32[]{:S(2)}) collective-permute-start(bf16[80,4224]{1,0:T(8,128)(2,1)S(1)} %get-tuple-element.146), channel_id=1, source_target_pairs={{0,2},{1,3},{2,0},{3,1},{4,6},{5,7},{6,4},{7,5},{8,10},{9,11},{10,... | collective-permute-start | bytes 2027528 | tf_op jit(solution)/shard_map/ppermute | solution.py:267
  62.1 25.9 %collective-permute-start.11 = (bf16[128,4224]{1,0:T(8,128)(2,1)S(1)}, bf16[128,4224]{1,0:T(8,128)(2,1)S(1)}, u32[]{:S(2)}, u32[]{:S(2)}) collective-permute-start(bf16[128,4224]{1,0:T(8,128)(2,1)S(1)} %collective-permute-done.7.refs_1_), channel_id=1, source_target_pairs={{0,4},{1,5},{2,6},{3,7},{4,0},{5,1},{6,2},{7,3},{8,12},{9,13},{10,... | collective-permute-start | bytes 3244040 | tf_op jit(solution)/shard_map/ppermute | solution.py:267
  78.1 2.6 %collective-permute-start.15 = (bf16[80,4224]{1,0:T(8,128)(2,1)S(1)}, bf16[80,4224]{1,0:T(8,128)(2,1)S(1)}, u32[]{:S(2)}, u32[]{:S(2)}) collective-permute-start(bf16[80,4224]{1,0:T(8,128)(2,1)S(1)} %collective-permute-done.13.refs_2_.refs_10_), channel_id=1, source_target_pairs={{0,1},{1,0},{2,3},{3,2},{4,5},{5,4},{6,7},{7,6},{8,9},{9,8},{10,11... | collective-permute-start | bytes 2027528 | tf_op jit(solution)/shard_map/ppermute | solution.py:267
  78.1 2.6 %collective-permute-start.12 = (bf16[40,4224]{1,0:T(8,128)(2,1)S(1)}, bf16[40,4224]{1,0:T(8,128)(2,1)S(1)}, u32[]{:S(2)}, u32[]{:S(2)}) collective-permute-start(bf16[40,4224]{1,0:T(8,128)(2,1)S(1)} %get-tuple-element.145), channel_id=1, source_target_pairs={{0,1},{1,0},{2,3},{3,2},{4,5},{5,4},{6,7},{7,6},{8,9},{9,8},{10,11... | collective-permute-start | bytes 1013768 | tf_op jit(solution)/shard_map/ppermute | solution.py:267
  86.0 11.1 %collective-permute-start.19 = (bf16[80,2176]{1,0:T(8,128)(2,1)S(1)}, bf16[80,2176]{1,0:T(8,128)(2,1)S(1)}, u32[]{:S(2)}, u32[]{:S(2)}) collective-permute-start(bf16[80,2176]{1,0:T(8,128)(2,1)S(1)} %get-tuple-element.166), channel_id=1, source_target_pairs={{0,2},{1,3},{2,0},{3,1},{4,6},{5,7},{6,4},{7,5},{8,10},{9,11},{10,... | collective-permute-start | bytes 1044488 | tf_op jit(solution)/shard_map/ppermute | solution.py:267
  90.2 20.6 %collective-permute-start.17 = (bf16[80,4224]{1,0:T(8,128)(2,1)S(1)}, bf16[80,4224]{1,0:T(8,128)(2,1)S(1)}, u32[]{:S(2)}, u32[]{:S(2)}) collective-permute-start(bf16[80,4224]{1,0:T(8,128)(2,1)S(1)} %get-tuple-element.162), channel_id=1, source_target_pairs={{0,2},{1,3},{2,0},{3,1},{4,6},{5,7},{6,4},{7,5},{8,10},{9,11},{10,... | collective-permute-start | bytes 2027528 | tf_op jit(solution)/shard_map/ppermute | solution.py:267
  97.1 1.9 %collective-permute-start.20 = (bf16[80,2176]{1,0:T(8,128)(2,1)S(1)}, bf16[80,2176]{1,0:T(8,128)(2,1)S(1)}, u32[]{:S(2)}, u32[]{:S(2)}) collective-permute-start(bf16[80,2176]{1,0:T(8,128)(2,1)S(1)} %collective-permute-done.19.refs_4_), channel_id=1, source_target_pairs={{0,1},{1,0},{2,3},{3,2},{4,5},{5,4},{6,7},{7,6},{8,9},{9,8},{10,11... | collective-permute-start | bytes 1044488 | tf_op jit(solution)/shard_map/ppermute | solution.py:267
  97.1 1.9 %collective-permute-start.18 = (bf16[40,2176]{1,0:T(8,128)(2,1)S(1)}, bf16[40,2176]{1,0:T(8,128)(2,1)S(1)}, u32[]{:S(2)}, u32[]{:S(2)}) collective-permute-start(bf16[40,2176]{1,0:T(8,128)(2,1)S(1)} %get-tuple-element.165), channel_id=1, source_target_pairs={{0,1},{1,0},{2,3},{3,2},{4,5},{5,4},{6,7},{7,6},{8,9},{9,8},{10,11... | collective-permute-start | bytes 522248 | tf_op jit(solution)/shard_map/ppermute | solution.py:267
  100.1 7.6 %collective-permute-start.21 = (bf16[128,640]{1,0:T(8,128)(2,1)S(1)}, bf16[128,640]{1,0:T(8,128)(2,1)S(1)}, u32[]{:S(2)}, u32[]{:S(2)}) collective-permute-start(bf16[128,640]{1,0:T(8,128)(2,1)S(1)} %get-tuple-element.170), channel_id=1, source_target_pairs={{0,8},{1,9},{2,10},{3,11},{4,12},{5,13},{6,14},{7,15},{8,0},{9,1},... | collective-permute-start | bytes 491528 | tf_op jit(solution)/shard_map/ppermute | solution.py:267
  110.8 3.2 %collective-permute-start.22 = (bf16[80,4224]{1,0:T(8,128)(2,1)S(1)}, bf16[80,4224]{1,0:T(8,128)(2,1)S(1)}, u32[]{:S(2)}, u32[]{:S(2)}) collective-permute-start(bf16[80,4224]{1,0:T(8,128)(2,1)S(1)} %collective-permute-done.17.refs_2_.refs_14_), channel_id=1, source_target_pairs={{0,1},{1,0},{2,3},{3,2},{4,5},{5,4},{6,7},{7,6},{8,9},{9,8},{10,11... | collective-permute-start | bytes 2027528 | tf_op jit(solution)/shard_map/ppermute | solution.py:267
  110.8 10.6 %collective-permute-start.27 = (bf16[80,2176]{1,0:T(8,128)(2,1)S(1)}, bf16[80,2176]{1,0:T(8,128)(2,1)S(1)}, u32[]{:S(2)}, u32[]{:S(2)}) collective-permute-start(bf16[80,2176]{1,0:T(8,128)(2,1)S(1)} %get-tuple-element.182), channel_id=1, source_target_pairs={{0,2},{1,3},{2,0},{3,1},{4,6},{5,7},{6,4},{7,5},{8,10},{9,11},{10,... | collective-permute-start | bytes 1044488 | tf_op jit(solution)/shard_map/ppermute | solution.py:267
  112.3 1.6 %collective-permute-start.16 = (bf16[40,4224]{1,0:T(8,128)(2,1)S(1)}, bf16[40,4224]{1,0:T(8,128)(2,1)S(1)}, u32[]{:S(2)}, u32[]{:S(2)}) collective-permute-start(bf16[40,4224]{1,0:T(8,128)(2,1)S(1)} %get-tuple-element.161), channel_id=1, source_target_pairs={{0,1},{1,0},{2,3},{3,2},{4,5},{5,4},{6,7},{7,6},{8,9},{9,8},{10,11... | collective-permute-start | bytes 1013768 | tf_op jit(solution)/shard_map/ppermute | solution.py:267
  112.5 17.7 %collective-permute-start.25 = (bf16[128,1536]{1,0:T(8,128)(2,1)S(1)}, bf16[128,1536]{1,0:T(8,128)(2,1)S(1)}, u32[]{:S(2)}, u32[]{:S(2)}) collective-permute-start(bf16[128,1536]{1,0:T(8,128)(2,1)S(1)} %get-tuple-element.178), channel_id=1, source_target_pairs={{0,8},{1,9},{2,10},{3,11},{4,12},{5,13},{6,14},{7,15},{8,0},{9,1},... | collective-permute-start | bytes 1179656 | tf_op jit(solution)/shard_map/ppermute | solution.py:267
  121.3 2.9 %collective-permute-start.28 = (bf16[80,2176]{1,0:T(8,128)(2,1)S(1)}, bf16[80,2176]{1,0:T(8,128)(2,1)S(1)}, u32[]{:S(2)}, u32[]{:S(2)}) collective-permute-start(bf16[80,2176]{1,0:T(8,128)(2,1)S(1)} %collective-permute-done.27.refs_4_), channel_id=1, source_target_pairs={{0,1},{1,0},{2,3},{3,2},{4,5},{5,4},{6,7},{7,6},{8,9},{9,8},{10,11... | collective-permute-start | bytes 1044488 | tf_op jit(solution)/shard_map/ppermute | solution.py:267
  121.3 10.6 %collective-permute-start.24 = (bf16[80,2176]{1,0:T(8,128)(2,1)S(1)}, bf16[80,2176]{1,0:T(8,128)(2,1)S(1)}, u32[]{:S(2)}, u32[]{:S(2)}) collective-permute-start(bf16[80,2176]{1,0:T(8,128)(2,1)S(1)} %get-tuple-element.177), channel_id=1, source_target_pairs={{0,2},{1,3},{2,0},{3,1},{4,6},{5,7},{6,4},{7,5},{8,10},{9,11},{10,... | collective-permute-start | bytes 1044488 | tf_op jit(solution)/shard_map/ppermute | solution.py:267
  131.9 2.7 %collective-permute-start.29 = (bf16[80,2176]{1,0:T(8,128)(2,1)S(1)}, bf16[80,2176]{1,0:T(8,128)(2,1)S(1)}, u32[]{:S(2)}, u32[]{:S(2)}) collective-permute-start(bf16[80,2176]{1,0:T(8,128)(2,1)S(1)} %collective-permute-done.24.refs_4_), channel_id=1, source_target_pairs={{0,1},{1,0},{2,3},{3,2},{4,5},{5,4},{6,7},{7,6},{8,9},{9,8},{10,11... | collective-permute-start | bytes 1044488 | tf_op jit(solution)/shard_map/ppermute | solution.py:267
  131.9 2.7 %collective-permute-start.23 = (bf16[40,2176]{1,0:T(8,128)(2,1)S(1)}, bf16[40,2176]{1,0:T(8,128)(2,1)S(1)}, u32[]{:S(2)}, u32[]{:S(2)}) collective-permute-start(bf16[40,2176]{1,0:T(8,128)(2,1)S(1)} %get-tuple-element.176), channel_id=1, source_target_pairs={{0,1},{1,0},{2,3},{3,2},{4,5},{5,4},{6,7},{7,6},{8,9},{9,8},{10,11... | collective-permute-start | bytes 522248 | tf_op jit(solution)/shard_map/ppermute | solution.py:267
  132.4 10.1 %collective-permute-start.6 = (bf16[80,2176]{1,0:T(8,128)(2,1)S(1)}, bf16[80,2176]{1,0:T(8,128)(2,1)S(1)}, u32[]{:S(2)}, u32[]{:S(2)}) collective-permute-start(bf16[80,2176]{1,0:T(8,128)(2,1)S(1)} %get-tuple-element.135), channel_id=1, source_target_pairs={{0,2},{1,3},{2,0},{3,1},{4,6},{5,7},{6,4},{7,5},{8,10},{9,11},{10,... | collective-permute-start | bytes 1044488 | tf_op jit(solution)/shard_map/ppermute | solution.py:267
  133.9 15.5 %collective-permute-start.31 = (bf16[128,2176]{1,0:T(8,128)(2,1)S(1)}, bf16[128,2176]{1,0:T(8,128)(2,1)S(1)}, u32[]{:S(2)}, u32[]{:S(2)}) collective-permute-start(bf16[128,2176]{1,0:T(8,128)(2,1)S(1)} %get-tuple-element.194), channel_id=1, source_target_pairs={{0,4},{1,5},{2,6},{3,7},{4,0},{5,1},{6,2},{7,3},{8,12},{9,13},{10,... | collective-permute-start | bytes 1671176 | tf_op jit(solution)/shard_map/ppermute | solution.py:267
  135.8 26.0 %collective-permute-start.32 = (bf16[128,2176]{1,0:T(8,128)(2,1)S(1)}, bf16[128,2176]{1,0:T(8,128)(2,1)S(1)}, u32[]{:S(2)}, u32[]{:S(2)}) collective-permute-start(bf16[128,2176]{1,0:T(8,128)(2,1)S(1)} %get-tuple-element.199), channel_id=1, source_target_pairs={{0,12},{1,13},{2,14},{3,15},{4,8},{5,9},{6,10},{7,11},{8,4},{9,5},... | collective-permute-start | bytes 1671176 | tf_op jit(solution)/shard_map/ppermute | solution.py:267
  142.5 1.9 %collective-permute-start.30 = (bf16[80,2176]{1,0:T(8,128)(2,1)S(1)}, bf16[80,2176]{1,0:T(8,128)(2,1)S(1)}, u32[]{:S(2)}, u32[]{:S(2)}) collective-permute-start(bf16[80,2176]{1,0:T(8,128)(2,1)S(1)} %collective-permute-done.6.refs_4_), channel_id=1, source_target_pairs={{0,1},{1,0},{2,3},{3,2},{4,5},{5,4},{6,7},{7,6},{8,9},{9,8},{10,11... | collective-permute-start | bytes 1044488 | tf_op jit(solution)/shard_map/ppermute | solution.py:267
  142.5 1.9 %collective-permute-start.5 = (bf16[40,2176]{1,0:T(8,128)(2,1)S(1)}, bf16[40,2176]{1,0:T(8,128)(2,1)S(1)}, u32[]{:S(2)}, u32[]{:S(2)}) collective-permute-start(bf16[40,2176]{1,0:T(8,128)(2,1)S(1)} %get-tuple-element.134), channel_id=1, source_target_pairs={{0,1},{1,0},{2,3},{3,2},{4,5},{5,4},{6,7},{7,6},{8,9},{9,8},{10,11... | collective-permute-start | bytes 522248 | tf_op jit(solution)/shard_map/ppermute | solution.py:267
  (12 other events, 51.0 us)

commit v4 on v3

--- a/solution.py
+++ b/solution.py
@@ -33,21 +33,27 @@
     return pl.BlockSpec(memory_space=pltpu.SMEM)
 
 
-def one_hots(names, slots, side, routes):
+def one_hots(names, half, rows, side, routes):
     turned = side.T
     tokens = side.shape[0]
     earlier = lax.broadcasted_iota(jnp.int32, (tokens, tokens), 0)
     later = lax.broadcasted_iota(jnp.int32, (tokens, tokens), 1)
     ahead = jnp.where(earlier < later, 1.0, 0.0).astype(BF16)
-    place = lax.broadcasted_iota(jnp.int32, (slots, tokens), 0).astype(F32)
+    place = lax.broadcasted_iota(jnp.int32, (rows, tokens), 0)
+    every = [[jnp.where(turned[k : k + 1, :] == name, 1.0, 0.0) for k in range(routes)] for name in names]
     found = []
-    for name in names:
-        hits = [jnp.where(turned[k : k + 1, :] == name, 1.0, 0.0) for k in range(routes)]
+    for n, hits in enumerate(every):
         member = sum(hits)
         wide = jnp.broadcast_to(member, (8, tokens)).astype(BF16)
-        slot = nn(wide, ahead)[0:1, :]
-        found.append((jnp.where((place == slot) & (member > 0.0), 1.0, 0.0), hits))
-    return turned, found
+        slot = nn(wide, ahead)[0:1, :].astype(jnp.int32) + half * (n % 2)
+        found.append(jnp.where((place == slot) & (member > 0.0), 1.0, 0.0))
+    return turned, every, [found[n] + found[n + 1] for n in range(0, len(names), 2)]
+
+
+def joined(refs, half, low, high):
+    first = lax.broadcasted_iota(jnp.int32, (refs[0].shape[0], 1), 0) < half
+    pieces = [r[:, low:high].astype(F32) for r in refs]
+    return jnp.concatenate([jnp.where(first, pieces[n], pieces[n + 1]) for n in range(0, len(refs), 2)], axis=0)
 
 
 def pack_kernel(routes, x_ref, grad_ref, ids_ref, weight_ref, out_ref, ids_buf, weight_buf, sems):
@@ -71,7 +77,7 @@
     copies[1].wait()
 
 
-def select_kernel(routes, slots, choices, stage, info_ref, *refs):
+def select_kernel(routes, half, choices, stage, info_ref, *refs):
     blocks, outs, side_ref = refs[:choices], refs[choices:-1], refs[-1]
     block = blocks[0]
     for i in range(1, choices):
@@ -84,26 +90,21 @@
     side_ref[...] = block[:, 2 * width :]
     side = block[:, 2 * width :].astype(F32)
     names = [info_ref[m].astype(F32) + 1.0 for m in range(PLANE)]
-    turned, found = one_hots(names, slots, side, routes)
-    lane = lax.broadcasted_iota(jnp.int32, (slots, LANES), 1)
-    picks = jnp.concatenate([hot for hot, _ in found], axis=0).astype(BF16)
-    chosen = nn(picks, block[:, : 2 * width])
-    tails = []
-    for hot, hits in found:
+    turned, every, hots = one_hots(names, half, outs[0].shape[0], side, routes)
+    lane = lax.broadcasted_iota(jnp.int32, (outs[0].shape[0], LANES), 1)
+    chosen = nn(jnp.concatenate(hots, axis=0).astype(BF16), block[:, : 2 * width])
+    rows = outs[0].shape[0]
+    first = lax.broadcasted_iota(jnp.int32, (rows, 1), 0) < half
+    for n, (hot, out) in enumerate(zip(hots, outs)):
         parts = []
         for group in (2, 3):
-            weight = sum(hits[k] * turned[group * routes + k : group * routes + k + 1, :] for k in range(routes))
-            parts.append(jnp.sum(hot * weight, axis=1, keepdims=True))
-        tails.append(jnp.where(lane == 0, parts[0], jnp.where(lane == 1, parts[1], 0.0)))
-    for out, low, high in ((outs[0], 0, 1), (outs[1], 1, 2), (outs[2], 2, 4)):
-        out[:, : 2 * width] = chosen[low * slots : high * slots].astype(BF16)
-        out[:, 2 * width :] = jnp.concatenate(tails[low:high], axis=0).astype(BF16)
-
-
-def stacked(refs, low, high):
-    own, near, across, around = (r[:, low:high].astype(F32) for r in refs)
-    half = own.shape[0]
-    return jnp.concatenate([own, near, across[:half], around[half:]], axis=0)
+            weights = [
+                sum(hits[k] * turned[group * routes + k : group * routes + k + 1, :] for k in range(routes))
+                for hits in every[2 * n : 2 * n + 2]
+            ]
+            parts.append(jnp.sum(hot * jnp.where(first, weights[0], weights[1]), axis=1, keepdims=True))
+        out[:, : 2 * width] = chosen[n * rows : (n + 1) * rows].astype(BF16)
+        out[:, 2 * width :] = jnp.where(lane == 0, parts[0], jnp.where(lane == 1, parts[1], 0.0)).astype(BF16)
 
 
 def prepare_kernel(gate_a, gate_b, up_a, up_b, down_a, down_b, *refs):
@@ -128,14 +129,14 @@
     last_t[...] = padded(down_b[...]).T.astype(BF16)
 
 
-def expert_kernel(routes, slots, *refs):
+def expert_kernel(routes, half, *refs):
     rows_in = refs[:PLANE]
     in_t, in_s, back_t, out_s, down_t, down_s, last_t, gate_w, up_w, down_w = refs[PLANE : PLANE + 10]
     *outs, acts_ref, lows_ref = refs[PLANE + 10 :]
     width, hidden_units = gate_w.shape
-    x = stacked(rows_in, 0, width).astype(BF16)
-    g = stacked(rows_in, width, 2 * width).astype(BF16)
-    side = stacked(rows_in, 2 * width, 2 * width + LANES)
+    x = joined(rows_in, half, 0, width).astype(BF16)
+    g = joined(rows_in, half, width, 2 * width).astype(BF16)
+    side = joined(rows_in, half, 2 * width, 2 * width + LANES)
     weight = side[:, 0:1] + side[:, 1:2]
 
     low = nn(x, in_t[...]).astype(BF16)
@@ -156,11 +157,12 @@
     back = (nn(gate_grad, back_t[0]) + nn(up_grad, back_t[1])).astype(BF16)
     input_grad = nt(gate_grad, gate_w[...]) + nt(up_grad, up_w[...]) + SCALE * nn(back, in_s[...])
     high, lesser = two_parts(dots)
-    lane = lax.broadcasted_iota(jnp.int32, (PLANE * slots, LANES), 1)
+    lane = lax.broadcasted_iota(jnp.int32, (x.shape[0], LANES), 1)
     side_back = jnp.where(lane < routes, high, jnp.where(lane < 2 * routes, lesser, 0.0))
-    for out, first, end in ((outs[0], 0, 1), (outs[1], 1, 2), (outs[2], 2, 4)):
-        out[:, :width] = input_grad[first * slots : end * slots].astype(BF16)
-        out[:, width:] = side_back[first * slots : end * slots].astype(BF16)
+    rows = x.shape[0] // 2
+    for n, out in enumerate(outs):
+        out[:, :width] = input_grad[n * rows : (n + 1) * rows].astype(BF16)
+        out[:, width:] = side_back[n * rows : (n + 1) * rows].astype(BF16)
     acts_ref[:, :hidden_units] = hidden
     acts_ref[:, hidden_units : 2 * hidden_units] = gate_grad
     acts_ref[:, 2 * hidden_units :] = up_grad
@@ -168,20 +170,23 @@
         lows_ref[:, n * LANES : (n + 1) * LANES] = value
 
 
-def combine_kernel(routes, slots, info_ref, side_ref, *refs):
+def combine_kernel(routes, half, info_ref, side_ref, *refs):
     backs, outs = refs[:PLANE], refs[PLANE:]
     width = backs[0].shape[1] - LANES
     side = side_ref[...].astype(F32)
     names = [info_ref[m].astype(F32) + 1.0 for m in range(PLANE)]
-    _, found = one_hots(names, slots, side, routes)
-    tails = stacked(backs, width, width + LANES).astype(BF16)
+    count = backs[0].shape[0]
+    _, _, hots = one_hots(names, half, count, side, routes)
+    tails = joined(backs, half, width, width + LANES).astype(BF16)
     extra = jnp.zeros((side.shape[0], LANES), F32)
+    first = lax.broadcasted_iota(jnp.int32, (count, 1), 0) < half
     for m in range(PLANE):
-        hot = jnp.concatenate([h if n == m else jnp.zeros_like(h) for n, (h, _) in enumerate(found)], axis=0)
-        spread = lax.dot_general(hot.astype(BF16), tails, (((0,), (0,)), ((), ())), preferred_element_type=F32)
+        hot = jnp.where(first if m % 2 == 0 else ~first, hots[m // 2], 0.0).astype(BF16)
+        part = tails[m // 2 * count : (m // 2 + 1) * count]
+        spread = lax.dot_general(hot, part, (((0,), (0,)), ((), ())), preferred_element_type=F32)
         extra = extra + jnp.where(side == names[m], spread, 0.0)
-    picks = jnp.concatenate([hot for hot, _ in found], axis=0).astype(BF16)
-    rows = stacked(backs, 0, width).astype(BF16)
+    picks = jnp.concatenate(hots, axis=0).astype(BF16)
+    rows = joined(backs, half, 0, width).astype(BF16)
     total = lax.dot_general(picks, rows, (((0,), (0,)), ((), ())), preferred_element_type=F32)
     low = 0
     for out in outs:
@@ -210,7 +215,7 @@
     combine_ref[...] = side[:routes] + side[routes : 2 * routes]
 
 
-def adapter_kernel(stages, rank, *refs):
+def adapter_kernel(stages, half, rank, *refs):
     rows_in, refs = refs[: stages * PLANE], refs[stages * PLANE :]
     acts, lows, outs = refs[:stages], refs[stages : 2 * stages], refs[2 * stages :]
     width, hidden_units = outs[0].shape[2], outs[1].shape[2]
@@ -219,7 +224,7 @@
         return SCALE * lax.dot_general(part, other, (((0,), (0,)), ((), ())), preferred_element_type=F32)
 
     def every(low, high):
-        pieces = [stacked(rows_in[n * PLANE : (n + 1) * PLANE], low, high) for n in range(stages)]
+        pieces = [joined(rows_in[n * PLANE : (n + 1) * PLANE], half, low, high) for n in range(stages)]
         return jnp.concatenate(pieces, axis=0).astype(BF16)
 
     parts = [jnp.concatenate([r[:, n * LANES : (n + 1) * LANES] for r in lows], axis=0) for n in range(4)]
@@ -239,7 +244,7 @@
     experts = lax.axis_size("expert")
     planes = experts // PLANE
     capacity = rows * routes * 9 // (8 * experts)
-    slots = -(-capacity // 8) * 8
+    pair = -(-2 * capacity // 8) * 8
     matrices = [w[0] for w in weights]
     hidden_units = matrices[0].shape[1]
     rank = matrices[3].shape[0]
@@ -307,9 +312,9 @@
 
     def expert(got):
         return kernel(
-            functools.partial(expert_kernel, routes, slots),
-            [shape((n * slots, wide), BF16) for n in (1, 1, 2)]
-            + [shape((PLANE * slots, 3 * hidden_units), BF16), shape((PLANE * slots, 4 * LANES), BF16)],
+            functools.partial(expert_kernel, routes, capacity),
+            [shape((pair, wide), BF16)] * 2
+            + [shape((2 * pair, 3 * hidden_units), BF16), shape((2 * pair, 4 * LANES), BF16)],
             (*got, *adapters, *matrices[:3]),
             8,
             "expert",
@@ -322,17 +327,17 @@
 
     rows_of, sides, parts, acts, lows = {}, {}, {}, {}, {}
 
-    def halfway(own, near, far):
-        return own, flipped(near, 1), flipped(far, 2)
-
-    def arrived(own, near, across):
+    def halfway(home, away):
+        return home, flipped(home, 1), flipped(away, 2)
+
+    def arrived(home, near, across):
         (across,) = together(across)
-        return own, near, across, flipped(across, 1)
+        return home, near, across, flipped(across, 1)
 
     def begin(stage, *found):
         *picked, sides[stage] = kernel(
-            functools.partial(select_kernel, routes, slots, len(found), stage),
-            [shape((n * slots, 2 * width + LANES), BF16) for n in (1, 1, 2)] + [shape((rows, LANES), BF16)],
+            functools.partial(select_kernel, routes, capacity, len(found), stage),
+            [shape((pair, 2 * width + LANES), BF16)] * 2 + [shape((rows, LANES), BF16)],
             (info, *found),
             4,
             "select",
@@ -348,7 +353,7 @@
 
     def end_of(stage, *columns):
         found = kernel(
-            functools.partial(combine_kernel, routes, slots),
+            functools.partial(combine_kernel, routes, capacity),
             [shape((rows, c), BF16) for c in columns or (wide,)],
             (info, sides[stage], *arrived(*parts[stage])),
             3,
@@ -381,6 +386,17 @@
             8,
         )
 
+    def adapter_sums():
+        order = sorted(rows_of)
+        return kernel(
+            functools.partial(adapter_kernel, len(order), capacity, rank),
+            [shape((1, rank, n), F32) for n in (width, hidden_units, width, hidden_units, hidden_units, width)],
+            (*(r for n in order for r in rows_of[n]), *(acts[n] for n in order), *(lows[n] for n in order)),
+            5,
+            "adapter_grads",
+            24,
+        )
+
     if planes == 4:
         mids = (1, 2)
         mate, across = flipped(packed, PLANE), flipped(packed, 3 * PLANE, mids)
@@ -397,12 +413,14 @@
         middle_of(2)
         (farthest,) = together(farthest)
         begin(3, across, farthest)
-        end_of(2, 640, wide - 640)
+        first = width * 5 // (16 * LANES) * LANES
+        end_of(2, first, wide - first)
         (parts[2][0],) = together(parts[2][0])
         middle_of(3)
         end_of(1)
         (parts[2][1],) = together(parts[2][1])
         end_of(3)
+        grads = adapter_sums()
         end_of(0)
     else:
         blocks = {0: packed}
@@ -414,17 +432,10 @@
             begin(stage, *(blocks[o] for o in offsets[stage]))
             middle_of(stage)
             end_of(stage)
+        grads = adapter_sums()
     order = sorted(rows_of)
     total = add(*(part for n in order[:-1] for part in parts[n]))
 
-    grads = kernel(
-        functools.partial(adapter_kernel, len(order), rank),
-        [shape((1, rank, n), F32) for n in (width, hidden_units, width, hidden_units, hidden_units, width)],
-        (*(r for n in order for r in rows_of[n]), *(acts[n] for n in order), *(lows[n] for n in order)),
-        5,
-        "adapter_grads",
-        24,
-    )
     grad_tokens, grad_combine = kernel(
         functools.partial(finish_kernel, routes),
         [shape((rows, width), BF16), shape((routes, rows), F32)],

time: 165 us -> 161 us (0.976)
  waiting for transfers between devices: 88.3 us -> 84.3 us
    ppermute x33, waiting for transfers between devices: 88.3 us -> 84.3 us  [flipped(): return lax.ppermute(value, 'expert', pairs)]
  transfers between devices with their start and end apart: 33 -> 33, of which waited for: 23 -> 20; matrix products, arithmetic and copies ran while one was open for 0% -> 0% of each run, Pallas kernels for 21% -> 21%
where the time goes in v4:
time: 161 us; the launch traced here: 159 us
  waiting for transfers between devices  84.3 us (52%)
  Pallas kernels  38.2 us (24%)
  starting transfers between devices  24.9 us (15%)
  local copies, waits for them, and re-layouts  10.9 us (7%)
    ppermute x33, waiting for transfers between devices, flipped(): return lax.ppermute(value, 'expert', pairs)  84.3 us
    pallas_call x17, Pallas kernels, kernel(): pl.pallas_call(run, out_shape=[*outs, shape((8, LANES), F32)], in_specs=[...  38.2 us
    ppermute x33, starting transfers between devices, flipped(): return lax.ppermute(value, 'expert', pairs)  24.9 us
    unnamed x22, local copies, waits for them, and re-layouts  10.8 us
  transfers between devices with their start and end apart: 33, of which 20 were waited for; matrix products, arithmetic and copies ran while one was open for 0% of the time, Pallas kernels for 21%

profile of v4, /device:TPU:16, one launch (start us, length us, event | category | flops | bytes accessed | tf_op | source)
XLA Modules:
  0.0 159.2 jit_solution(11412563347783127862)
XLA Ops:
  0.6 2.4 %pack.1 = (bf16[128,4224]{1,0:T(8,128)(2,1)}, f32[8,128]{1,0:T(8,128)}) custom-call(bf16[128,2048]{1,0:T(8,128)(2,1)} %refs_0_.1, bf16[128,2048]{1,0:T(8,128)(2,1)} %refs_1_.1, s32[4,128]{1,0:T(4,128)} %bitcast.35, f32[4,128]{1,0:T(4,128)} %bitcast.36), custom_call_target="tpu_custom_call" | custom-call | flops 1 | bytes 6000000 | tf_op jit(solution)/shard_map/pack/pallas_call | solution.py:282
  3.1 1.6 %collective-permute-start.2 = (bf16[128,4224]{1,0:T(8,128)(2,1)}, bf16[128,4224]{1,0:T(8,128)(2,1)}, u32[]{:S(2)}, u32[]{:S(2)}) collective-permute-start(bf16[128,4224]{1,0:T(8,128)(2,1)} %get-tuple-element.105.refs_1_), channel_id=1, source_target_pairs={{0,4},{1,5},{2,6},{3,7},{4,0},{5,1},{6,2},{7,3},{8,12},{9,13},{10,... | collective-permute-start | bytes 3244040 | tf_op jit(solution)/shard_map/ppermute | solution.py:272
  4.7 1.9 %collective-permute-start.3 = (bf16[128,4224]{1,0:T(8,128)(2,1)}, bf16[128,4224]{1,0:T(8,128)(2,1)}, u32[]{:S(2)}, u32[]{:S(2)}) collective-permute-start(bf16[128,4224]{1,0:T(8,128)(2,1)} %get-tuple-element.105.refs_1_), channel_id=1, source_target_pairs={{4,8},{5,9},{6,10},{7,11},{8,4},{9,5},{10,6},{11,7},{20,24},{21,25... | collective-permute-start | bytes 3244040 | tf_op jit(solution)/shard_map/ppermute | solution.py:272
  9.9 1.6 collective-permute-start.1
  17.1 12.0 %collective-permute-done.2.refs_1_ = bf16[128,4224]{1,0:T(8,128)(2,1)} collective-permute-done((bf16[128,4224]{1,0:T(8,128)(2,1)}, bf16[128,4224]{1,0:T(8,128)(2,1)}, u32[]{:S(2)}, u32[]{:S(2)}) %collective-permute-start.2) | collective-permute-done | bytes 1081376 | tf_op jit(solution)/shard_map/ppermute | solution.py:272
  29.1 3.2 %collective-permute-done.3.refs_1_ = bf16[128,4224]{1,0:T(8,128)(2,1)} collective-permute-done((bf16[128,4224]{1,0:T(8,128)(2,1)}, bf16[128,4224]{1,0:T(8,128)(2,1)}, u32[]{:S(2)}, u32[]{:S(2)}) %collective-permute-start.3) | collective-permute-done | bytes 1081376 | tf_op jit(solution)/shard_map/ppermute | solution.py:272
  32.2 2.2 %collective-permute-start.7 = (bf16[128,4224]{1,0:T(8,128)(2,1)}, bf16[128,4224]{1,0:T(8,128)(2,1)S(1)}, u32[]{:S(2)}, u32[]{:S(2)}) collective-permute-start(bf16[128,4224]{1,0:T(8,128)(2,1)} %collective-permute-done.2.refs_1_), channel_id=1, source_target_pairs={{4,8},{5,9},{6,10},{7,11},{8,4},{9,5},{10,6},{11,7},{20,24},{21,25... | collective-permute-start | bytes 3244040 | tf_op jit(solution)/shard_map/ppermute | solution.py:272
  34.5 1.9 %select.11 = (bf16[72,4224]{1,0:T(8,128)(2,1)S(1)}, bf16[72,4224]{1,0:T(8,128)(2,1)S(1)}, bf16[128,128]{1,0:T(8,128)(2,1)S(1)}, f32[8,128]{1,0:T(8,128)S(1)}) custom-call(s32[8]{0:T(128)S(1)} %stack.28.refs_0_, bf16[128,4224]{1,0:T(8,128)(2,1)} %collective-permute-done.2.refs_1_, f32[8,128]{1,0:T(8,128)S(1)} %get-tuple-element.113.refs_2_), custom_call_target="tpu_custom_call" | custom-call | flops 1 | bytes 12000000 | tf_op jit(solution)/shard_map/select/pallas_call | solution.py:282
  38.5 1.9 %copy-done.1 = bf16[1,2048,768]{2,1,0:T(8,128)(2,1)S(1)} copy-done((bf16[1,2048,768]{2,1,0:T(8,128)(2,1)S(1)}, bf16[1,2048,768]{2,1,0:T(8,128)(2,1)}, u32[]{:S(2)}) %copy-start.1) | copy-done | bytes 3145752
  40.4 1.9 %copy-done.2 = bf16[1,768,2048]{2,1,0:T(8,128)(2,1)S(1)} copy-done((bf16[1,768,2048]{2,1,0:T(8,128)(2,1)S(1)}, bf16[1,768,2048]{2,1,0:T(8,128)(2,1)}, u32[]{:S(2)}) %copy-start.2) | copy-done | bytes 3145752
  42.3 5.1 %expert.4 = (bf16[72,2176]{1,0:T(8,128)(2,1)S(1)}, bf16[72,2176]{1,0:T(8,128)(2,1)S(1)}, bf16[144,2304]{1,0:T(8,128)(2,1)S(1)}, bf16[144,512]{1,0:T(8,128)(2,1)S(1)}, f32[8,128]{1,0:T(8,128)S(1)}) custom-call(bf16[72,4224]{1,0:T(8,128)(2,1)S(1)} %get-tuple-element.108.refs_0_, bf16[72,4224]{1,0:T(8,128)(2,1)S(1)} %collective-permute-done.refs_1_, ...), custom_call_target="tpu_custom_call" | custom-call | flops 1 | bytes 24000000 | tf_op jit(solution)/shard_map/expert/pallas_call | solution.py:282
  47.5 5.2 %collective-permute-done.10.refs_2_.refs_6_ = bf16[72,4224]{1,0:T(8,128)(2,1)S(1)} collective-permute-done((bf16[72,4224]{1,0:T(8,128)(2,1)S(1)}, bf16[72,4224]{1,0:T(8,128)(2,1)S(1)}, u32[]{:S(2)}, u32[]{:S(2)}) %collective-permute-start.10) | collective-permute-done | bytes 608288 | tf_op jit(solution)/shard_map/ppermute | solution.py:272
  52.7 6.1 %collective-permute-done.7.refs_1_ = bf16[128,4224]{1,0:T(8,128)(2,1)S(1)} collective-permute-done((bf16[128,4224]{1,0:T(8,128)(2,1)}, bf16[128,4224]{1,0:T(8,128)(2,1)S(1)}, u32[]{:S(2)}, u32[]{:S(2)}) %collective-permute-start.7) | collective-permute-done | bytes 1081376 | tf_op jit(solution)/shard_map/ppermute | solution.py:272
  62.6 5.2 %expert.5 = (bf16[72,2176]{1,0:T(8,128)(2,1)S(1)}, bf16[72,2176]{1,0:T(8,128)(2,1)S(1)}, bf16[144,2304]{1,0:T(8,128)(2,1)S(1)}, bf16[144,512]{1,0:T(8,128)(2,1)S(1)}, f32[8,128]{1,0:T(8,128)S(1)}) custom-call(bf16[72,4224]{1,0:T(8,128)(2,1)S(1)} %get-tuple-element.130.refs_0_.refs_4_, bf16[72,4224]{1,0:T(8,128)(2,1)S(1)} %collective-permute-done.9.refs_1_.refs_5_, ...), custom_call_target="tpu_custom_call" | custom-call | flops 1 | bytes 24000000 | tf_op jit(solution)/shard_map/expert/pallas_call | solution.py:282
  67.8 9.0 %collective-permute-done.13.refs_2_.refs_10_ = bf16[72,4224]{1,0:T(8,128)(2,1)S(1)} collective-permute-done((bf16[72,4224]{1,0:T(8,128)(2,1)S(1)}, bf16[72,4224]{1,0:T(8,128)(2,1)S(1)}, u32[]{:S(2)}, u32[]{:S(2)}) %collective-permute-start.13) | collective-permute-done | bytes 608288 | tf_op jit(solution)/shard_map/ppermute | solution.py:272
  76.8 2.0 %collective-permute-done.14.refs_3_.refs_11_ = bf16[72,4224]{1,0:T(8,128)(2,1)S(1)} collective-permute-done((bf16[72,4224]{1,0:T(8,128)(2,1)S(1)}, bf16[72,4224]{1,0:T(8,128)(2,1)S(1)}, u32[]{:S(2)}, u32[]{:S(2)}) %collective-permute-start.14) | collective-permute-done | bytes 608288 | tf_op jit(solution)/shard_map/ppermute | solution.py:272
  78.8 5.2 %expert.6 = (bf16[72,2176]{1,0:T(8,128)(2,1)S(1)}, bf16[72,2176]{1,0:T(8,128)(2,1)S(1)}, bf16[144,2304]{1,0:T(8,128)(2,1)S(1)}, bf16[144,512]{1,0:T(8,128)(2,1)S(1)}, f32[8,128]{1,0:T(8,128)S(1)}) custom-call(bf16[72,4224]{1,0:T(8,128)(2,1)S(1)} %get-tuple-element.138.refs_0_.refs_8_, bf16[72,4224]{1,0:T(8,128)(2,1)S(1)} %collective-permute-done.12.refs_1_.refs_9_, ...), custom_call_target="tpu_custom_call" | custom-call | flops 1 | bytes 24000000 | tf_op jit(solution)/shard_map/expert/pallas_call | solution.py:282
  84.0 1.6 collective-permute-start.19
  85.5 2.6 %collective-permute-done.15.refs_2_ = bf16[128,4224]{1,0:T(8,128)(2,1)S(1)} collective-permute-done((bf16[128,4224]{1,0:T(8,128)(2,1)S(1)}, bf16[128,4224]{1,0:T(8,128)(2,1)S(1)}, u32[]{:S(2)}, u32[]{:S(2)}) %collective-permute-start.15) | collective-permute-done | bytes 1081376 | tf_op jit(solution)/shard_map/ppermute | solution.py:272
  88.1 2.1 %select.13 = (bf16[72,4224]{1,0:T(8,128)(2,1)S(1)}, bf16[72,4224]{1,0:T(8,128)(2,1)S(1)}, bf16[128,128]{1,0:T(8,128)(2,1)S(1)}, f32[8,128]{1,0:T(8,128)S(1)}) custom-call(s32[8]{0:T(128)S(1)} %stack.28.refs_0_, bf16[128,4224]{1,0:T(8,128)(2,1)} %collective-permute-done.3.refs_1_, bf16[128,4224]{1,0:T(8,128)(2,1)S(1)} %collective-permute-done.15.refs_2_, ...), custom_call_target="tpu_custom_call" | custom-call | flops 1 | bytes 12000000 | tf_op jit(solution)/shard_map/select/pallas_call | solution.py:282
  90.8 3.4 %collective-permute-done.19.refs_4_ = bf16[72,2176]{1,0:T(8,128)(2,1)S(1)} collective-permute-done((bf16[72,2176]{1,0:T(8,128)(2,1)S(1)}, bf16[72,2176]{1,0:T(8,128)(2,1)S(1)}, u32[]{:S(2)}, u32[]{:S(2)}) %collective-permute-start.19) | collective-permute-done | bytes 313376 | tf_op jit(solution)/shard_map/ppermute | solution.py:272
  94.3 1.6 %collective-permute-done.20.refs_5_ = bf16[72,2176]{1,0:T(8,128)(2,1)S(1)} collective-permute-done((bf16[72,2176]{1,0:T(8,128)(2,1)S(1)}, bf16[72,2176]{1,0:T(8,128)(2,1)S(1)}, u32[]{:S(2)}, u32[]{:S(2)}) %collective-permute-start.20) | collective-permute-done | bytes 313376 | tf_op jit(solution)/shard_map/ppermute | solution.py:272
  98.3 7.3 %collective-permute-done.21.refs_2_ = bf16[128,640]{1,0:T(8,128)(2,1)S(1)} collective-permute-done((bf16[128,640]{1,0:T(8,128)(2,1)S(1)}, bf16[128,640]{1,0:T(8,128)(2,1)S(1)}, u32[]{:S(2)}, u32[]{:S(2)}) %collective-permute-start.21) | collective-permute-done | bytes 163872 | tf_op jit(solution)/shard_map/ppermute | solution.py:272
  108.0 2.5 %collective-permute-start.25 = (bf16[128,1536]{1,0:T(8,128)(2,1)S(1)}, bf16[128,1536]{1,0:T(8,128)(2,1)S(1)}, u32[]{:S(2)}, u32[]{:S(2)}) collective-permute-start(bf16[128,1536]{1,0:T(8,128)(2,1)S(1)} %get-tuple-element.171), channel_id=1, source_target_pairs={{0,8},{1,9},{2,10},{3,11},{4,12},{5,13},{6,14},{7,15},{8,0},{9,1},... | collective-permute-start | bytes 1179656 | tf_op jit(solution)/shard_map/ppermute | solution.py:272
  110.5 5.2 %expert.7 = (bf16[72,2176]{1,0:T(8,128)(2,1)S(1)}, bf16[72,2176]{1,0:T(8,128)(2,1)S(1)}, bf16[144,2304]{1,0:T(8,128)(2,1)S(1)}, bf16[144,512]{1,0:T(8,128)(2,1)S(1)}, f32[8,128]{1,0:T(8,128)S(1)}) custom-call(bf16[72,4224]{1,0:T(8,128)(2,1)S(1)} %get-tuple-element.147.refs_0_.refs_12_, bf16[72,4224]{1,0:T(8,128)(2,1)S(1)} %collective-permute-done.16.refs_1_.refs_13_, ...), custom_call_target="tpu_custom_call" | custom-call | flops 1 | bytes 24000000 | tf_op jit(solution)/shard_map/expert/pallas_call | solution.py:282
  119.2 8.3 %collective-permute-done.25.refs_3_ = bf16[128,1536]{1,0:T(8,128)(2,1)S(1)} collective-permute-done((bf16[128,1536]{1,0:T(8,128)(2,1)S(1)}, bf16[128,1536]{1,0:T(8,128)(2,1)S(1)}, u32[]{:S(2)}, u32[]{:S(2)}) %collective-permute-start.25) | collective-permute-done | bytes 393248 | tf_op jit(solution)/shard_map/ppermute | solution.py:272
  128.1 2.5 %collective-permute-start.31 = (bf16[128,2176]{1,0:T(8,128)(2,1)S(1)}, bf16[128,2176]{1,0:T(8,128)(2,1)S(1)}, u32[]{:S(2)}, u32[]{:S(2)}) collective-permute-start(bf16[128,2176]{1,0:T(8,128)(2,1)S(1)} %get-tuple-element.187), channel_id=1, source_target_pairs={{0,4},{1,5},{2,6},{3,7},{4,0},{5,1},{6,2},{7,3},{8,12},{9,13},{10,... | collective-permute-start | bytes 1671176 | tf_op jit(solution)/shard_map/ppermute | solution.py:272
  133.3 2.3 %adapter_grads.1 = (f32[1,32,2048]{2,1,0:T(8,128)}, f32[1,32,768]{2,1,0:T(8,128)}, f32[1,32,2048]{2,1,0:T(8,128)}, f32[1,32,768]{2,1,0:T(8,128)}, f32[1,32,768]{...) custom-call(bf16[72,4224]{1,0:T(8,128)(2,1)S(1)} %get-tuple-element.108.refs_0_, ...), custom_call_target="tpu_custom_call" | custom-call | flops 1 | bytes 15000000 | tf_op jit(solution)/shard_map/adapter_grads/pallas_call | solution.py:282
  135.6 1.8 %collective-permute-done.6.refs_4_ = bf16[72,2176]{1,0:T(8,128)(2,1)S(1)} collective-permute-done((bf16[72,2176]{1,0:T(8,128)(2,1)S(1)}, bf16[72,2176]{1,0:T(8,128)(2,1)S(1)}, u32[]{:S(2)}, u32[]{:S(2)}) %collective-permute-start.6) | collective-permute-done | bytes 313376 | tf_op jit(solution)/shard_map/ppermute | solution.py:272
  137.4 1.6 %collective-permute-done.30.refs_5_ = bf16[72,2176]{1,0:T(8,128)(2,1)S(1)} collective-permute-done((bf16[72,2176]{1,0:T(8,128)(2,1)S(1)}, bf16[72,2176]{1,0:T(8,128)(2,1)S(1)}, u32[]{:S(2)}, u32[]{:S(2)}) %collective-permute-start.30) | collective-permute-done | bytes 313376 | tf_op jit(solution)/shard_map/ppermute | solution.py:272
  140.1 3.9 %collective-permute-done.31.refs_1_ = bf16[128,2176]{1,0:T(8,128)(2,1)S(1)} collective-permute-done((bf16[128,2176]{1,0:T(8,128)(2,1)S(1)}, bf16[128,2176]{1,0:T(8,128)(2,1)S(1)}, u32[]{:S(2)}, u32[]{:S(2)}) %collective-permute-start.31) | collective-permute-done | bytes 557088 | tf_op jit(solution)/shard_map/ppermute | solution.py:272
  144.2 14.0 %collective-permute-done.32.refs_1_ = bf16[128,2176]{1,0:T(8,128)(2,1)S(1)} collective-permute-done((bf16[128,2176]{1,0:T(8,128)(2,1)S(1)}, bf16[128,2176]{1,0:T(8,128)(2,1)S(1)}, u32[]{:S(2)}, u32[]{:S(2)}) %collective-permute-start.32) | collective-permute-done | bytes 557088 | tf_op jit(solution)/shard_map/ppermute | solution.py:272
  (75 shorter events, 29.4 us)
Async XLA Ops:
  3.1 26.0 %collective-permute-start.2 = (bf16[128,4224]{1,0:T(8,128)(2,1)}, bf16[128,4224]{1,0:T(8,128)(2,1)}, u32[]{:S(2)}, u32[]{:S(2)}) collective-permute-start(bf16[128,4224]{1,0:T(8,128)(2,1)} %get-tuple-element.105.refs_1_), channel_id=1, source_target_pairs={{0,4},{1,5},{2,6},{3,7},{4,0},{5,1},{6,2},{7,3},{8,12},{9,13},{10,... | collective-permute-start | bytes 3244040 | tf_op jit(solution)/shard_map/ppermute | solution.py:272
  4.7 27.5 %collective-permute-start.3 = (bf16[128,4224]{1,0:T(8,128)(2,1)}, bf16[128,4224]{1,0:T(8,128)(2,1)}, u32[]{:S(2)}, u32[]{:S(2)}) collective-permute-start(bf16[128,4224]{1,0:T(8,128)(2,1)} %get-tuple-element.105.refs_1_), channel_id=1, source_target_pairs={{4,8},{5,9},{6,10},{7,11},{8,4},{9,5},{10,6},{11,7},{20,24},{21,25... | collective-permute-start | bytes 3244040 | tf_op jit(solution)/shard_map/ppermute | solution.py:272
  9.9 26.5 %collective-permute-start.1 = (bf16[72,4224]{1,0:T(8,128)(2,1)S(1)}, bf16[72,4224]{1,0:T(8,128)(2,1)S(1)}, u32[]{:S(2)}, u32[]{:S(2)}) collective-permute-start(bf16[72,4224]{1,0:T(8,128)(2,1)S(1)} %get-tuple-element.109), channel_id=1, source_target_pairs={{0,2},{1,3},{2,0},{3,1},{4,6},{5,7},{6,4},{7,5},{8,10},{9,11},{10,... | collective-permute-start | bytes 1824776 | tf_op jit(solution)/shard_map/ppermute | solution.py:272
  11.5 26.6 %collective-permute-start = (bf16[72,4224]{1,0:T(8,128)(2,1)S(1)}, bf16[72,4224]{1,0:T(8,128)(2,1)S(1)}, u32[]{:S(2)}, u32[]{:S(2)}) collective-permute-start(bf16[72,4224]{1,0:T(8,128)(2,1)S(1)} %get-tuple-element.108.refs_0_), channel_id=1, source_target_pairs={{0,1},{1,0},{2,3},{3,2},{4,5},{5,4},{6,7},{7,6},{8,9},{9,8},{10,11... | collective-permute-start | bytes 1824776 | tf_op jit(solution)/shard_map/ppermute | solution.py:272
  32.2 26.5 %collective-permute-start.7 = (bf16[128,4224]{1,0:T(8,128)(2,1)}, bf16[128,4224]{1,0:T(8,128)(2,1)S(1)}, u32[]{:S(2)}, u32[]{:S(2)}) collective-permute-start(bf16[128,4224]{1,0:T(8,128)(2,1)} %collective-permute-done.2.refs_1_), channel_id=1, source_target_pairs={{4,8},{5,9},{6,10},{7,11},{8,4},{9,5},{10,6},{11,7},{20,24},{21,25... | collective-permute-start | bytes 3244040 | tf_op jit(solution)/shard_map/ppermute | solution.py:272
  34.4 24.7 %collective-permute-start.8 = (bf16[128,4224]{1,0:T(8,128)(2,1)}, bf16[128,4224]{1,0:T(8,128)(2,1)S(1)}, u32[]{:S(2)}, u32[]{:S(2)}) collective-permute-start(bf16[128,4224]{1,0:T(8,128)(2,1)} %collective-permute-done.3.refs_1_), channel_id=1, source_target_pairs={{0,4},{1,5},{2,6},{3,7},{4,0},{5,1},{6,2},{7,3},{8,12},{9,13},{10,... | collective-permute-start | bytes 3244040 | tf_op jit(solution)/shard_map/ppermute | solution.py:272
  36.4 2.1 %collective-permute-start.4 = (bf16[72,4224]{1,0:T(8,128)(2,1)S(1)}, bf16[72,4224]{1,0:T(8,128)(2,1)S(1)}, u32[]{:S(2)}, u32[]{:S(2)}) collective-permute-start(bf16[72,4224]{1,0:T(8,128)(2,1)S(1)} %collective-permute-done.1.refs_2_), channel_id=1, source_target_pairs={{0,1},{1,0},{2,3},{3,2},{4,5},{5,4},{6,7},{7,6},{8,9},{9,8},{10,11... | collective-permute-start | bytes 1824776 | tf_op jit(solution)/shard_map/ppermute | solution.py:272
  36.5 16.1 %collective-permute-start.10 = (bf16[72,4224]{1,0:T(8,128)(2,1)S(1)}, bf16[72,4224]{1,0:T(8,128)(2,1)S(1)}, u32[]{:S(2)}, u32[]{:S(2)}) collective-permute-start(bf16[72,4224]{1,0:T(8,128)(2,1)S(1)} %get-tuple-element.128), channel_id=1, source_target_pairs={{0,2},{1,3},{2,0},{3,1},{4,6},{5,7},{6,4},{7,5},{8,10},{9,11},{10,... | collective-permute-start | bytes 1824776 | tf_op jit(solution)/shard_map/ppermute | solution.py:272
  38.1 14.6 %collective-permute-start.9 = (bf16[72,4224]{1,0:T(8,128)(2,1)S(1)}, bf16[72,4224]{1,0:T(8,128)(2,1)S(1)}, u32[]{:S(2)}, u32[]{:S(2)}) collective-permute-start(bf16[72,4224]{1,0:T(8,128)(2,1)S(1)} %get-tuple-element.130.refs_0_.refs_4_), channel_id=1, source_target_pairs={{0,1},{1,0},{2,3},{3,2},{4,5},{5,4},{6,7},{7,6},{8,9},{9,8},{10,11... | collective-permute-start | bytes 1824776 | tf_op jit(solution)/shard_map/ppermute | solution.py:272
  60.5 2.1 %collective-permute-start.11 = (bf16[72,4224]{1,0:T(8,128)(2,1)S(1)}, bf16[72,4224]{1,0:T(8,128)(2,1)S(1)}, u32[]{:S(2)}, u32[]{:S(2)}) collective-permute-start(bf16[72,4224]{1,0:T(8,128)(2,1)S(1)} %collective-permute-done.10.refs_2_.refs_6_), channel_id=1, source_target_pairs={{0,1},{1,0},{2,3},{3,2},{4,5},{5,4},{6,7},{7,6},{8,9},{9,8},{10,11... | collective-permute-start | bytes 1824776 | tf_op jit(solution)/shard_map/ppermute | solution.py:272
  60.6 16.1 %collective-permute-start.13 = (bf16[72,4224]{1,0:T(8,128)(2,1)S(1)}, bf16[72,4224]{1,0:T(8,128)(2,1)S(1)}, u32[]{:S(2)}, u32[]{:S(2)}) collective-permute-start(bf16[72,4224]{1,0:T(8,128)(2,1)S(1)} %get-tuple-element.139), channel_id=1, source_target_pairs={{0,2},{1,3},{2,0},{3,1},{4,6},{5,7},{6,4},{7,5},{8,10},{9,11},{10,... | collective-permute-start | bytes 1824776 | tf_op jit(solution)/shard_map/ppermute | solution.py:272
  62.2 25.9 %collective-permute-start.15 = (bf16[128,4224]{1,0:T(8,128)(2,1)S(1)}, bf16[128,4224]{1,0:T(8,128)(2,1)S(1)}, u32[]{:S(2)}, u32[]{:S(2)}) collective-permute-start(bf16[128,4224]{1,0:T(8,128)(2,1)S(1)} %collective-permute-done.7.refs_1_), channel_id=1, source_target_pairs={{0,4},{1,5},{2,6},{3,7},{4,0},{5,1},{6,2},{7,3},{8,12},{9,13},{10,... | collective-permute-start | bytes 3244040 | tf_op jit(solution)/shard_map/ppermute | solution.py:272
  62.6 14.2 %collective-permute-start.12 = (bf16[72,4224]{1,0:T(8,128)(2,1)S(1)}, bf16[72,4224]{1,0:T(8,128)(2,1)S(1)}, u32[]{:S(2)}, u32[]{:S(2)}) collective-permute-start(bf16[72,4224]{1,0:T(8,128)(2,1)S(1)} %get-tuple-element.138.refs_0_.refs_8_), channel_id=1, source_target_pairs={{0,1},{1,0},{2,3},{3,2},{4,5},{5,4},{6,7},{7,6},{8,9},{9,8},{10,11... | collective-permute-start | bytes 1824776 | tf_op jit(solution)/shard_map/ppermute | solution.py:272
  76.8 2.0 %collective-permute-start.14 = (bf16[72,4224]{1,0:T(8,128)(2,1)S(1)}, bf16[72,4224]{1,0:T(8,128)(2,1)S(1)}, u32[]{:S(2)}, u32[]{:S(2)}) collective-permute-start(bf16[72,4224]{1,0:T(8,128)(2,1)S(1)} %collective-permute-done.13.refs_2_.refs_10_), channel_id=1, source_target_pairs={{0,1},{1,0},{2,3},{3,2},{4,5},{5,4},{6,7},{7,6},{8,9},{9,8},{10,11... | collective-permute-start | bytes 1824776 | tf_op jit(solution)/shard_map/ppermute | solution.py:272
  84.0 10.3 %collective-permute-start.19 = (bf16[72,2176]{1,0:T(8,128)(2,1)S(1)}, bf16[72,2176]{1,0:T(8,128)(2,1)S(1)}, u32[]{:S(2)}, u32[]{:S(2)}) collective-permute-start(bf16[72,2176]{1,0:T(8,128)(2,1)S(1)} %get-tuple-element.151), channel_id=1, source_target_pairs={{0,2},{1,3},{2,0},{3,1},{4,6},{5,7},{6,4},{7,5},{8,10},{9,11},{10,... | collective-permute-start | bytes 940040 | tf_op jit(solution)/shard_map/ppermute | solution.py:272
  90.3 16.3 %collective-permute-start.17 = (bf16[72,4224]{1,0:T(8,128)(2,1)S(1)}, bf16[72,4224]{1,0:T(8,128)(2,1)S(1)}, u32[]{:S(2)}, u32[]{:S(2)}) collective-permute-start(bf16[72,4224]{1,0:T(8,128)(2,1)S(1)} %get-tuple-element.148), channel_id=1, source_target_pairs={{0,2},{1,3},{2,0},{3,1},{4,6},{5,7},{6,4},{7,5},{8,10},{9,11},{10,... | collective-permute-start | bytes 1824776 | tf_op jit(solution)/shard_map/ppermute | solution.py:272
  90.8 3.5 %collective-permute-start.18 = (bf16[72,2176]{1,0:T(8,128)(2,1)S(1)}, bf16[72,2176]{1,0:T(8,128)(2,1)S(1)}, u32[]{:S(2)}, u32[]{:S(2)}) collective-permute-start(bf16[72,2176]{1,0:T(8,128)(2,1)S(1)} %get-tuple-element.150.refs_2_), channel_id=1, source_target_pairs={{0,1},{1,0},{2,3},{3,2},{4,5},{5,4},{6,7},{7,6},{8,9},{9,8},{10,11... | collective-permute-start | bytes 940040 | tf_op jit(solution)/shard_map/ppermute | solution.py:272
  94.3 1.6 %collective-permute-start.20 = (bf16[72,2176]{1,0:T(8,128)(2,1)S(1)}, bf16[72,2176]{1,0:T(8,128)(2,1)S(1)}, u32[]{:S(2)}, u32[]{:S(2)}) collective-permute-start(bf16[72,2176]{1,0:T(8,128)(2,1)S(1)} %collective-permute-done.19.refs_4_), channel_id=1, source_target_pairs={{0,1},{1,0},{2,3},{3,2},{4,5},{5,4},{6,7},{7,6},{8,9},{9,8},{10,11... | collective-permute-start | bytes 940040 | tf_op jit(solution)/shard_map/ppermute | solution.py:272
  97.0 8.5 %collective-permute-start.21 = (bf16[128,640]{1,0:T(8,128)(2,1)S(1)}, bf16[128,640]{1,0:T(8,128)(2,1)S(1)}, u32[]{:S(2)}, u32[]{:S(2)}) collective-permute-start(bf16[128,640]{1,0:T(8,128)(2,1)S(1)} %get-tuple-element.155), channel_id=1, source_target_pairs={{0,8},{1,9},{2,10},{3,11},{4,12},{5,13},{6,14},{7,15},{8,0},{9,1},... | collective-permute-start | bytes 491528 | tf_op jit(solution)/shard_map/ppermute | solution.py:272
  98.3 12.2 %collective-permute-start.16 = (bf16[72,4224]{1,0:T(8,128)(2,1)S(1)}, bf16[72,4224]{1,0:T(8,128)(2,1)S(1)}, u32[]{:S(2)}, u32[]{:S(2)}) collective-permute-start(bf16[72,4224]{1,0:T(8,128)(2,1)S(1)} %get-tuple-element.147.refs_0_.refs_12_), channel_id=1, source_target_pairs={{0,1},{1,0},{2,3},{3,2},{4,5},{5,4},{6,7},{7,6},{8,9},{9,8},{10,11... | collective-permute-start | bytes 1824776 | tf_op jit(solution)/shard_map/ppermute | solution.py:272
  106.5 4.0 %collective-permute-start.22 = (bf16[72,4224]{1,0:T(8,128)(2,1)S(1)}, bf16[72,4224]{1,0:T(8,128)(2,1)S(1)}, u32[]{:S(2)}, u32[]{:S(2)}) collective-permute-start(bf16[72,4224]{1,0:T(8,128)(2,1)S(1)} %collective-permute-done.17.refs_2_.refs_14_), channel_id=1, source_target_pairs={{0,1},{1,0},{2,3},{3,2},{4,5},{5,4},{6,7},{7,6},{8,9},{9,8},{10,11... | collective-permute-start | bytes 1824776 | tf_op jit(solution)/shard_map/ppermute | solution.py:272
  106.5 9.8 %collective-permute-start.27 = (bf16[72,2176]{1,0:T(8,128)(2,1)S(1)}, bf16[72,2176]{1,0:T(8,128)(2,1)S(1)}, u32[]{:S(2)}, u32[]{:S(2)}) collective-permute-start(bf16[72,2176]{1,0:T(8,128)(2,1)S(1)} %get-tuple-element.174), channel_id=1, source_target_pairs={{0,2},{1,3},{2,0},{3,1},{4,6},{5,7},{6,4},{7,5},{8,10},{9,11},{10,... | collective-permute-start | bytes 940040 | tf_op jit(solution)/shard_map/ppermute | solution.py:272
  108.0 19.5 %collective-permute-start.25 = (bf16[128,1536]{1,0:T(8,128)(2,1)S(1)}, bf16[128,1536]{1,0:T(8,128)(2,1)S(1)}, u32[]{:S(2)}, u32[]{:S(2)}) collective-permute-start(bf16[128,1536]{1,0:T(8,128)(2,1)S(1)} %get-tuple-element.171), channel_id=1, source_target_pairs={{0,8},{1,9},{2,10},{3,11},{4,12},{5,13},{6,14},{7,15},{8,0},{9,1},... | collective-permute-start | bytes 1179656 | tf_op jit(solution)/shard_map/ppermute | solution.py:272
  110.5 7.6 %collective-permute-start.26 = (bf16[72,2176]{1,0:T(8,128)(2,1)S(1)}, bf16[72,2176]{1,0:T(8,128)(2,1)S(1)}, u32[]{:S(2)}, u32[]{:S(2)}) collective-permute-start(bf16[72,2176]{1,0:T(8,128)(2,1)S(1)} %get-tuple-element.173.refs_2_), channel_id=1, source_target_pairs={{0,1},{1,0},{2,3},{3,2},{4,5},{5,4},{6,7},{7,6},{8,9},{9,8},{10,11... | collective-permute-start | bytes 940040 | tf_op jit(solution)/shard_map/ppermute | solution.py:272
  116.3 1.8 %collective-permute-start.28 = (bf16[72,2176]{1,0:T(8,128)(2,1)S(1)}, bf16[72,2176]{1,0:T(8,128)(2,1)S(1)}, u32[]{:S(2)}, u32[]{:S(2)}) collective-permute-start(bf16[72,2176]{1,0:T(8,128)(2,1)S(1)} %collective-permute-done.27.refs_4_), channel_id=1, source_target_pairs={{0,1},{1,0},{2,3},{3,2},{4,5},{5,4},{6,7},{7,6},{8,9},{9,8},{10,11... | collective-permute-start | bytes 940040 | tf_op jit(solution)/shard_map/ppermute | solution.py:272
  116.3 11.2 %collective-permute-start.24 = (bf16[72,2176]{1,0:T(8,128)(2,1)S(1)}, bf16[72,2176]{1,0:T(8,128)(2,1)S(1)}, u32[]{:S(2)}, u32[]{:S(2)}) collective-permute-start(bf16[72,2176]{1,0:T(8,128)(2,1)S(1)} %get-tuple-element.170), channel_id=1, source_target_pairs={{0,2},{1,3},{2,0},{3,1},{4,6},{5,7},{6,4},{7,5},{8,10},{9,11},{10,... | collective-permute-start | bytes 940040 | tf_op jit(solution)/shard_map/ppermute | solution.py:272
  117.9 12.8 %collective-permute-start.23 = (bf16[72,2176]{1,0:T(8,128)(2,1)S(1)}, bf16[72,2176]{1,0:T(8,128)(2,1)S(1)}, u32[]{:S(2)}, u32[]{:S(2)}) collective-permute-start(bf16[72,2176]{1,0:T(8,128)(2,1)S(1)} %get-tuple-element.169.refs_2_), channel_id=1, source_target_pairs={{0,1},{1,0},{2,3},{3,2},{4,5},{5,4},{6,7},{7,6},{8,9},{9,8},{10,11... | collective-permute-start | bytes 940040 | tf_op jit(solution)/shard_map/ppermute | solution.py:272
  127.5 3.1 %collective-permute-start.29 = (bf16[72,2176]{1,0:T(8,128)(2,1)S(1)}, bf16[72,2176]{1,0:T(8,128)(2,1)S(1)}, u32[]{:S(2)}, u32[]{:S(2)}) collective-permute-start(bf16[72,2176]{1,0:T(8,128)(2,1)S(1)} %collective-permute-done.24.refs_4_), channel_id=1, source_target_pairs={{0,1},{1,0},{2,3},{3,2},{4,5},{5,4},{6,7},{7,6},{8,9},{9,8},{10,11... | collective-permute-start | bytes 940040 | tf_op jit(solution)/shard_map/ppermute | solution.py:272
  127.6 9.8 %collective-permute-start.6 = (bf16[72,2176]{1,0:T(8,128)(2,1)S(1)}, bf16[72,2176]{1,0:T(8,128)(2,1)S(1)}, u32[]{:S(2)}, u32[]{:S(2)}) collective-permute-start(bf16[72,2176]{1,0:T(8,128)(2,1)S(1)} %get-tuple-element.125), channel_id=1, source_target_pairs={{0,2},{1,3},{2,0},{3,1},{4,6},{5,7},{6,4},{7,5},{8,10},{9,11},{10,... | collective-permute-start | bytes 940040 | tf_op jit(solution)/shard_map/ppermute | solution.py:272
  128.1 15.9 %collective-permute-start.31 = (bf16[128,2176]{1,0:T(8,128)(2,1)S(1)}, bf16[128,2176]{1,0:T(8,128)(2,1)S(1)}, u32[]{:S(2)}, u32[]{:S(2)}) collective-permute-start(bf16[128,2176]{1,0:T(8,128)(2,1)S(1)} %get-tuple-element.187), channel_id=1, source_target_pairs={{0,4},{1,5},{2,6},{3,7},{4,0},{5,1},{6,2},{7,3},{8,12},{9,13},{10,... | collective-permute-start | bytes 1671176 | tf_op jit(solution)/shard_map/ppermute | solution.py:272
  131.8 26.4 %collective-permute-start.32 = (bf16[128,2176]{1,0:T(8,128)(2,1)S(1)}, bf16[128,2176]{1,0:T(8,128)(2,1)S(1)}, u32[]{:S(2)}, u32[]{:S(2)}) collective-permute-start(bf16[128,2176]{1,0:T(8,128)(2,1)S(1)} %get-tuple-element.192), channel_id=1, source_target_pairs={{0,12},{1,13},{2,14},{3,15},{4,8},{5,9},{6,10},{7,11},{8,4},{9,5},... | collective-permute-start | bytes 1671176 | tf_op jit(solution)/shard_map/ppermute | solution.py:272
  133.3 4.1 %collective-permute-start.5 = (bf16[72,2176]{1,0:T(8,128)(2,1)S(1)}, bf16[72,2176]{1,0:T(8,128)(2,1)S(1)}, u32[]{:S(2)}, u32[]{:S(2)}) collective-permute-start(bf16[72,2176]{1,0:T(8,128)(2,1)S(1)} %get-tuple-element.124.refs_2_), channel_id=1, source_target_pairs={{0,1},{1,0},{2,3},{3,2},{4,5},{5,4},{6,7},{7,6},{8,9},{9,8},{10,11... | collective-permute-start | bytes 940040 | tf_op jit(solution)/shard_map/ppermute | solution.py:272
  (12 other events, 50.3 us)

commit v5 on v4

--- a/solution.py
+++ b/solution.py
@@ -406,7 +406,7 @@
         mate_across, far = flipped(mate, 3 * PLANE, mids), flipped(across, PLANE)
         begin(1, mate)
         middle_of(0)
-        mate_across, far, *rows_of[1] = together(mate_across, far, *rows_of[1])
+        mate_across, far = together(mate_across, far)
         farthest = flipped(mate_across, PLANE)
         begin(2, mate_across, far)
         middle_of(1)

time: 161 us -> 160 us (level)
  starting transfers between devices: 24.9 us -> 23.1 us
    ppermute x33, starting transfers between devices: 24.9 us -> 23.1 us  [flipped(): return lax.ppermute(value, 'expert', pairs)]
  transfers between devices with their start and end apart: 33 -> 33, of which waited for: 20 -> 19; matrix products, arithmetic and copies ran while one was open for 0% -> 0% of each run, Pallas kernels for 21% -> 22%
where the time goes in v5:
time: 160 us; the launch traced here: 158 us
  waiting for transfers between devices  84.9 us (53%)
  Pallas kernels  38.2 us (24%)
  starting transfers between devices  23.1 us (14%)
  local copies, waits for them, and re-layouts  10.9 us (7%)
    ppermute x33, waiting for transfers between devices, flipped(): return lax.ppermute(value, 'expert', pairs)  84.9 us
    pallas_call x17, Pallas kernels, kernel(): pl.pallas_call(run, out_shape=[*outs, shape((8, LANES), F32)], in_specs=[...  38.2 us
    ppermute x33, starting transfers between devices, flipped(): return lax.ppermute(value, 'expert', pairs)  23.1 us
    unnamed x22, local copies, waits for them, and re-layouts  10.8 us
  transfers between devices with their start and end apart: 33, of which 19 were waited for; matrix products, arithmetic and copies ran while one was open for 0% of the time, Pallas kernels for 22%

profile of v5, /device:TPU:16, one launch (start us, length us, event | category | flops | bytes accessed | tf_op | source)
XLA Modules:
  0.0 158.0 jit_solution(16542277766268434846)
XLA Ops:
  0.6 2.4 %pack.1 = (bf16[128,4224]{1,0:T(8,128)(2,1)}, f32[8,128]{1,0:T(8,128)}) custom-call(bf16[128,2048]{1,0:T(8,128)(2,1)} %refs_0_.1, bf16[128,2048]{1,0:T(8,128)(2,1)} %refs_1_.1, s32[4,128]{1,0:T(4,128)} %bitcast.35, f32[4,128]{1,0:T(4,128)} %bitcast.36), custom_call_target="tpu_custom_call" | custom-call | flops 1 | bytes 6000000 | tf_op jit(solution)/shard_map/pack/pallas_call | solution.py:282
  3.1 1.6 %collective-permute-start.2 = (bf16[128,4224]{1,0:T(8,128)(2,1)}, bf16[128,4224]{1,0:T(8,128)(2,1)}, u32[]{:S(2)}, u32[]{:S(2)}) collective-permute-start(bf16[128,4224]{1,0:T(8,128)(2,1)} %get-tuple-element.102.refs_1_), channel_id=1, source_target_pairs={{0,4},{1,5},{2,6},{3,7},{4,0},{5,1},{6,2},{7,3},{8,12},{9,13},{10,... | collective-permute-start | bytes 3244040 | tf_op jit(solution)/shard_map/ppermute | solution.py:272
  4.7 1.9 %collective-permute-start.3 = (bf16[128,4224]{1,0:T(8,128)(2,1)}, bf16[128,4224]{1,0:T(8,128)(2,1)}, u32[]{:S(2)}, u32[]{:S(2)}) collective-permute-start(bf16[128,4224]{1,0:T(8,128)(2,1)} %get-tuple-element.102.refs_1_), channel_id=1, source_target_pairs={{4,8},{5,9},{6,10},{7,11},{8,4},{9,5},{10,6},{11,7},{20,24},{21,25... | collective-permute-start | bytes 3244040 | tf_op jit(solution)/shard_map/ppermute | solution.py:272
  9.9 1.6 %collective-permute-start.1 = (bf16[72,4224]{1,0:T(8,128)(2,1)S(1)}, bf16[72,4224]{1,0:T(8,128)(2,1)S(1)}, u32[]{:S(2)}, u32[]{:S(2)}) collective-permute-start(bf16[72,4224]{1,0:T(8,128)(2,1)S(1)} %get-tuple-element.106), channel_id=1, source_target_pairs={{0,2},{1,3},{2,0},{3,1},{4,6},{5,7},{6,4},{7,5},{8,10},{9,11},{10,... | collective-permute-start | bytes 1824776 | tf_op jit(solution)/shard_map/ppermute | solution.py:272
  17.1 12.0 %collective-permute-done.2.refs_1_ = bf16[128,4224]{1,0:T(8,128)(2,1)} collective-permute-done((bf16[128,4224]{1,0:T(8,128)(2,1)}, bf16[128,4224]{1,0:T(8,128)(2,1)}, u32[]{:S(2)}, u32[]{:S(2)}) %collective-permute-start.2) | collective-permute-done | bytes 1081376 | tf_op jit(solution)/shard_map/ppermute | solution.py:272
  29.1 3.2 %collective-permute-done.3.refs_1_ = bf16[128,4224]{1,0:T(8,128)(2,1)} collective-permute-done((bf16[128,4224]{1,0:T(8,128)(2,1)}, bf16[128,4224]{1,0:T(8,128)(2,1)}, u32[]{:S(2)}, u32[]{:S(2)}) %collective-permute-start.3) | collective-permute-done | bytes 1081376 | tf_op jit(solution)/shard_map/ppermute | solution.py:272
  32.3 2.2 %collective-permute-start.9 = (bf16[128,4224]{1,0:T(8,128)(2,1)}, bf16[128,4224]{1,0:T(8,128)(2,1)S(1)}, u32[]{:S(2)}, u32[]{:S(2)}) collective-permute-start(bf16[128,4224]{1,0:T(8,128)(2,1)} %collective-permute-done.2.refs_1_), channel_id=1, source_target_pairs={{4,8},{5,9},{6,10},{7,11},{8,4},{9,5},{10,6},{11,7},{20,24},{21,25... | collective-permute-start | bytes 3244040 | tf_op jit(solution)/shard_map/ppermute | solution.py:272
  34.5 1.9 %select.11 = (bf16[72,4224]{1,0:T(8,128)(2,1)S(1)}, bf16[72,4224]{1,0:T(8,128)(2,1)S(1)}, bf16[128,128]{1,0:T(8,128)(2,1)S(1)}, f32[8,128]{1,0:T(8,128)S(1)}) custom-call(s32[8]{0:T(128)S(1)} %stack.28.refs_0_, bf16[128,4224]{1,0:T(8,128)(2,1)} %collective-permute-done.2.refs_1_, f32[8,128]{1,0:T(8,128)S(1)} %get-tuple-element.110.refs_2_), custom_call_target="tpu_custom_call" | custom-call | flops 1 | bytes 12000000 | tf_op jit(solution)/shard_map/select/pallas_call | solution.py:282
  38.7 1.9 %copy-done.1 = bf16[1,2048,768]{2,1,0:T(8,128)(2,1)S(1)} copy-done((bf16[1,2048,768]{2,1,0:T(8,128)(2,1)S(1)}, bf16[1,2048,768]{2,1,0:T(8,128)(2,1)}, u32[]{:S(2)}) %copy-start.1) | copy-done | bytes 3145752
  40.5 1.9 %copy-done.2 = bf16[1,768,2048]{2,1,0:T(8,128)(2,1)S(1)} copy-done((bf16[1,768,2048]{2,1,0:T(8,128)(2,1)S(1)}, bf16[1,768,2048]{2,1,0:T(8,128)(2,1)}, u32[]{:S(2)}) %copy-start.2) | copy-done | bytes 3145752
  42.4 5.2 %expert.4 = (bf16[72,2176]{1,0:T(8,128)(2,1)S(1)}, bf16[72,2176]{1,0:T(8,128)(2,1)S(1)}, bf16[144,2304]{1,0:T(8,128)(2,1)S(1)}, bf16[144,512]{1,0:T(8,128)(2,1)S(1)}, f32[8,128]{1,0:T(8,128)S(1)}) custom-call(bf16[72,4224]{1,0:T(8,128)(2,1)S(1)} %get-tuple-element.105.refs_0_, bf16[72,4224]{1,0:T(8,128)(2,1)S(1)} %collective-permute-done.refs_1_, ...), custom_call_target="tpu_custom_call" | custom-call | flops 1 | bytes 24000000 | tf_op jit(solution)/shard_map/expert/pallas_call | solution.py:282
  47.6 9.3 %collective-permute-done.10.refs_2_ = bf16[128,4224]{1,0:T(8,128)(2,1)S(1)} collective-permute-done((bf16[128,4224]{1,0:T(8,128)(2,1)}, bf16[128,4224]{1,0:T(8,128)(2,1)S(1)}, u32[]{:S(2)}, u32[]{:S(2)}) %collective-permute-start.10) | collective-permute-done | bytes 1081376 | tf_op jit(solution)/shard_map/ppermute | solution.py:272
  56.9 1.9 %collective-permute-done.9.refs_1_ = bf16[128,4224]{1,0:T(8,128)(2,1)S(1)} collective-permute-done((bf16[128,4224]{1,0:T(8,128)(2,1)}, bf16[128,4224]{1,0:T(8,128)(2,1)S(1)}, u32[]{:S(2)}, u32[]{:S(2)}) %collective-permute-start.9) | collective-permute-done | bytes 1081376 | tf_op jit(solution)/shard_map/ppermute | solution.py:272
  62.2 5.1 %expert.5 = (bf16[72,2176]{1,0:T(8,128)(2,1)S(1)}, bf16[72,2176]{1,0:T(8,128)(2,1)S(1)}, bf16[144,2304]{1,0:T(8,128)(2,1)S(1)}, bf16[144,512]{1,0:T(8,128)(2,1)S(1)}, f32[8,128]{1,0:T(8,128)S(1)}) custom-call(bf16[72,4224]{1,0:T(8,128)(2,1)S(1)} %get-tuple-element.123.refs_0_.refs_4_, bf16[72,4224]{1,0:T(8,128)(2,1)S(1)} %collective-permute-done.7.refs_1_.refs_5_, ...), custom_call_target="tpu_custom_call" | custom-call | flops 1 | bytes 24000000 | tf_op jit(solution)/shard_map/expert/pallas_call | solution.py:282
  67.4 9.0 %collective-permute-done.13.refs_2_.refs_10_ = bf16[72,4224]{1,0:T(8,128)(2,1)S(1)} collective-permute-done((bf16[72,4224]{1,0:T(8,128)(2,1)S(1)}, bf16[72,4224]{1,0:T(8,128)(2,1)S(1)}, u32[]{:S(2)}, u32[]{:S(2)}) %collective-permute-start.13) | collective-permute-done | bytes 608288 | tf_op jit(solution)/shard_map/ppermute | solution.py:272
  76.4 2.0 %collective-permute-done.14.refs_3_.refs_11_ = bf16[72,4224]{1,0:T(8,128)(2,1)S(1)} collective-permute-done((bf16[72,4224]{1,0:T(8,128)(2,1)S(1)}, bf16[72,4224]{1,0:T(8,128)(2,1)S(1)}, u32[]{:S(2)}, u32[]{:S(2)}) %collective-permute-start.14) | collective-permute-done | bytes 608288 | tf_op jit(solution)/shard_map/ppermute | solution.py:272
  78.4 5.1 %expert.6 = (bf16[72,2176]{1,0:T(8,128)(2,1)S(1)}, bf16[72,2176]{1,0:T(8,128)(2,1)S(1)}, bf16[144,2304]{1,0:T(8,128)(2,1)S(1)}, bf16[144,512]{1,0:T(8,128)(2,1)S(1)}, f32[8,128]{1,0:T(8,128)S(1)}) custom-call(bf16[72,4224]{1,0:T(8,128)(2,1)S(1)} %get-tuple-element.132.refs_0_.refs_8_, bf16[72,4224]{1,0:T(8,128)(2,1)S(1)} %collective-permute-done.12.refs_1_.refs_9_, ...), custom_call_target="tpu_custom_call" | custom-call | flops 1 | bytes 24000000 | tf_op jit(solution)/shard_map/expert/pallas_call | solution.py:282
  83.5 1.6 %collective-permute-start.19 = (bf16[72,2176]{1,0:T(8,128)(2,1)S(1)}, bf16[72,2176]{1,0:T(8,128)(2,1)S(1)}, u32[]{:S(2)}, u32[]{:S(2)}) collective-permute-start(bf16[72,2176]{1,0:T(8,128)(2,1)S(1)} %get-tuple-element.145), channel_id=1, source_target_pairs={{0,2},{1,3},{2,0},{3,1},{4,6},{5,7},{6,4},{7,5},{8,10},{9,11},{10,... | collective-permute-start | bytes 940040 | tf_op jit(solution)/shard_map/ppermute | solution.py:272
  85.1 2.6 %collective-permute-done.15.refs_2_ = bf16[128,4224]{1,0:T(8,128)(2,1)S(1)} collective-permute-done((bf16[128,4224]{1,0:T(8,128)(2,1)S(1)}, bf16[128,4224]{1,0:T(8,128)(2,1)S(1)}, u32[]{:S(2)}, u32[]{:S(2)}) %collective-permute-start.15) | collective-permute-done | bytes 1081376 | tf_op jit(solution)/shard_map/ppermute | solution.py:272
  87.7 2.1 %select.13 = (bf16[72,4224]{1,0:T(8,128)(2,1)S(1)}, bf16[72,4224]{1,0:T(8,128)(2,1)S(1)}, bf16[128,128]{1,0:T(8,128)(2,1)S(1)}, f32[8,128]{1,0:T(8,128)S(1)}) custom-call(s32[8]{0:T(128)S(1)} %stack.28.refs_0_, bf16[128,4224]{1,0:T(8,128)(2,1)} %collective-permute-done.3.refs_1_, bf16[128,4224]{1,0:T(8,128)(2,1)S(1)} %collective-permute-done.15.refs_2_, ...), custom_call_target="tpu_custom_call" | custom-call | flops 1 | bytes 12000000 | tf_op jit(solution)/shard_map/select/pallas_call | solution.py:282
  90.4 3.4 %collective-permute-done.19.refs_4_ = bf16[72,2176]{1,0:T(8,128)(2,1)S(1)} collective-permute-done((bf16[72,2176]{1,0:T(8,128)(2,1)S(1)}, bf16[72,2176]{1,0:T(8,128)(2,1)S(1)}, u32[]{:S(2)}, u32[]{:S(2)}) %collective-permute-start.19) | collective-permute-done | bytes 313376 | tf_op jit(solution)/shard_map/ppermute | solution.py:272
  93.8 1.6 %collective-permute-done.20.refs_5_ = bf16[72,2176]{1,0:T(8,128)(2,1)S(1)} collective-permute-done((bf16[72,2176]{1,0:T(8,128)(2,1)S(1)}, bf16[72,2176]{1,0:T(8,128)(2,1)S(1)}, u32[]{:S(2)}, u32[]{:S(2)}) %collective-permute-start.20) | collective-permute-done | bytes 313376 | tf_op jit(solution)/shard_map/ppermute | solution.py:272
  96.9 7.3 %collective-permute-done.21.refs_2_ = bf16[128,640]{1,0:T(8,128)(2,1)S(1)} collective-permute-done((bf16[128,640]{1,0:T(8,128)(2,1)S(1)}, bf16[128,640]{1,0:T(8,128)(2,1)S(1)}, u32[]{:S(2)}, u32[]{:S(2)}) %collective-permute-start.21) | collective-permute-done | bytes 163872 | tf_op jit(solution)/shard_map/ppermute | solution.py:272
  104.2 1.8 %collective-permute-done.17.refs_2_.refs_14_ = bf16[72,4224]{1,0:T(8,128)(2,1)S(1)} collective-permute-done((bf16[72,4224]{1,0:T(8,128)(2,1)S(1)}, bf16[72,4224]{1,0:T(8,128)(2,1)S(1)}, u32[]{:S(2)}, u32[]{:S(2)}) %collective-permute-start.17) | collective-permute-done | bytes 608288 | tf_op jit(solution)/shard_map/ppermute | solution.py:272
  109.1 5.2 %expert.7 = (bf16[72,2176]{1,0:T(8,128)(2,1)S(1)}, bf16[72,2176]{1,0:T(8,128)(2,1)S(1)}, bf16[144,2304]{1,0:T(8,128)(2,1)S(1)}, bf16[144,512]{1,0:T(8,128)(2,1)S(1)}, f32[8,128]{1,0:T(8,128)S(1)}) custom-call(bf16[72,4224]{1,0:T(8,128)(2,1)S(1)} %get-tuple-element.141.refs_0_.refs_12_, bf16[72,4224]{1,0:T(8,128)(2,1)S(1)} %collective-permute-done.16.refs_1_.refs_13_, ...), custom_call_target="tpu_custom_call" | custom-call | flops 1 | bytes 24000000 | tf_op jit(solution)/shard_map/expert/pallas_call | solution.py:282
  118.8 7.5 %collective-permute-done.25.refs_3_ = bf16[128,1536]{1,0:T(8,128)(2,1)S(1)} collective-permute-done((bf16[128,1536]{1,0:T(8,128)(2,1)S(1)}, bf16[128,1536]{1,0:T(8,128)(2,1)S(1)}, u32[]{:S(2)}, u32[]{:S(2)}) %collective-permute-start.25) | collective-permute-done | bytes 393248 | tf_op jit(solution)/shard_map/ppermute | solution.py:272
  127.2 2.1 %collective-permute-start.31 = (bf16[128,2176]{1,0:T(8,128)(2,1)S(1)}, bf16[128,2176]{1,0:T(8,128)(2,1)S(1)}, u32[]{:S(2)}, u32[]{:S(2)}) collective-permute-start(bf16[128,2176]{1,0:T(8,128)(2,1)S(1)} %get-tuple-element.181), channel_id=1, source_target_pairs={{0,4},{1,5},{2,6},{3,7},{4,0},{5,1},{6,2},{7,3},{8,12},{9,13},{10,... | collective-permute-start | bytes 1671176 | tf_op jit(solution)/shard_map/ppermute | solution.py:272
  132.0 2.3 %adapter_grads.1 = (f32[1,32,2048]{2,1,0:T(8,128)}, f32[1,32,768]{2,1,0:T(8,128)}, f32[1,32,2048]{2,1,0:T(8,128)}, f32[1,32,768]{2,1,0:T(8,128)}, f32[1,32,768]{...) custom-call(bf16[72,4224]{1,0:T(8,128)(2,1)S(1)} %get-tuple-element.105.refs_0_, ...), custom_call_target="tpu_custom_call" | custom-call | flops 1 | bytes 15000000 | tf_op jit(solution)/shard_map/adapter_grads/pallas_call | solution.py:282
  134.4 1.8 %collective-permute-done.6.refs_4_ = bf16[72,2176]{1,0:T(8,128)(2,1)S(1)} collective-permute-done((bf16[72,2176]{1,0:T(8,128)(2,1)S(1)}, bf16[72,2176]{1,0:T(8,128)(2,1)S(1)}, u32[]{:S(2)}, u32[]{:S(2)}) %collective-permute-start.6) | collective-permute-done | bytes 313376 | tf_op jit(solution)/shard_map/ppermute | solution.py:272
  136.1 1.6 %collective-permute-done.30.refs_5_ = bf16[72,2176]{1,0:T(8,128)(2,1)S(1)} collective-permute-done((bf16[72,2176]{1,0:T(8,128)(2,1)S(1)}, bf16[72,2176]{1,0:T(8,128)(2,1)S(1)}, u32[]{:S(2)}, u32[]{:S(2)}) %collective-permute-start.30) | collective-permute-done | bytes 313376 | tf_op jit(solution)/shard_map/ppermute | solution.py:272
  138.9 3.9 %collective-permute-done.31.refs_1_ = bf16[128,2176]{1,0:T(8,128)(2,1)S(1)} collective-permute-done((bf16[128,2176]{1,0:T(8,128)(2,1)S(1)}, bf16[128,2176]{1,0:T(8,128)(2,1)S(1)}, u32[]{:S(2)}, u32[]{:S(2)}) %collective-permute-start.31) | collective-permute-done | bytes 557088 | tf_op jit(solution)/shard_map/ppermute | solution.py:272
  143.0 14.0 %collective-permute-done.32.refs_1_ = bf16[128,2176]{1,0:T(8,128)(2,1)S(1)} collective-permute-done((bf16[128,2176]{1,0:T(8,128)(2,1)S(1)}, bf16[128,2176]{1,0:T(8,128)(2,1)S(1)}, u32[]{:S(2)}, u32[]{:S(2)}) %collective-permute-start.32) | collective-permute-done | bytes 557088 | tf_op jit(solution)/shard_map/ppermute | solution.py:272
  (75 shorter events, 30.1 us)
Async XLA Ops:
  3.1 26.0 %collective-permute-start.2 = (bf16[128,4224]{1,0:T(8,128)(2,1)}, bf16[128,4224]{1,0:T(8,128)(2,1)}, u32[]{:S(2)}, u32[]{:S(2)}) collective-permute-start(bf16[128,4224]{1,0:T(8,128)(2,1)} %get-tuple-element.102.refs_1_), channel_id=1, source_target_pairs={{0,4},{1,5},{2,6},{3,7},{4,0},{5,1},{6,2},{7,3},{8,12},{9,13},{10,... | collective-permute-start | bytes 3244040 | tf_op jit(solution)/shard_map/ppermute | solution.py:272
  4.7 27.5 %collective-permute-start.3 = (bf16[128,4224]{1,0:T(8,128)(2,1)}, bf16[128,4224]{1,0:T(8,128)(2,1)}, u32[]{:S(2)}, u32[]{:S(2)}) collective-permute-start(bf16[128,4224]{1,0:T(8,128)(2,1)} %get-tuple-element.102.refs_1_), channel_id=1, source_target_pairs={{4,8},{5,9},{6,10},{7,11},{8,4},{9,5},{10,6},{11,7},{20,24},{21,25... | collective-permute-start | bytes 3244040 | tf_op jit(solution)/shard_map/ppermute | solution.py:272
  9.9 26.5 %collective-permute-start.1 = (bf16[72,4224]{1,0:T(8,128)(2,1)S(1)}, bf16[72,4224]{1,0:T(8,128)(2,1)S(1)}, u32[]{:S(2)}, u32[]{:S(2)}) collective-permute-start(bf16[72,4224]{1,0:T(8,128)(2,1)S(1)} %get-tuple-element.106), channel_id=1, source_target_pairs={{0,2},{1,3},{2,0},{3,1},{4,6},{5,7},{6,4},{7,5},{8,10},{9,11},{10,... | collective-permute-start | bytes 1824776 | tf_op jit(solution)/shard_map/ppermute | solution.py:272
  32.2 24.6 %collective-permute-start.10 = (bf16[128,4224]{1,0:T(8,128)(2,1)}, bf16[128,4224]{1,0:T(8,128)(2,1)S(1)}, u32[]{:S(2)}, u32[]{:S(2)}) collective-permute-start(bf16[128,4224]{1,0:T(8,128)(2,1)} %collective-permute-done.3.refs_1_), channel_id=1, source_target_pairs={{0,4},{1,5},{2,6},{3,7},{4,0},{5,1},{6,2},{7,3},{8,12},{9,13},{10,... | collective-permute-start | bytes 3244040 | tf_op jit(solution)/shard_map/ppermute | solution.py:272
  32.3 26.5 %collective-permute-start.9 = (bf16[128,4224]{1,0:T(8,128)(2,1)}, bf16[128,4224]{1,0:T(8,128)(2,1)S(1)}, u32[]{:S(2)}, u32[]{:S(2)}) collective-permute-start(bf16[128,4224]{1,0:T(8,128)(2,1)} %collective-permute-done.2.refs_1_), channel_id=1, source_target_pairs={{4,8},{5,9},{6,10},{7,11},{8,4},{9,5},{10,6},{11,7},{20,24},{21,25... | collective-permute-start | bytes 3244040 | tf_op jit(solution)/shard_map/ppermute | solution.py:272
  34.5 4.1 %collective-permute-start = (bf16[72,4224]{1,0:T(8,128)(2,1)S(1)}, bf16[72,4224]{1,0:T(8,128)(2,1)S(1)}, u32[]{:S(2)}, u32[]{:S(2)}) collective-permute-start(bf16[72,4224]{1,0:T(8,128)(2,1)S(1)} %get-tuple-element.105.refs_0_), channel_id=1, source_target_pairs={{0,1},{1,0},{2,3},{3,2},{4,5},{5,4},{6,7},{7,6},{8,9},{9,8},{10,11... | collective-permute-start | bytes 1824776 | tf_op jit(solution)/shard_map/ppermute | solution.py:272
  36.4 2.2 %collective-permute-start.4 = (bf16[72,4224]{1,0:T(8,128)(2,1)S(1)}, bf16[72,4224]{1,0:T(8,128)(2,1)S(1)}, u32[]{:S(2)}, u32[]{:S(2)}) collective-permute-start(bf16[72,4224]{1,0:T(8,128)(2,1)S(1)} %collective-permute-done.1.refs_2_), channel_id=1, source_target_pairs={{0,1},{1,0},{2,3},{3,2},{4,5},{5,4},{6,7},{7,6},{8,9},{9,8},{10,11... | collective-permute-start | bytes 1824776 | tf_op jit(solution)/shard_map/ppermute | solution.py:272
  37.0 23.1 %collective-permute-start.8 = (bf16[72,4224]{1,0:T(8,128)(2,1)S(1)}, bf16[72,4224]{1,0:T(8,128)(2,1)S(1)}, u32[]{:S(2)}, u32[]{:S(2)}) collective-permute-start(bf16[72,4224]{1,0:T(8,128)(2,1)S(1)} %get-tuple-element.124), channel_id=1, source_target_pairs={{0,2},{1,3},{2,0},{3,1},{4,6},{5,7},{6,4},{7,5},{8,10},{9,11},{10,... | collective-permute-start | bytes 1824776 | tf_op jit(solution)/shard_map/ppermute | solution.py:272
  38.5 23.5 %collective-permute-start.7 = (bf16[72,4224]{1,0:T(8,128)(2,1)S(1)}, bf16[72,4224]{1,0:T(8,128)(2,1)S(1)}, u32[]{:S(2)}, u32[]{:S(2)}) collective-permute-start(bf16[72,4224]{1,0:T(8,128)(2,1)S(1)} %get-tuple-element.123.refs_0_.refs_4_), channel_id=1, source_target_pairs={{0,1},{1,0},{2,3},{3,2},{4,5},{5,4},{6,7},{7,6},{8,9},{9,8},{10,11... | collective-permute-start | bytes 1824776 | tf_op jit(solution)/shard_map/ppermute | solution.py:272
  60.1 2.1 %collective-permute-start.11 = (bf16[72,4224]{1,0:T(8,128)(2,1)S(1)}, bf16[72,4224]{1,0:T(8,128)(2,1)S(1)}, u32[]{:S(2)}, u32[]{:S(2)}) collective-permute-start(bf16[72,4224]{1,0:T(8,128)(2,1)S(1)} %collective-permute-done.8.refs_2_.refs_6_), channel_id=1, source_target_pairs={{0,1},{1,0},{2,3},{3,2},{4,5},{5,4},{6,7},{7,6},{8,9},{9,8},{10,11... | collective-permute-start | bytes 1824776 | tf_op jit(solution)/shard_map/ppermute | solution.py:272
  60.2 16.1 %collective-permute-start.13 = (bf16[72,4224]{1,0:T(8,128)(2,1)S(1)}, bf16[72,4224]{1,0:T(8,128)(2,1)S(1)}, u32[]{:S(2)}, u32[]{:S(2)}) collective-permute-start(bf16[72,4224]{1,0:T(8,128)(2,1)S(1)} %get-tuple-element.133), channel_id=1, source_target_pairs={{0,2},{1,3},{2,0},{3,1},{4,6},{5,7},{6,4},{7,5},{8,10},{9,11},{10,... | collective-permute-start | bytes 1824776 | tf_op jit(solution)/shard_map/ppermute | solution.py:272
  61.8 25.9 %collective-permute-start.15 = (bf16[128,4224]{1,0:T(8,128)(2,1)S(1)}, bf16[128,4224]{1,0:T(8,128)(2,1)S(1)}, u32[]{:S(2)}, u32[]{:S(2)}) collective-permute-start(bf16[128,4224]{1,0:T(8,128)(2,1)S(1)} %collective-permute-done.9.refs_1_), channel_id=1, source_target_pairs={{0,4},{1,5},{2,6},{3,7},{4,0},{5,1},{6,2},{7,3},{8,12},{9,13},{10,... | collective-permute-start | bytes 3244040 | tf_op jit(solution)/shard_map/ppermute | solution.py:272
  61.8 14.6 %collective-permute-start.12 = (bf16[72,4224]{1,0:T(8,128)(2,1)S(1)}, bf16[72,4224]{1,0:T(8,128)(2,1)S(1)}, u32[]{:S(2)}, u32[]{:S(2)}) collective-permute-start(bf16[72,4224]{1,0:T(8,128)(2,1)S(1)} %get-tuple-element.132.refs_0_.refs_8_), channel_id=1, source_target_pairs={{0,1},{1,0},{2,3},{3,2},{4,5},{5,4},{6,7},{7,6},{8,9},{9,8},{10,11... | collective-permute-start | bytes 1824776 | tf_op jit(solution)/shard_map/ppermute | solution.py:272
  76.4 2.0 %collective-permute-start.14 = (bf16[72,4224]{1,0:T(8,128)(2,1)S(1)}, bf16[72,4224]{1,0:T(8,128)(2,1)S(1)}, u32[]{:S(2)}, u32[]{:S(2)}) collective-permute-start(bf16[72,4224]{1,0:T(8,128)(2,1)S(1)} %collective-permute-done.13.refs_2_.refs_10_), channel_id=1, source_target_pairs={{0,1},{1,0},{2,3},{3,2},{4,5},{5,4},{6,7},{7,6},{8,9},{9,8},{10,11... | collective-permute-start | bytes 1824776 | tf_op jit(solution)/shard_map/ppermute | solution.py:272
  83.5 10.3 %collective-permute-start.19 = (bf16[72,2176]{1,0:T(8,128)(2,1)S(1)}, bf16[72,2176]{1,0:T(8,128)(2,1)S(1)}, u32[]{:S(2)}, u32[]{:S(2)}) collective-permute-start(bf16[72,2176]{1,0:T(8,128)(2,1)S(1)} %get-tuple-element.145), channel_id=1, source_target_pairs={{0,2},{1,3},{2,0},{3,1},{4,6},{5,7},{6,4},{7,5},{8,10},{9,11},{10,... | collective-permute-start | bytes 940040 | tf_op jit(solution)/shard_map/ppermute | solution.py:272
  89.9 16.2 %collective-permute-start.17 = (bf16[72,4224]{1,0:T(8,128)(2,1)S(1)}, bf16[72,4224]{1,0:T(8,128)(2,1)S(1)}, u32[]{:S(2)}, u32[]{:S(2)}) collective-permute-start(bf16[72,4224]{1,0:T(8,128)(2,1)S(1)} %get-tuple-element.142), channel_id=1, source_target_pairs={{0,2},{1,3},{2,0},{3,1},{4,6},{5,7},{6,4},{7,5},{8,10},{9,11},{10,... | collective-permute-start | bytes 1824776 | tf_op jit(solution)/shard_map/ppermute | solution.py:272
  90.4 3.4 %collective-permute-start.18 = (bf16[72,2176]{1,0:T(8,128)(2,1)S(1)}, bf16[72,2176]{1,0:T(8,128)(2,1)S(1)}, u32[]{:S(2)}, u32[]{:S(2)}) collective-permute-start(bf16[72,2176]{1,0:T(8,128)(2,1)S(1)} %get-tuple-element.144.refs_2_), channel_id=1, source_target_pairs={{0,1},{1,0},{2,3},{3,2},{4,5},{5,4},{6,7},{7,6},{8,9},{9,8},{10,11... | collective-permute-start | bytes 940040 | tf_op jit(solution)/shard_map/ppermute | solution.py:272
  93.8 1.6 %collective-permute-start.20 = (bf16[72,2176]{1,0:T(8,128)(2,1)S(1)}, bf16[72,2176]{1,0:T(8,128)(2,1)S(1)}, u32[]{:S(2)}, u32[]{:S(2)}) collective-permute-start(bf16[72,2176]{1,0:T(8,128)(2,1)S(1)} %collective-permute-done.19.refs_4_), channel_id=1, source_target_pairs={{0,1},{1,0},{2,3},{3,2},{4,5},{5,4},{6,7},{7,6},{8,9},{9,8},{10,11... | collective-permute-start | bytes 940040 | tf_op jit(solution)/shard_map/ppermute | solution.py:272
  96.6 7.6 %collective-permute-start.21 = (bf16[128,640]{1,0:T(8,128)(2,1)S(1)}, bf16[128,640]{1,0:T(8,128)(2,1)S(1)}, u32[]{:S(2)}, u32[]{:S(2)}) collective-permute-start(bf16[128,640]{1,0:T(8,128)(2,1)S(1)} %get-tuple-element.149), channel_id=1, source_target_pairs={{0,8},{1,9},{2,10},{3,11},{4,12},{5,13},{6,14},{7,15},{8,0},{9,1},... | collective-permute-start | bytes 491528 | tf_op jit(solution)/shard_map/ppermute | solution.py:272
  96.7 12.5 %collective-permute-start.16 = (bf16[72,4224]{1,0:T(8,128)(2,1)S(1)}, bf16[72,4224]{1,0:T(8,128)(2,1)S(1)}, u32[]{:S(2)}, u32[]{:S(2)}) collective-permute-start(bf16[72,4224]{1,0:T(8,128)(2,1)S(1)} %get-tuple-element.141.refs_0_.refs_12_), channel_id=1, source_target_pairs={{0,1},{1,0},{2,3},{3,2},{4,5},{5,4},{6,7},{7,6},{8,9},{9,8},{10,11... | collective-permute-start | bytes 1824776 | tf_op jit(solution)/shard_map/ppermute | solution.py:272
  106.1 3.1 %collective-permute-start.22 = (bf16[72,4224]{1,0:T(8,128)(2,1)S(1)}, bf16[72,4224]{1,0:T(8,128)(2,1)S(1)}, u32[]{:S(2)}, u32[]{:S(2)}) collective-permute-start(bf16[72,4224]{1,0:T(8,128)(2,1)S(1)} %collective-permute-done.17.refs_2_.refs_14_), channel_id=1, source_target_pairs={{0,1},{1,0},{2,3},{3,2},{4,5},{5,4},{6,7},{7,6},{8,9},{9,8},{10,11... | collective-permute-start | bytes 1824776 | tf_op jit(solution)/shard_map/ppermute | solution.py:272
  106.1 9.8 %collective-permute-start.27 = (bf16[72,2176]{1,0:T(8,128)(2,1)S(1)}, bf16[72,2176]{1,0:T(8,128)(2,1)S(1)}, u32[]{:S(2)}, u32[]{:S(2)}) collective-permute-start(bf16[72,2176]{1,0:T(8,128)(2,1)S(1)} %get-tuple-element.168), channel_id=1, source_target_pairs={{0,2},{1,3},{2,0},{3,1},{4,6},{5,7},{6,4},{7,5},{8,10},{9,11},{10,... | collective-permute-start | bytes 940040 | tf_op jit(solution)/shard_map/ppermute | solution.py:272
  107.6 18.7 %collective-permute-start.25 = (bf16[128,1536]{1,0:T(8,128)(2,1)S(1)}, bf16[128,1536]{1,0:T(8,128)(2,1)S(1)}, u32[]{:S(2)}, u32[]{:S(2)}) collective-permute-start(bf16[128,1536]{1,0:T(8,128)(2,1)S(1)} %get-tuple-element.165), channel_id=1, source_target_pairs={{0,8},{1,9},{2,10},{3,11},{4,12},{5,13},{6,14},{7,15},{8,0},{9,1},... | collective-permute-start | bytes 1179656 | tf_op jit(solution)/shard_map/ppermute | solution.py:272
  109.1 8.5 %collective-permute-start.26 = (bf16[72,2176]{1,0:T(8,128)(2,1)S(1)}, bf16[72,2176]{1,0:T(8,128)(2,1)S(1)}, u32[]{:S(2)}, u32[]{:S(2)}) collective-permute-start(bf16[72,2176]{1,0:T(8,128)(2,1)S(1)} %get-tuple-element.167.refs_2_), channel_id=1, source_target_pairs={{0,1},{1,0},{2,3},{3,2},{4,5},{5,4},{6,7},{7,6},{8,9},{9,8},{10,11... | collective-permute-start | bytes 940040 | tf_op jit(solution)/shard_map/ppermute | solution.py:272
  115.9 1.8 %collective-permute-start.28 = (bf16[72,2176]{1,0:T(8,128)(2,1)S(1)}, bf16[72,2176]{1,0:T(8,128)(2,1)S(1)}, u32[]{:S(2)}, u32[]{:S(2)}) collective-permute-start(bf16[72,2176]{1,0:T(8,128)(2,1)S(1)} %collective-permute-done.27.refs_4_), channel_id=1, source_target_pairs={{0,1},{1,0},{2,3},{3,2},{4,5},{5,4},{6,7},{7,6},{8,9},{9,8},{10,11... | collective-permute-start | bytes 940040 | tf_op jit(solution)/shard_map/ppermute | solution.py:272
  115.9 10.4 %collective-permute-start.24 = (bf16[72,2176]{1,0:T(8,128)(2,1)S(1)}, bf16[72,2176]{1,0:T(8,128)(2,1)S(1)}, u32[]{:S(2)}, u32[]{:S(2)}) collective-permute-start(bf16[72,2176]{1,0:T(8,128)(2,1)S(1)} %get-tuple-element.164), channel_id=1, source_target_pairs={{0,2},{1,3},{2,0},{3,1},{4,6},{5,7},{6,4},{7,5},{8,10},{9,11},{10,... | collective-permute-start | bytes 940040 | tf_op jit(solution)/shard_map/ppermute | solution.py:272
  117.4 11.9 %collective-permute-start.23 = (bf16[72,2176]{1,0:T(8,128)(2,1)S(1)}, bf16[72,2176]{1,0:T(8,128)(2,1)S(1)}, u32[]{:S(2)}, u32[]{:S(2)}) collective-permute-start(bf16[72,2176]{1,0:T(8,128)(2,1)S(1)} %get-tuple-element.163.refs_2_), channel_id=1, source_target_pairs={{0,1},{1,0},{2,3},{3,2},{4,5},{5,4},{6,7},{7,6},{8,9},{9,8},{10,11... | collective-permute-start | bytes 940040 | tf_op jit(solution)/shard_map/ppermute | solution.py:272
  126.3 3.1 %collective-permute-start.29 = (bf16[72,2176]{1,0:T(8,128)(2,1)S(1)}, bf16[72,2176]{1,0:T(8,128)(2,1)S(1)}, u32[]{:S(2)}, u32[]{:S(2)}) collective-permute-start(bf16[72,2176]{1,0:T(8,128)(2,1)S(1)} %collective-permute-done.24.refs_4_), channel_id=1, source_target_pairs={{0,1},{1,0},{2,3},{3,2},{4,5},{5,4},{6,7},{7,6},{8,9},{9,8},{10,11... | collective-permute-start | bytes 940040 | tf_op jit(solution)/shard_map/ppermute | solution.py:272
  126.4 9.8 %collective-permute-start.6 = (bf16[72,2176]{1,0:T(8,128)(2,1)S(1)}, bf16[72,2176]{1,0:T(8,128)(2,1)S(1)}, u32[]{:S(2)}, u32[]{:S(2)}) collective-permute-start(bf16[72,2176]{1,0:T(8,128)(2,1)S(1)} %get-tuple-element.122), channel_id=1, source_target_pairs={{0,2},{1,3},{2,0},{3,1},{4,6},{5,7},{6,4},{7,5},{8,10},{9,11},{10,... | collective-permute-start | bytes 940040 | tf_op jit(solution)/shard_map/ppermute | solution.py:272
  127.2 15.5 %collective-permute-start.31 = (bf16[128,2176]{1,0:T(8,128)(2,1)S(1)}, bf16[128,2176]{1,0:T(8,128)(2,1)S(1)}, u32[]{:S(2)}, u32[]{:S(2)}) collective-permute-start(bf16[128,2176]{1,0:T(8,128)(2,1)S(1)} %get-tuple-element.181), channel_id=1, source_target_pairs={{0,4},{1,5},{2,6},{3,7},{4,0},{5,1},{6,2},{7,3},{8,12},{9,13},{10,... | collective-permute-start | bytes 1671176 | tf_op jit(solution)/shard_map/ppermute | solution.py:272
  130.5 26.5 %collective-permute-start.32 = (bf16[128,2176]{1,0:T(8,128)(2,1)S(1)}, bf16[128,2176]{1,0:T(8,128)(2,1)S(1)}, u32[]{:S(2)}, u32[]{:S(2)}) collective-permute-start(bf16[128,2176]{1,0:T(8,128)(2,1)S(1)} %get-tuple-element.186), channel_id=1, source_target_pairs={{0,12},{1,13},{2,14},{3,15},{4,8},{5,9},{6,10},{7,11},{8,4},{9,5},... | collective-permute-start | bytes 1671176 | tf_op jit(solution)/shard_map/ppermute | solution.py:272
  132.0 4.1 %collective-permute-start.5 = (bf16[72,2176]{1,0:T(8,128)(2,1)S(1)}, bf16[72,2176]{1,0:T(8,128)(2,1)S(1)}, u32[]{:S(2)}, u32[]{:S(2)}) collective-permute-start(bf16[72,2176]{1,0:T(8,128)(2,1)S(1)} %get-tuple-element.121.refs_2_), channel_id=1, source_target_pairs={{0,1},{1,0},{2,3},{3,2},{4,5},{5,4},{6,7},{7,6},{8,9},{9,8},{10,11... | collective-permute-start | bytes 940040 | tf_op jit(solution)/shard_map/ppermute | solution.py:272
  (12 other events, 50.4 us)

commit v6 on v5

--- a/solution.py
+++ b/solution.py
@@ -79,13 +79,9 @@
 
 def select_kernel(routes, half, choices, stage, info_ref, *refs):
     blocks, outs, side_ref = refs[:choices], refs[choices:-1], refs[-1]
-    block = blocks[0]
+    block = blocks[0][...]
     for i in range(1, choices):
-
-        @pl.when(info_ref[PLANE + stage] == i)
-        def _():
-            block[...] = blocks[i][...]
-
+        block = jnp.where(info_ref[PLANE + stage] == i, blocks[i][...], block)
     width = (block.shape[1] - LANES) // 2
     side_ref[...] = block[:, 2 * width :]
     side = block[:, 2 * width :].astype(F32)

time: 160 us -> 160 us (level)
  no operation moved by 1% of the time
where the time goes in v6:
time: 160 us; the launch traced here: 158 us
  waiting for transfers between devices  85.1 us (53%)
  Pallas kernels  38 us (24%)
  starting transfers between devices  23.1 us (14%)
  local copies, waits for them, and re-layouts  10.9 us (7%)
    ppermute x33, waiting for transfers between devices, flipped(): return lax.ppermute(value, 'expert', pairs)  85.1 us
    pallas_call x17, Pallas kernels, kernel(): pl.pallas_call(run, out_shape=[*outs, shape((8, LANES), F32)], in_specs=[...  38 us
    ppermute x33, starting transfers between devices, flipped(): return lax.ppermute(value, 'expert', pairs)  23.1 us
    unnamed x22, local copies, waits for them, and re-layouts  10.8 us
  transfers between devices with their start and end apart: 33, of which 19 were waited for; matrix products, arithmetic and copies ran while one was open for 0% of the time, Pallas kernels for 22%

profile of v6, /device:TPU:16, one launch (start us, length us, event | category | flops | bytes accessed | tf_op | source)
XLA Modules:
  0.0 158.1 jit_solution(7481177872649677296)
XLA Ops:
  0.6 2.4 %pack.1 = (bf16[128,4224]{1,0:T(8,128)(2,1)}, f32[8,128]{1,0:T(8,128)}) custom-call(bf16[128,2048]{1,0:T(8,128)(2,1)} %refs_0_.1, bf16[128,2048]{1,0:T(8,128)(2,1)} %refs_1_.1, s32[4,128]{1,0:T(4,128)} %bitcast.35, f32[4,128]{1,0:T(4,128)} %bitcast.36), custom_call_target="tpu_custom_call" | custom-call | flops 1 | bytes 6000000 | tf_op jit(solution)/shard_map/pack/pallas_call | solution.py:278
  3.1 1.6 %collective-permute-start.2 = (bf16[128,4224]{1,0:T(8,128)(2,1)}, bf16[128,4224]{1,0:T(8,128)(2,1)}, u32[]{:S(2)}, u32[]{:S(2)}) collective-permute-start(bf16[128,4224]{1,0:T(8,128)(2,1)} %get-tuple-element.102.refs_1_), channel_id=1, source_target_pairs={{0,4},{1,5},{2,6},{3,7},{4,0},{5,1},{6,2},{7,3},{8,12},{9,13},{10,... | collective-permute-start | bytes 3244040 | tf_op jit(solution)/shard_map/ppermute | solution.py:268
  4.7 1.9 %collective-permute-start.3 = (bf16[128,4224]{1,0:T(8,128)(2,1)}, bf16[128,4224]{1,0:T(8,128)(2,1)}, u32[]{:S(2)}, u32[]{:S(2)}) collective-permute-start(bf16[128,4224]{1,0:T(8,128)(2,1)} %get-tuple-element.102.refs_1_), channel_id=1, source_target_pairs={{4,8},{5,9},{6,10},{7,11},{8,4},{9,5},{10,6},{11,7},{20,24},{21,25... | collective-permute-start | bytes 3244040 | tf_op jit(solution)/shard_map/ppermute | solution.py:268
  9.9 1.6 %collective-permute-start.1 = (bf16[72,4224]{1,0:T(8,128)(2,1)S(1)}, bf16[72,4224]{1,0:T(8,128)(2,1)S(1)}, u32[]{:S(2)}, u32[]{:S(2)}) collective-permute-start(bf16[72,4224]{1,0:T(8,128)(2,1)S(1)} %get-tuple-element.106), channel_id=1, source_target_pairs={{0,2},{1,3},{2,0},{3,1},{4,6},{5,7},{6,4},{7,5},{8,10},{9,11},{10,... | collective-permute-start | bytes 1824776 | tf_op jit(solution)/shard_map/ppermute | solution.py:268
  17.1 12.0 %collective-permute-done.2.refs_1_ = bf16[128,4224]{1,0:T(8,128)(2,1)} collective-permute-done((bf16[128,4224]{1,0:T(8,128)(2,1)}, bf16[128,4224]{1,0:T(8,128)(2,1)}, u32[]{:S(2)}, u32[]{:S(2)}) %collective-permute-start.2) | collective-permute-done | bytes 1081376 | tf_op jit(solution)/shard_map/ppermute | solution.py:268
  29.1 3.2 %collective-permute-done.3.refs_1_ = bf16[128,4224]{1,0:T(8,128)(2,1)} collective-permute-done((bf16[128,4224]{1,0:T(8,128)(2,1)}, bf16[128,4224]{1,0:T(8,128)(2,1)}, u32[]{:S(2)}, u32[]{:S(2)}) %collective-permute-start.3) | collective-permute-done | bytes 1081376 | tf_op jit(solution)/shard_map/ppermute | solution.py:268
  32.3 2.2 %collective-permute-start.9 = (bf16[128,4224]{1,0:T(8,128)(2,1)}, bf16[128,4224]{1,0:T(8,128)(2,1)S(1)}, u32[]{:S(2)}, u32[]{:S(2)}) collective-permute-start(bf16[128,4224]{1,0:T(8,128)(2,1)} %collective-permute-done.2.refs_1_), channel_id=1, source_target_pairs={{4,8},{5,9},{6,10},{7,11},{8,4},{9,5},{10,6},{11,7},{20,24},{21,25... | collective-permute-start | bytes 3244040 | tf_op jit(solution)/shard_map/ppermute | solution.py:268
  34.5 1.9 %select.11 = (bf16[72,4224]{1,0:T(8,128)(2,1)S(1)}, bf16[72,4224]{1,0:T(8,128)(2,1)S(1)}, bf16[128,128]{1,0:T(8,128)(2,1)S(1)}, f32[8,128]{1,0:T(8,128)S(1)}) custom-call(s32[8]{0:T(128)S(1)} %stack.28.refs_0_, bf16[128,4224]{1,0:T(8,128)(2,1)} %collective-permute-done.2.refs_1_, f32[8,128]{1,0:T(8,128)S(1)} %get-tuple-element.110.refs_2_), custom_call_target="tpu_custom_call" | custom-call | flops 1 | bytes 12000000 | tf_op jit(solution)/shard_map/select/pallas_call | solution.py:278
  38.7 1.9 %copy-done.1 = bf16[1,2048,768]{2,1,0:T(8,128)(2,1)S(1)} copy-done((bf16[1,2048,768]{2,1,0:T(8,128)(2,1)S(1)}, bf16[1,2048,768]{2,1,0:T(8,128)(2,1)}, u32[]{:S(2)}) %copy-start.1) | copy-done | bytes 3145752
  40.5 1.9 %copy-done.2 = bf16[1,768,2048]{2,1,0:T(8,128)(2,1)S(1)} copy-done((bf16[1,768,2048]{2,1,0:T(8,128)(2,1)S(1)}, bf16[1,768,2048]{2,1,0:T(8,128)(2,1)}, u32[]{:S(2)}) %copy-start.2) | copy-done | bytes 3145752
  42.4 5.2 %expert.4 = (bf16[72,2176]{1,0:T(8,128)(2,1)S(1)}, bf16[72,2176]{1,0:T(8,128)(2,1)S(1)}, bf16[144,2304]{1,0:T(8,128)(2,1)S(1)}, bf16[144,512]{1,0:T(8,128)(2,1)S(1)}, f32[8,128]{1,0:T(8,128)S(1)}) custom-call(bf16[72,4224]{1,0:T(8,128)(2,1)S(1)} %get-tuple-element.105.refs_0_, bf16[72,4224]{1,0:T(8,128)(2,1)S(1)} %collective-permute-done.refs_1_, ...), custom_call_target="tpu_custom_call" | custom-call | flops 1 | bytes 24000000 | tf_op jit(solution)/shard_map/expert/pallas_call | solution.py:278
  47.6 9.3 %collective-permute-done.10.refs_2_ = bf16[128,4224]{1,0:T(8,128)(2,1)S(1)} collective-permute-done((bf16[128,4224]{1,0:T(8,128)(2,1)}, bf16[128,4224]{1,0:T(8,128)(2,1)S(1)}, u32[]{:S(2)}, u32[]{:S(2)}) %collective-permute-start.10) | collective-permute-done | bytes 1081376 | tf_op jit(solution)/shard_map/ppermute | solution.py:268
  56.9 1.9 %collective-permute-done.9.refs_1_ = bf16[128,4224]{1,0:T(8,128)(2,1)S(1)} collective-permute-done((bf16[128,4224]{1,0:T(8,128)(2,1)}, bf16[128,4224]{1,0:T(8,128)(2,1)S(1)}, u32[]{:S(2)}, u32[]{:S(2)}) %collective-permute-start.9) | collective-permute-done | bytes 1081376 | tf_op jit(solution)/shard_map/ppermute | solution.py:268
  62.1 5.1 %expert.5 = (bf16[72,2176]{1,0:T(8,128)(2,1)S(1)}, bf16[72,2176]{1,0:T(8,128)(2,1)S(1)}, bf16[144,2304]{1,0:T(8,128)(2,1)S(1)}, bf16[144,512]{1,0:T(8,128)(2,1)S(1)}, f32[8,128]{1,0:T(8,128)S(1)}) custom-call(bf16[72,4224]{1,0:T(8,128)(2,1)S(1)} %get-tuple-element.123.refs_0_.refs_4_, bf16[72,4224]{1,0:T(8,128)(2,1)S(1)} %collective-permute-done.7.refs_1_.refs_5_, ...), custom_call_target="tpu_custom_call" | custom-call | flops 1 | bytes 24000000 | tf_op jit(solution)/shard_map/expert/pallas_call | solution.py:278
  67.2 9.0 %collective-permute-done.13.refs_2_.refs_10_ = bf16[72,4224]{1,0:T(8,128)(2,1)S(1)} collective-permute-done((bf16[72,4224]{1,0:T(8,128)(2,1)S(1)}, bf16[72,4224]{1,0:T(8,128)(2,1)S(1)}, u32[]{:S(2)}, u32[]{:S(2)}) %collective-permute-start.13) | collective-permute-done | bytes 608288 | tf_op jit(solution)/shard_map/ppermute | solution.py:268
  76.2 2.0 %collective-permute-done.14.refs_3_.refs_11_ = bf16[72,4224]{1,0:T(8,128)(2,1)S(1)} collective-permute-done((bf16[72,4224]{1,0:T(8,128)(2,1)S(1)}, bf16[72,4224]{1,0:T(8,128)(2,1)S(1)}, u32[]{:S(2)}, u32[]{:S(2)}) %collective-permute-start.14) | collective-permute-done | bytes 608288 | tf_op jit(solution)/shard_map/ppermute | solution.py:268
  78.2 5.3 %expert.6 = (bf16[72,2176]{1,0:T(8,128)(2,1)S(1)}, bf16[72,2176]{1,0:T(8,128)(2,1)S(1)}, bf16[144,2304]{1,0:T(8,128)(2,1)S(1)}, bf16[144,512]{1,0:T(8,128)(2,1)S(1)}, f32[8,128]{1,0:T(8,128)S(1)}) custom-call(bf16[72,4224]{1,0:T(8,128)(2,1)S(1)} %get-tuple-element.132.refs_0_.refs_8_, bf16[72,4224]{1,0:T(8,128)(2,1)S(1)} %collective-permute-done.12.refs_1_.refs_9_, ...), custom_call_target="tpu_custom_call" | custom-call | flops 1 | bytes 24000000 | tf_op jit(solution)/shard_map/expert/pallas_call | solution.py:278
  85.1 2.4 %collective-permute-done.15.refs_2_ = bf16[128,4224]{1,0:T(8,128)(2,1)S(1)} collective-permute-done((bf16[128,4224]{1,0:T(8,128)(2,1)S(1)}, bf16[128,4224]{1,0:T(8,128)(2,1)S(1)}, u32[]{:S(2)}, u32[]{:S(2)}) %collective-permute-start.15) | collective-permute-done | bytes 1081376 | tf_op jit(solution)/shard_map/ppermute | solution.py:268
  87.6 1.9 %select.13 = (bf16[72,4224]{1,0:T(8,128)(2,1)S(1)}, bf16[72,4224]{1,0:T(8,128)(2,1)S(1)}, bf16[128,128]{1,0:T(8,128)(2,1)S(1)}, f32[8,128]{1,0:T(8,128)S(1)}) custom-call(s32[8]{0:T(128)S(1)} %stack.28.refs_0_, bf16[128,4224]{1,0:T(8,128)(2,1)} %collective-permute-done.3.refs_1_, bf16[128,4224]{1,0:T(8,128)(2,1)S(1)} %collective-permute-done.15.refs_2_, ...), custom_call_target="tpu_custom_call" | custom-call | flops 1 | bytes 12000000 | tf_op jit(solution)/shard_map/select/pallas_call | solution.py:278
  90.0 3.8 %collective-permute-done.19.refs_4_ = bf16[72,2176]{1,0:T(8,128)(2,1)S(1)} collective-permute-done((bf16[72,2176]{1,0:T(8,128)(2,1)S(1)}, bf16[72,2176]{1,0:T(8,128)(2,1)S(1)}, u32[]{:S(2)}, u32[]{:S(2)}) %collective-permute-start.19) | collective-permute-done | bytes 313376 | tf_op jit(solution)/shard_map/ppermute | solution.py:268
  93.9 1.6 %collective-permute-done.20.refs_5_ = bf16[72,2176]{1,0:T(8,128)(2,1)S(1)} collective-permute-done((bf16[72,2176]{1,0:T(8,128)(2,1)S(1)}, bf16[72,2176]{1,0:T(8,128)(2,1)S(1)}, u32[]{:S(2)}, u32[]{:S(2)}) %collective-permute-start.20) | collective-permute-done | bytes 313376 | tf_op jit(solution)/shard_map/ppermute | solution.py:268
  96.9 7.3 %collective-permute-done.21.refs_2_ = bf16[128,640]{1,0:T(8,128)(2,1)S(1)} collective-permute-done((bf16[128,640]{1,0:T(8,128)(2,1)S(1)}, bf16[128,640]{1,0:T(8,128)(2,1)S(1)}, u32[]{:S(2)}, u32[]{:S(2)}) %collective-permute-start.21) | collective-permute-done | bytes 163872 | tf_op jit(solution)/shard_map/ppermute | solution.py:268
  104.2 1.9 %collective-permute-done.17.refs_2_.refs_14_ = bf16[72,4224]{1,0:T(8,128)(2,1)S(1)} collective-permute-done((bf16[72,4224]{1,0:T(8,128)(2,1)S(1)}, bf16[72,4224]{1,0:T(8,128)(2,1)S(1)}, u32[]{:S(2)}, u32[]{:S(2)}) %collective-permute-start.17) | collective-permute-done | bytes 608288 | tf_op jit(solution)/shard_map/ppermute | solution.py:268
  109.2 5.1 %expert.7 = (bf16[72,2176]{1,0:T(8,128)(2,1)S(1)}, bf16[72,2176]{1,0:T(8,128)(2,1)S(1)}, bf16[144,2304]{1,0:T(8,128)(2,1)S(1)}, bf16[144,512]{1,0:T(8,128)(2,1)S(1)}, f32[8,128]{1,0:T(8,128)S(1)}) custom-call(bf16[72,4224]{1,0:T(8,128)(2,1)S(1)} %get-tuple-element.141.refs_0_.refs_12_, bf16[72,4224]{1,0:T(8,128)(2,1)S(1)} %collective-permute-done.16.refs_1_.refs_13_, ...), custom_call_target="tpu_custom_call" | custom-call | flops 1 | bytes 24000000 | tf_op jit(solution)/shard_map/expert/pallas_call | solution.py:278
  114.3 1.6 %collective-permute-done.27.refs_4_ = bf16[72,2176]{1,0:T(8,128)(2,1)S(1)} collective-permute-done((bf16[72,2176]{1,0:T(8,128)(2,1)S(1)}, bf16[72,2176]{1,0:T(8,128)(2,1)S(1)}, u32[]{:S(2)}, u32[]{:S(2)}) %collective-permute-start.27) | collective-permute-done | bytes 313376 | tf_op jit(solution)/shard_map/ppermute | solution.py:268
  118.8 7.5 %collective-permute-done.25.refs_3_ = bf16[128,1536]{1,0:T(8,128)(2,1)S(1)} collective-permute-done((bf16[128,1536]{1,0:T(8,128)(2,1)S(1)}, bf16[128,1536]{1,0:T(8,128)(2,1)S(1)}, u32[]{:S(2)}, u32[]{:S(2)}) %collective-permute-start.25) | collective-permute-done | bytes 393248 | tf_op jit(solution)/shard_map/ppermute | solution.py:268
  127.3 2.1 %collective-permute-start.31 = (bf16[128,2176]{1,0:T(8,128)(2,1)S(1)}, bf16[128,2176]{1,0:T(8,128)(2,1)S(1)}, u32[]{:S(2)}, u32[]{:S(2)}) collective-permute-start(bf16[128,2176]{1,0:T(8,128)(2,1)S(1)} %get-tuple-element.181), channel_id=1, source_target_pairs={{0,4},{1,5},{2,6},{3,7},{4,0},{5,1},{6,2},{7,3},{8,12},{9,13},{10,... | collective-permute-start | bytes 1671176 | tf_op jit(solution)/shard_map/ppermute | solution.py:268
  132.0 2.3 %adapter_grads.1 = (f32[1,32,2048]{2,1,0:T(8,128)}, f32[1,32,768]{2,1,0:T(8,128)}, f32[1,32,2048]{2,1,0:T(8,128)}, f32[1,32,768]{2,1,0:T(8,128)}, f32[1,32,768]{...) custom-call(bf16[72,4224]{1,0:T(8,128)(2,1)S(1)} %get-tuple-element.105.refs_0_, ...), custom_call_target="tpu_custom_call" | custom-call | flops 1 | bytes 15000000 | tf_op jit(solution)/shard_map/adapter_grads/pallas_call | solution.py:278
  134.4 1.8 %collective-permute-done.6.refs_4_ = bf16[72,2176]{1,0:T(8,128)(2,1)S(1)} collective-permute-done((bf16[72,2176]{1,0:T(8,128)(2,1)S(1)}, bf16[72,2176]{1,0:T(8,128)(2,1)S(1)}, u32[]{:S(2)}, u32[]{:S(2)}) %collective-permute-start.6) | collective-permute-done | bytes 313376 | tf_op jit(solution)/shard_map/ppermute | solution.py:268
  136.1 1.6 %collective-permute-done.30.refs_5_ = bf16[72,2176]{1,0:T(8,128)(2,1)S(1)} collective-permute-done((bf16[72,2176]{1,0:T(8,128)(2,1)S(1)}, bf16[72,2176]{1,0:T(8,128)(2,1)S(1)}, u32[]{:S(2)}, u32[]{:S(2)}) %collective-permute-start.30) | collective-permute-done | bytes 313376 | tf_op jit(solution)/shard_map/ppermute | solution.py:268
  138.9 3.9 %collective-permute-done.31.refs_1_ = bf16[128,2176]{1,0:T(8,128)(2,1)S(1)} collective-permute-done((bf16[128,2176]{1,0:T(8,128)(2,1)S(1)}, bf16[128,2176]{1,0:T(8,128)(2,1)S(1)}, u32[]{:S(2)}, u32[]{:S(2)}) %collective-permute-start.31) | collective-permute-done | bytes 557088 | tf_op jit(solution)/shard_map/ppermute | solution.py:268
  143.0 14.0 %collective-permute-done.32.refs_1_ = bf16[128,2176]{1,0:T(8,128)(2,1)S(1)} collective-permute-done((bf16[128,2176]{1,0:T(8,128)(2,1)S(1)}, bf16[128,2176]{1,0:T(8,128)(2,1)S(1)}, u32[]{:S(2)}, u32[]{:S(2)}) %collective-permute-start.32) | collective-permute-done | bytes 557088 | tf_op jit(solution)/shard_map/ppermute | solution.py:268
  (75 shorter events, 29.9 us)
Async XLA Ops:
  3.1 26.0 %collective-permute-start.2 = (bf16[128,4224]{1,0:T(8,128)(2,1)}, bf16[128,4224]{1,0:T(8,128)(2,1)}, u32[]{:S(2)}, u32[]{:S(2)}) collective-permute-start(bf16[128,4224]{1,0:T(8,128)(2,1)} %get-tuple-element.102.refs_1_), channel_id=1, source_target_pairs={{0,4},{1,5},{2,6},{3,7},{4,0},{5,1},{6,2},{7,3},{8,12},{9,13},{10,... | collective-permute-start | bytes 3244040 | tf_op jit(solution)/shard_map/ppermute | solution.py:268
  4.7 27.5 %collective-permute-start.3 = (bf16[128,4224]{1,0:T(8,128)(2,1)}, bf16[128,4224]{1,0:T(8,128)(2,1)}, u32[]{:S(2)}, u32[]{:S(2)}) collective-permute-start(bf16[128,4224]{1,0:T(8,128)(2,1)} %get-tuple-element.102.refs_1_), channel_id=1, source_target_pairs={{4,8},{5,9},{6,10},{7,11},{8,4},{9,5},{10,6},{11,7},{20,24},{21,25... | collective-permute-start | bytes 3244040 | tf_op jit(solution)/shard_map/ppermute | solution.py:268
  9.9 26.5 %collective-permute-start.1 = (bf16[72,4224]{1,0:T(8,128)(2,1)S(1)}, bf16[72,4224]{1,0:T(8,128)(2,1)S(1)}, u32[]{:S(2)}, u32[]{:S(2)}) collective-permute-start(bf16[72,4224]{1,0:T(8,128)(2,1)S(1)} %get-tuple-element.106), channel_id=1, source_target_pairs={{0,2},{1,3},{2,0},{3,1},{4,6},{5,7},{6,4},{7,5},{8,10},{9,11},{10,... | collective-permute-start | bytes 1824776 | tf_op jit(solution)/shard_map/ppermute | solution.py:268
  32.2 24.6 %collective-permute-start.10 = (bf16[128,4224]{1,0:T(8,128)(2,1)}, bf16[128,4224]{1,0:T(8,128)(2,1)S(1)}, u32[]{:S(2)}, u32[]{:S(2)}) collective-permute-start(bf16[128,4224]{1,0:T(8,128)(2,1)} %collective-permute-done.3.refs_1_), channel_id=1, source_target_pairs={{0,4},{1,5},{2,6},{3,7},{4,0},{5,1},{6,2},{7,3},{8,12},{9,13},{10,... | collective-permute-start | bytes 3244040 | tf_op jit(solution)/shard_map/ppermute | solution.py:268
  32.3 26.5 %collective-permute-start.9 = (bf16[128,4224]{1,0:T(8,128)(2,1)}, bf16[128,4224]{1,0:T(8,128)(2,1)S(1)}, u32[]{:S(2)}, u32[]{:S(2)}) collective-permute-start(bf16[128,4224]{1,0:T(8,128)(2,1)} %collective-permute-done.2.refs_1_), channel_id=1, source_target_pairs={{4,8},{5,9},{6,10},{7,11},{8,4},{9,5},{10,6},{11,7},{20,24},{21,25... | collective-permute-start | bytes 3244040 | tf_op jit(solution)/shard_map/ppermute | solution.py:268
  34.5 4.1 %collective-permute-start = (bf16[72,4224]{1,0:T(8,128)(2,1)S(1)}, bf16[72,4224]{1,0:T(8,128)(2,1)S(1)}, u32[]{:S(2)}, u32[]{:S(2)}) collective-permute-start(bf16[72,4224]{1,0:T(8,128)(2,1)S(1)} %get-tuple-element.105.refs_0_), channel_id=1, source_target_pairs={{0,1},{1,0},{2,3},{3,2},{4,5},{5,4},{6,7},{7,6},{8,9},{9,8},{10,11... | collective-permute-start | bytes 1824776 | tf_op jit(solution)/shard_map/ppermute | solution.py:268
  36.4 2.2 %collective-permute-start.4 = (bf16[72,4224]{1,0:T(8,128)(2,1)S(1)}, bf16[72,4224]{1,0:T(8,128)(2,1)S(1)}, u32[]{:S(2)}, u32[]{:S(2)}) collective-permute-start(bf16[72,4224]{1,0:T(8,128)(2,1)S(1)} %collective-permute-done.1.refs_2_), channel_id=1, source_target_pairs={{0,1},{1,0},{2,3},{3,2},{4,5},{5,4},{6,7},{7,6},{8,9},{9,8},{10,11... | collective-permute-start | bytes 1824776 | tf_op jit(solution)/shard_map/ppermute | solution.py:268
  37.0 23.0 %collective-permute-start.8 = (bf16[72,4224]{1,0:T(8,128)(2,1)S(1)}, bf16[72,4224]{1,0:T(8,128)(2,1)S(1)}, u32[]{:S(2)}, u32[]{:S(2)}) collective-permute-start(bf16[72,4224]{1,0:T(8,128)(2,1)S(1)} %get-tuple-element.124), channel_id=1, source_target_pairs={{0,2},{1,3},{2,0},{3,1},{4,6},{5,7},{6,4},{7,5},{8,10},{9,11},{10,... | collective-permute-start | bytes 1824776 | tf_op jit(solution)/shard_map/ppermute | solution.py:268
  38.5 23.3 %collective-permute-start.7 = (bf16[72,4224]{1,0:T(8,128)(2,1)S(1)}, bf16[72,4224]{1,0:T(8,128)(2,1)S(1)}, u32[]{:S(2)}, u32[]{:S(2)}) collective-permute-start(bf16[72,4224]{1,0:T(8,128)(2,1)S(1)} %get-tuple-element.123.refs_0_.refs_4_), channel_id=1, source_target_pairs={{0,1},{1,0},{2,3},{3,2},{4,5},{5,4},{6,7},{7,6},{8,9},{9,8},{10,11... | collective-permute-start | bytes 1824776 | tf_op jit(solution)/shard_map/ppermute | solution.py:268
  60.0 2.1 %collective-permute-start.11 = (bf16[72,4224]{1,0:T(8,128)(2,1)S(1)}, bf16[72,4224]{1,0:T(8,128)(2,1)S(1)}, u32[]{:S(2)}, u32[]{:S(2)}) collective-permute-start(bf16[72,4224]{1,0:T(8,128)(2,1)S(1)} %collective-permute-done.8.refs_2_.refs_6_), channel_id=1, source_target_pairs={{0,1},{1,0},{2,3},{3,2},{4,5},{5,4},{6,7},{7,6},{8,9},{9,8},{10,11... | collective-permute-start | bytes 1824776 | tf_op jit(solution)/shard_map/ppermute | solution.py:268
  60.1 16.1 %collective-permute-start.13 = (bf16[72,4224]{1,0:T(8,128)(2,1)S(1)}, bf16[72,4224]{1,0:T(8,128)(2,1)S(1)}, u32[]{:S(2)}, u32[]{:S(2)}) collective-permute-start(bf16[72,4224]{1,0:T(8,128)(2,1)S(1)} %get-tuple-element.133), channel_id=1, source_target_pairs={{0,2},{1,3},{2,0},{3,1},{4,6},{5,7},{6,4},{7,5},{8,10},{9,11},{10,... | collective-permute-start | bytes 1824776 | tf_op jit(solution)/shard_map/ppermute | solution.py:268
  61.6 25.9 %collective-permute-start.15 = (bf16[128,4224]{1,0:T(8,128)(2,1)S(1)}, bf16[128,4224]{1,0:T(8,128)(2,1)S(1)}, u32[]{:S(2)}, u32[]{:S(2)}) collective-permute-start(bf16[128,4224]{1,0:T(8,128)(2,1)S(1)} %collective-permute-done.9.refs_1_), channel_id=1, source_target_pairs={{0,4},{1,5},{2,6},{3,7},{4,0},{5,1},{6,2},{7,3},{8,12},{9,13},{10,... | collective-permute-start | bytes 3244040 | tf_op jit(solution)/shard_map/ppermute | solution.py:268
  61.6 14.6 %collective-permute-start.12 = (bf16[72,4224]{1,0:T(8,128)(2,1)S(1)}, bf16[72,4224]{1,0:T(8,128)(2,1)S(1)}, u32[]{:S(2)}, u32[]{:S(2)}) collective-permute-start(bf16[72,4224]{1,0:T(8,128)(2,1)S(1)} %get-tuple-element.132.refs_0_.refs_8_), channel_id=1, source_target_pairs={{0,1},{1,0},{2,3},{3,2},{4,5},{5,4},{6,7},{7,6},{8,9},{9,8},{10,11... | collective-permute-start | bytes 1824776 | tf_op jit(solution)/shard_map/ppermute | solution.py:268
  76.2 2.0 %collective-permute-start.14 = (bf16[72,4224]{1,0:T(8,128)(2,1)S(1)}, bf16[72,4224]{1,0:T(8,128)(2,1)S(1)}, u32[]{:S(2)}, u32[]{:S(2)}) collective-permute-start(bf16[72,4224]{1,0:T(8,128)(2,1)S(1)} %collective-permute-done.13.refs_2_.refs_10_), channel_id=1, source_target_pairs={{0,1},{1,0},{2,3},{3,2},{4,5},{5,4},{6,7},{7,6},{8,9},{9,8},{10,11... | collective-permute-start | bytes 1824776 | tf_op jit(solution)/shard_map/ppermute | solution.py:268
  83.5 10.3 %collective-permute-start.19 = (bf16[72,2176]{1,0:T(8,128)(2,1)S(1)}, bf16[72,2176]{1,0:T(8,128)(2,1)S(1)}, u32[]{:S(2)}, u32[]{:S(2)}) collective-permute-start(bf16[72,2176]{1,0:T(8,128)(2,1)S(1)} %get-tuple-element.145), channel_id=1, source_target_pairs={{0,2},{1,3},{2,0},{3,1},{4,6},{5,7},{6,4},{7,5},{8,10},{9,11},{10,... | collective-permute-start | bytes 940040 | tf_op jit(solution)/shard_map/ppermute | solution.py:268
  89.5 16.6 %collective-permute-start.17 = (bf16[72,4224]{1,0:T(8,128)(2,1)S(1)}, bf16[72,4224]{1,0:T(8,128)(2,1)S(1)}, u32[]{:S(2)}, u32[]{:S(2)}) collective-permute-start(bf16[72,4224]{1,0:T(8,128)(2,1)S(1)} %get-tuple-element.142), channel_id=1, source_target_pairs={{0,2},{1,3},{2,0},{3,1},{4,6},{5,7},{6,4},{7,5},{8,10},{9,11},{10,... | collective-permute-start | bytes 1824776 | tf_op jit(solution)/shard_map/ppermute | solution.py:268
  90.0 3.8 %collective-permute-start.18 = (bf16[72,2176]{1,0:T(8,128)(2,1)S(1)}, bf16[72,2176]{1,0:T(8,128)(2,1)S(1)}, u32[]{:S(2)}, u32[]{:S(2)}) collective-permute-start(bf16[72,2176]{1,0:T(8,128)(2,1)S(1)} %get-tuple-element.144.refs_2_), channel_id=1, source_target_pairs={{0,1},{1,0},{2,3},{3,2},{4,5},{5,4},{6,7},{7,6},{8,9},{9,8},{10,11... | collective-permute-start | bytes 940040 | tf_op jit(solution)/shard_map/ppermute | solution.py:268
  96.6 7.6 %collective-permute-start.21 = (bf16[128,640]{1,0:T(8,128)(2,1)S(1)}, bf16[128,640]{1,0:T(8,128)(2,1)S(1)}, u32[]{:S(2)}, u32[]{:S(2)}) collective-permute-start(bf16[128,640]{1,0:T(8,128)(2,1)S(1)} %get-tuple-element.149), channel_id=1, source_target_pairs={{0,8},{1,9},{2,10},{3,11},{4,12},{5,13},{6,14},{7,15},{8,0},{9,1},... | collective-permute-start | bytes 491528 | tf_op jit(solution)/shard_map/ppermute | solution.py:268
  96.7 12.5 %collective-permute-start.16 = (bf16[72,4224]{1,0:T(8,128)(2,1)S(1)}, bf16[72,4224]{1,0:T(8,128)(2,1)S(1)}, u32[]{:S(2)}, u32[]{:S(2)}) collective-permute-start(bf16[72,4224]{1,0:T(8,128)(2,1)S(1)} %get-tuple-element.141.refs_0_.refs_12_), channel_id=1, source_target_pairs={{0,1},{1,0},{2,3},{3,2},{4,5},{5,4},{6,7},{7,6},{8,9},{9,8},{10,11... | collective-permute-start | bytes 1824776 | tf_op jit(solution)/shard_map/ppermute | solution.py:268
  106.1 3.1 %collective-permute-start.22 = (bf16[72,4224]{1,0:T(8,128)(2,1)S(1)}, bf16[72,4224]{1,0:T(8,128)(2,1)S(1)}, u32[]{:S(2)}, u32[]{:S(2)}) collective-permute-start(bf16[72,4224]{1,0:T(8,128)(2,1)S(1)} %collective-permute-done.17.refs_2_.refs_14_), channel_id=1, source_target_pairs={{0,1},{1,0},{2,3},{3,2},{4,5},{5,4},{6,7},{7,6},{8,9},{9,8},{10,11... | collective-permute-start | bytes 1824776 | tf_op jit(solution)/shard_map/ppermute | solution.py:268
  106.1 9.8 %collective-permute-start.27 = (bf16[72,2176]{1,0:T(8,128)(2,1)S(1)}, bf16[72,2176]{1,0:T(8,128)(2,1)S(1)}, u32[]{:S(2)}, u32[]{:S(2)}) collective-permute-start(bf16[72,2176]{1,0:T(8,128)(2,1)S(1)} %get-tuple-element.168), channel_id=1, source_target_pairs={{0,2},{1,3},{2,0},{3,1},{4,6},{5,7},{6,4},{7,5},{8,10},{9,11},{10,... | collective-permute-start | bytes 940040 | tf_op jit(solution)/shard_map/ppermute | solution.py:268
  107.6 18.7 %collective-permute-start.25 = (bf16[128,1536]{1,0:T(8,128)(2,1)S(1)}, bf16[128,1536]{1,0:T(8,128)(2,1)S(1)}, u32[]{:S(2)}, u32[]{:S(2)}) collective-permute-start(bf16[128,1536]{1,0:T(8,128)(2,1)S(1)} %get-tuple-element.165), channel_id=1, source_target_pairs={{0,8},{1,9},{2,10},{3,11},{4,12},{5,13},{6,14},{7,15},{8,0},{9,1},... | collective-permute-start | bytes 1179656 | tf_op jit(solution)/shard_map/ppermute | solution.py:268
  109.1 8.5 %collective-permute-start.26 = (bf16[72,2176]{1,0:T(8,128)(2,1)S(1)}, bf16[72,2176]{1,0:T(8,128)(2,1)S(1)}, u32[]{:S(2)}, u32[]{:S(2)}) collective-permute-start(bf16[72,2176]{1,0:T(8,128)(2,1)S(1)} %get-tuple-element.167.refs_2_), channel_id=1, source_target_pairs={{0,1},{1,0},{2,3},{3,2},{4,5},{5,4},{6,7},{7,6},{8,9},{9,8},{10,11... | collective-permute-start | bytes 940040 | tf_op jit(solution)/shard_map/ppermute | solution.py:268
  115.9 1.8 %collective-permute-start.28 = (bf16[72,2176]{1,0:T(8,128)(2,1)S(1)}, bf16[72,2176]{1,0:T(8,128)(2,1)S(1)}, u32[]{:S(2)}, u32[]{:S(2)}) collective-permute-start(bf16[72,2176]{1,0:T(8,128)(2,1)S(1)} %collective-permute-done.27.refs_4_), channel_id=1, source_target_pairs={{0,1},{1,0},{2,3},{3,2},{4,5},{5,4},{6,7},{7,6},{8,9},{9,8},{10,11... | collective-permute-start | bytes 940040 | tf_op jit(solution)/shard_map/ppermute | solution.py:268
  115.9 10.4 %collective-permute-start.24 = (bf16[72,2176]{1,0:T(8,128)(2,1)S(1)}, bf16[72,2176]{1,0:T(8,128)(2,1)S(1)}, u32[]{:S(2)}, u32[]{:S(2)}) collective-permute-start(bf16[72,2176]{1,0:T(8,128)(2,1)S(1)} %get-tuple-element.164), channel_id=1, source_target_pairs={{0,2},{1,3},{2,0},{3,1},{4,6},{5,7},{6,4},{7,5},{8,10},{9,11},{10,... | collective-permute-start | bytes 940040 | tf_op jit(solution)/shard_map/ppermute | solution.py:268
  117.4 12.0 %collective-permute-start.23 = (bf16[72,2176]{1,0:T(8,128)(2,1)S(1)}, bf16[72,2176]{1,0:T(8,128)(2,1)S(1)}, u32[]{:S(2)}, u32[]{:S(2)}) collective-permute-start(bf16[72,2176]{1,0:T(8,128)(2,1)S(1)} %get-tuple-element.163.refs_2_), channel_id=1, source_target_pairs={{0,1},{1,0},{2,3},{3,2},{4,5},{5,4},{6,7},{7,6},{8,9},{9,8},{10,11... | collective-permute-start | bytes 940040 | tf_op jit(solution)/shard_map/ppermute | solution.py:268
  126.3 3.1 %collective-permute-start.29 = (bf16[72,2176]{1,0:T(8,128)(2,1)S(1)}, bf16[72,2176]{1,0:T(8,128)(2,1)S(1)}, u32[]{:S(2)}, u32[]{:S(2)}) collective-permute-start(bf16[72,2176]{1,0:T(8,128)(2,1)S(1)} %collective-permute-done.24.refs_4_), channel_id=1, source_target_pairs={{0,1},{1,0},{2,3},{3,2},{4,5},{5,4},{6,7},{7,6},{8,9},{9,8},{10,11... | collective-permute-start | bytes 940040 | tf_op jit(solution)/shard_map/ppermute | solution.py:268
  126.4 9.8 %collective-permute-start.6 = (bf16[72,2176]{1,0:T(8,128)(2,1)S(1)}, bf16[72,2176]{1,0:T(8,128)(2,1)S(1)}, u32[]{:S(2)}, u32[]{:S(2)}) collective-permute-start(bf16[72,2176]{1,0:T(8,128)(2,1)S(1)} %get-tuple-element.122), channel_id=1, source_target_pairs={{0,2},{1,3},{2,0},{3,1},{4,6},{5,7},{6,4},{7,5},{8,10},{9,11},{10,... | collective-permute-start | bytes 940040 | tf_op jit(solution)/shard_map/ppermute | solution.py:268
  127.3 15.5 %collective-permute-start.31 = (bf16[128,2176]{1,0:T(8,128)(2,1)S(1)}, bf16[128,2176]{1,0:T(8,128)(2,1)S(1)}, u32[]{:S(2)}, u32[]{:S(2)}) collective-permute-start(bf16[128,2176]{1,0:T(8,128)(2,1)S(1)} %get-tuple-element.181), channel_id=1, source_target_pairs={{0,4},{1,5},{2,6},{3,7},{4,0},{5,1},{6,2},{7,3},{8,12},{9,13},{10,... | collective-permute-start | bytes 1671176 | tf_op jit(solution)/shard_map/ppermute | solution.py:268
  130.5 26.5 %collective-permute-start.32 = (bf16[128,2176]{1,0:T(8,128)(2,1)S(1)}, bf16[128,2176]{1,0:T(8,128)(2,1)S(1)}, u32[]{:S(2)}, u32[]{:S(2)}) collective-permute-start(bf16[128,2176]{1,0:T(8,128)(2,1)S(1)} %get-tuple-element.186), channel_id=1, source_target_pairs={{0,12},{1,13},{2,14},{3,15},{4,8},{5,9},{6,10},{7,11},{8,4},{9,5},... | collective-permute-start | bytes 1671176 | tf_op jit(solution)/shard_map/ppermute | solution.py:268
  132.0 4.1 %collective-permute-start.5 = (bf16[72,2176]{1,0:T(8,128)(2,1)S(1)}, bf16[72,2176]{1,0:T(8,128)(2,1)S(1)}, u32[]{:S(2)}, u32[]{:S(2)}) collective-permute-start(bf16[72,2176]{1,0:T(8,128)(2,1)S(1)} %get-tuple-element.121.refs_2_), channel_id=1, source_target_pairs={{0,1},{1,0},{2,3},{3,2},{4,5},{5,4},{6,7},{7,6},{8,9},{9,8},{10,11... | collective-permute-start | bytes 940040 | tf_op jit(solution)/shard_map/ppermute | solution.py:268
  136.1 1.6 %collective-permute-start.30 = (bf16[72,2176]{1,0:T(8,128)(2,1)S(1)}, bf16[72,2176]{1,0:T(8,128)(2,1)S(1)}, u32[]{:S(2)}, u32[]{:S(2)}) collective-permute-start(bf16[72,2176]{1,0:T(8,128)(2,1)S(1)} %collective-permute-done.6.refs_4_), channel_id=1, source_target_pairs={{0,1},{1,0},{2,3},{3,2},{4,5},{5,4},{6,7},{7,6},{8,9},{9,8},{10,11... | collective-permute-start | bytes 940040 | tf_op jit(solution)/shard_map/ppermute | solution.py:268
  (12 other events, 50.4 us)
